TPU v7x, 32 devices: a whole 2x2x4 slice. The times are simulated.
32 devices in a mesh: dp: 8 (over y, x, core), tensor: 4 (over z).
Axes of the slice: x: 2, y: 2, z: 4, core: 2. Of those that a mesh axis runs over, the one named last changes fastest.
Arguments:
- tokens: bfloat16 [30720, 512], P(('dp', 'tensor')), may hold values from -6 to 6
- cotangent: bfloat16 [30720, 512], P(('dp', 'tensor')), may hold values from -6 to 6
- lengths: int32 [32], P('dp'), may hold values from 96 to 720, as said below
- neighbours: int32 [30720, 8], P('dp'), may hold values from -1 to 3779, as said below
- ln1_gain: float32 [512], replicated, may hold values from 0.5 to 1.5
- ln1_shift: float32 [512], replicated, may hold values from -1.75 to 1.75
- w_qkv: bfloat16 [3, 512, 512], P(None, None, 'tensor'), may hold values from -0.25 to 0.25
- w_out: bfloat16 [512, 512], P('tensor'), may hold values from -0.5 to 0.5
- b_out: float32 [512], replicated, may hold values from -1.75 to 1.75
- ln2_gain: float32 [512], replicated, may hold values from 0.5 to 1.5
- ln2_shift: float32 [512], replicated, may hold values from -1.75 to 1.75
- w_up: bfloat16 [512, 2048], P(None, 'tensor'), may hold values from -0.25 to 0.25
- b_up: bfloat16 [2048], P('tensor'), may hold values from -3 to 3
- w_down: bfloat16 [2048, 512], P('tensor'), may hold values from -0.1875 to 0.1875
- b_down: float32 [512], replicated, may hold values from -1.75 to 1.75
Outputs:
- output: bfloat16 [30720, 512], P(('dp', 'tensor'))
- grad_tokens: float32 [30720, 512], P(('dp', 'tensor'))
- grad_ln1_gain: float32 [512], replicated
- grad_ln1_shift: float32 [512], replicated
- grad_w_qkv: float32 [3, 512, 512], P(None, None, 'tensor')
- grad_w_out: float32 [512, 512], P('tensor')
- grad_b_out: float32 [512], replicated
- grad_ln2_gain: float32 [512], replicated
- grad_ln2_shift: float32 [512], replicated
- grad_w_up: float32 [512, 2048], P(None, 'tensor')
- grad_b_up: float32 [2048], P('tensor')
- grad_w_down: float32 [2048, 512], P('tensor')
- grad_b_down: float32 [512], replicated
Inputs may be any that keep to these rules, and one draw needn't show every extreme that they name: `lengths`: lengths are multiples of 16; among the 4 windows of each index of dp one has exactly 720 steps. `neighbours`: within a group of 3840 rows window w (of that group) step p sits at level 0 in row w * 720 + p, its level 1 node p at row 2880 + w * 180 + p and its level 2 node p at row 3600 + w * 45 + p. A live node lists, as row numbers within the group: itself, the node before and after it on its level within its window, its parent (p / 4 one level up) and its four children (4 * p to 4 * p + 3 one level down), -1 where none exists; nodes past a window's length at their level and the remaining rows list -1 only.
All inputs are finite; a program needn't handle non-finite values.
Results may differ from a plain program's by a relative error of at most 0.014.
Values may be sent and summed in bfloat16 or wider, within the bound.
No kernel may reach another device: no remote copies, remote signals or barrier semaphores. Data moves between devices by JAX's collectives and lax.ppermute only.
A program may use at most 128 MiB of HBM per device.

v0:
```python
import math

import jax
import jax.numpy as jnp
from jax import lax
from jax.experimental import pallas as pl
from jax.experimental.pallas import tpu as pltpu
from jax.sharding import PartitionSpec as P

D = 512
DH = 64
MAXLEN = 720
NODES_GRP = 3840
SHARD = NODES_GRP // 4
F32 = jnp.float32
BF16 = jnp.bfloat16

BLK = 48
QUAD = 4 * BLK
L1_ROW = 4 * QUAD
L2_ROW = L1_ROW + QUAD
USED = L2_ROW + BLK
ROWS = 1024
EXT_C = (0, 240, 432, 672)
EXT_LEFT = (624, 0, 240, 432)
EXT_RIGHT = (240, 432, 672, 48)
EXT_L1 = 912
EXT_L2 = 1200
EXT = 1296
VMEM_BYTES = 60 * 1024 * 1024
SEND_LO = SHARD - MAXLEN
LOW_HEAD = (0, 176, 352)
LOW_TAIL = (720, 752, 800)


def split_blocks(row):
    block = row * 1366 >> 16
    return block, row - BLK * block


def gather_source(start, t):
    row = lax.broadcasted_iota(jnp.int32, (256, 1), 0) + start
    block, step = split_blocks(row)
    child, node = block >> 2, block & 3
    at = 720 - 240 * t + 16 * step + 4 * node + child
    level0 = jnp.where(at < 720, SHARD + at, at - 720)
    level1 = 4 * step + node + jnp.where(t == 3, 540, SHARD + 720 + 4 * t)
    tail = jnp.where(t == 0, 0, jnp.where(t == 1, 13, 10))
    level2 = step + jnp.where(t == 3, 855, SHARD + 720 + 192 + tail)
    spare = 3 * block + step - 45
    spare = jnp.where((t == 3) & (spare < 60) & (row < USED), 900 + spare, -1)
    live = jnp.where(row < L1_ROW, level0, jnp.where(row < L2_ROW, level1, level2))
    return jnp.where((step < 45) & (row < USED), live, spare)


def spread_source(start, t):
    row = lax.broadcasted_iota(jnp.int32, (240, 1), 0) + start
    at = 240 * t + row
    place = jnp.where(at < 720, at, at - 720)
    high = QUAD * (place & 3) + BLK * (place >> 2 & 3) + (place >> 4) + jnp.where(at < 720, 0, ROWS)
    first = (row >= 180).astype(jnp.int32) + (row >= 360).astype(jnp.int32) + (row >= 540).astype(jnp.int32)
    inside = row - 180 * first
    level1 = L1_ROW + BLK * (inside & 3) + (inside >> 2)
    rest = row - 720
    second = (rest >= 45).astype(jnp.int32) + (rest >= 90).astype(jnp.int32) + (rest >= 135).astype(jnp.int32)
    level2 = L2_ROW + rest - 45 * second
    spare = row - 900
    third = spare * 21846 >> 16
    low = jnp.where(row < 720, level1, level2)
    window = jnp.where(row < 720, first, second)
    low = jnp.where(window == 3, low, ROWS - L1_ROW + 240 * window + low)
    low = jnp.where(row < 900, low, BLK * third + 45 + spare - 3 * third)
    return jnp.where(t == 3, low, high)


def dot_nn(a, b):
    return jnp.dot(a, b, preferred_element_type=F32)


def dot_nt(a, b):
    return lax.dot_general(a, b, (((1,), (1,)), ((), ())), preferred_element_type=F32)


def dot_tn(a, b):
    return lax.dot_general(a, b, (((0,), (0,)), ((), ())), preferred_element_type=F32)


def one_hot(source, base, count):
    return (source - base == lax.broadcasted_iota(jnp.int32, (source.shape[0], count), 1)).astype(BF16)


def gathered_rows(start, t, own, recv, low):
    source = gather_source(start, t)
    total = dot_nn(one_hot(source, 0, SHARD), own[...])
    if start < L1_ROW:
        return total + dot_nn(one_hot(source, SHARD, 720), recv[...])
    return total + dot_nn(one_hot(source, SHARD + 720, 256), low[0][...] + low[1][...] + low[2][...])


def begin(sems, *pairs):
    copies = [pltpu.make_async_copy(src, dst, sems.at[i]) for i, (src, dst) in enumerate(pairs)]
    for copy in copies:
        copy.start()
    return copies


def finish(copies):
    for copy in copies:
        copy.wait()


def moments(values):
    center = values - jnp.mean(values, axis=-1, keepdims=True)
    spread = jnp.mean(center * center, axis=-1, keepdims=True)
    rstd = lax.rsqrt(spread + 1e-05)
    return center * rstd, rstd


def head_sum_matrix():
    row = lax.broadcasted_iota(jnp.int32, (8 * D, 128), 0)
    col = lax.broadcasted_iota(jnp.int32, (8 * D, 128), 1)
    return (row // DH == col % 64).astype(BF16)


def head_spread_matrix():
    row = lax.broadcasted_iota(jnp.int32, (128, 8 * D), 0)
    col = lax.broadcasted_iota(jnp.int32, (128, 8 * D), 1)
    return (row == col // DH).astype(BF16)


def slot_max(values):
    for step in (8, 16, 32):
        values = jnp.maximum(values, pltpu.roll(values, step, 1))
    return values


def slot_sum(values):
    for step in (8, 16, 32):
        values = values + pltpu.roll(values, step, 1)
    return values


def shift_down(block):
    row = lax.broadcasted_iota(jnp.int32, block.shape, 0)
    return jnp.where(row == 0, 0.0, pltpu.roll(block, 1, 0))


def shift_up(block):
    row = lax.broadcasted_iota(jnp.int32, block.shape, 0)
    return jnp.where(row == BLK - 1, 0.0, pltpu.roll(block, BLK - 1, 0))


def extend(ext, rows):
    kind = ext.dtype
    for c in range(4):
        ext[EXT_C[c] : EXT_C[c] + QUAD, :] = rows(QUAD * c, QUAD).astype(kind)
    ext[EXT_L1 : EXT_L1 + QUAD, :] = rows(L1_ROW, QUAD).astype(kind)
    last = rows(L2_ROW, BLK)
    ext[EXT_L2 : EXT_L2 + BLK, :] = last.astype(kind)
    ext[192:240, :] = shift_up(rows(0, BLK)).astype(kind)
    ext[624:672, :] = shift_down(rows(3 * QUAD + 144, BLK)).astype(kind)
    ext[864:912, :] = shift_down(rows(L1_ROW + 144, BLK)).astype(kind)
    ext[1104:1152, :] = shift_up(rows(L1_ROW, BLK)).astype(kind)
    ext[1152:1200, :] = shift_down(last).astype(kind)
    ext[1248:1296, :] = shift_up(last).astype(kind)


def present(count, level, child, live_steps):
    row = lax.broadcasted_iota(jnp.int32, (count, 128), 0)
    slot = lax.broadcasted_iota(jnp.int32, (count, 128), 1) % 64 // 8
    step = row
    for start in (BLK, 2 * BLK, 3 * BLK):
        if start < count:
            step = jnp.where(row >= start, row - start, step)
    here = step < live_steps
    if level == 0:
        here = here & (slot < 4)
    if level == 2:
        here = here & (slot != 3)
    if level > 0 or child == 0:
        here = here & ((slot != 1) | (row > 0))
    if level > 0 or child == 3:
        here = here & ((slot != 2) | (row < count - BLK) | (step + 1 < live_steps))
    return here


def groups(ext):
    def quad(at):
        return lambda: ext[at : at + QUAD, :]

    def block(at):
        return lambda: ext[at : at + BLK, :]

    def tiled(at):
        return lambda: jnp.concatenate([ext[at : at + BLK, :]] * 4, axis=0)

    out = []
    for c in range(4):
        out.append((QUAD * c, QUAD, 0, c, [quad(EXT_C[c]), quad(EXT_LEFT[c]), quad(EXT_RIGHT[c]), quad(EXT_L1)]))
    out.append(
        (L1_ROW, QUAD, 1, 0, [quad(EXT_L1), quad(864), quad(960), tiled(EXT_L2)] + [quad(EXT_C[c]) for c in range(4)])
    )
    children = [block(EXT_L1 + BLK * d) for d in range(4)]
    out.append((L2_ROW, BLK, 2, 0, [block(EXT_L2), block(1152), block(1248), None] + children))
    return out


def attention_forward(
    lengths, own, recv, low0, low1, low2, gain, shift, b_out, w_qkv, w_out, plane, other, *rest
):
    x_hbm, n_hbm, qkv_hbm, prob_out, ctx_out, mid_out, w_hbm = rest[:7]
    x_out, n_out, qkv_out, w_full, own_qkv, own_out, near, far, kx, vx, heads_in, heads_out, in_sems, out_sems = rest[7:]
    me, t = lax.axis_index("dp") & 7, lax.axis_index("tensor")
    live_steps = lengths[t] >> 4
    loading = begin(in_sems, (w_qkv, own_qkv), (w_out, own_out), (plane, near), (other, far))
    for start in range(0, ROWS, 256):
        run = slice(start, start + 256)
        rows = gathered_rows(start, t, own, recv, (low0, low1, low2))
        x_out[run, :] = rows.astype(BF16)
        n_out[run, :] = (moments(rows)[0] * gain[...] + shift[...]).astype(BF16)
    heads_in[...] = head_sum_matrix()
    heads_out[...] = head_spread_matrix()
    finish(loading)
    for i in range(3):
        w_full[i, :, 0:128] = own_qkv[i]
    w_full[3, 0:128, :] = own_out[...]
    for half, pieces in enumerate((near, far)):
        for k in range(4):
            parity = (me & 1) ^ half
            at = pl.multiple_of((2 * k + parity) * 64, 64)
            for s in range(1, 4):
                for i in range(3):
                    w_full[i, pl.ds(at, 64), 128 * s : 128 * s + 128] = pieces[k, s - 1, i]
                top = pl.multiple_of(128 * s + 64 * parity, 64)
                w_full[3, pl.ds(top, 64), 128 * k : 128 * k + 128] = pieces[k, s - 1, 3]
    for i in range(3):
        for start in range(0, ROWS, 512):
            run = slice(start, start + 512)
            qkv_out[i, run, :] = dot_nn(n_out[run, :], w_full[i]).astype(BF16)
    storing = begin(out_sems, (x_out, x_hbm), (n_out, n_hbm), (qkv_out, qkv_hbm), (w_full, w_hbm))
    extend(kx, lambda at, count: qkv_out[1, at : at + count, :].astype(F32))
    extend(vx, lambda at, count: qkv_out[2, at : at + count, :].astype(F32))
    ctx_out[USED:ROWS, :] = jnp.zeros((ROWS - USED, D), BF16)
    prob_out[USED:ROWS, :] = jnp.zeros((ROWS - USED, 128), F32)
    for (first, count, level, child, keys), (_, _, _, _, values) in zip(groups(kx), groups(vx)):
        query = qkv_out[0, first : first + count, :] * jnp.bfloat16(1.0 / math.sqrt(DH))
        slots = [s for s in range(len(keys)) if keys[s] is not None]
        score = jnp.zeros((count, 128), F32)
        for s in slots:
            score = score + dot_nn(query * keys[s](), heads_in[D * s : D * s + D, :])
        here = present(count, level, child, live_steps)
        score = jnp.where(here, score, -1000000000.0)
        weight = jnp.where(here, jnp.exp(score - slot_max(score)), 0.0)
        prob = weight / jnp.maximum(slot_sum(weight), 1.0)
        prob_out[first : first + count, :] = prob
        prob_low = prob.astype(BF16)
        context = jnp.zeros((count, D), F32)
        for s in slots:
            context = context + dot_nn(prob_low, heads_out[:, D * s : D * s + D]) * values[s]()
        ctx_out[first : first + count, :] = context.astype(BF16)
    for start in range(0, ROWS, 512):
        run = slice(start, start + 512)
        mid_out[run, :] = x_out[run, :].astype(F32) + dot_nn(ctx_out[run, :], w_full[3]) + b_out[...]
    finish(storing)


def feed_forward(
    own, recv, low0, low1, low2, mid, gain, shift, b_down, w_up, b_up, w_down, pieces, *rest
):
    y_quad, y_low, keep_hbm, send_hbm, gnorm, grad_hbm, grad_bias = rest[:7]
    up_w, down_w, up_t, down_t, bias, normed, grad, normed_t, grad_t = rest[7:16]
    act_s, gup_s, total, tmp, arrived, keep, send, in_sems, out_sems = rest[16:]
    me, t = lax.axis_index("dp") & 7, lax.axis_index("tensor")
    loading = begin(in_sems, (w_up, up_w.at[0]), (w_down, down_w.at[0]), (pieces, arrived))
    for start in range(0, ROWS, 256):
        run = slice(start, start + 256)
        low = (moments(mid[run, :])[0] * gain[...] + shift[...]).astype(BF16)
        normed[run, :] = low
        normed_t[:, run] = low.T
        cot = gathered_rows(start, t, own, recv, (low0, low1, low2)).astype(BF16)
        grad[run, :] = cot
        grad_t[:, run] = cot.T
    total[...] = jnp.zeros_like(total)
    gnorm[...] = jnp.zeros_like(gnorm)
    finish(loading)
    storing = begin(out_sems.at[8:9], (grad, grad_hbm))
    bias[0:1, :] = b_up[...].astype(F32)
    for piece in range(8):
        for s in range(1, 4):
            up_w[s, 64 * piece : 64 * piece + 64, :] = arrived[piece, s - 1, 0:64, :]
            down_w[s, 64 * piece : 64 * piece + 64, :] = arrived[piece, s - 1, 64:128, :]
    for s in range(1, 4):
        bias[s : s + 1, :] = arrived[0, s - 1, 128:129, :].astype(F32)

    def hidden(s, carry):
        up_here, down_here = up_w[s], down_w[s]
        up_t[...] = up_here.T
        down_t[...] = down_here.T
        sums = jnp.zeros((1, D), F32)
        for start in range(0, ROWS, 256):
            run = slice(start, start + 256)
            pre = dot_nn(normed[run, :], up_here) + bias[pl.ds(s, 1), :]
            square = pre * pre
            root = math.sqrt(2.0 / math.pi)
            bent = jnp.tanh(pre * (root + (root * 0.044715) * square))
            half = 0.5 * pre
            act = (half + half * bent).astype(BF16)
            slope = (0.5 + 0.5 * bent) + half * (1.0 - bent * bent) * (root + (3.0 * root * 0.044715) * square)
            gup = (slope * dot_nn(grad[run, :], down_t[...])).astype(BF16)
            act_s[run, :] = act
            gup_s[run, :] = gup
            sums = sums + jnp.sum(gup.astype(F32), axis=0, keepdims=True)
            total[run, :] += dot_nn(act, down_here)
            gnorm[run, :] += dot_nn(gup, up_t[...])
        grad_bias[pl.ds(s, 1), :] = sums
        tmp[0] = dot_nn(normed_t[...], gup_s[...]).astype(BF16)
        tmp[1] = dot_nn(grad_t[...], act_s[...]).astype(BF16)
        slot = ((t - s) & 3) ^ t
        for half, target in enumerate((keep, send)):
            for k in range(4):
                at = pl.multiple_of((me ^ (2 * k + half)) * 64, 64)
                target[slot, k, 0:64, :] = tmp[0, pl.ds(at, 64), :]
                target[slot, k, 64:128, :] = tmp[1, pl.ds(at, 64), :]
        begin(out_sems.at[pl.ds(2 * s, 2)], (keep.at[slot], keep_hbm.at[slot]), (send.at[slot], send_hbm.at[slot]))
        return carry

    lax.fori_loop(0, 4, hidden, 0)
    for start in range(0, ROWS, 256):
        run = slice(start, start + 256)
        out = (mid[run, :] + (total[run, :] + b_down[...])).astype(BF16)
        if start < L1_ROW:
            y_quad[run, :] = out
        else:
            y_low[...] = out[0 : USED - L1_ROW, :]
    for s in range(4):
        pltpu.make_async_copy(keep.at[s], keep_hbm.at[s], out_sems.at[2 * s]).wait()
        pltpu.make_async_copy(send.at[s], send_hbm.at[s], out_sems.at[2 * s + 1]).wait()
    finish(storing)


def norm_backward(lengths, mid, gnorm, grad, gain, ctx, w_full, keep_hbm, far_hbm, *rest):
    gmid, gcontext, gw_out, small = rest[:4]
    both, (attn, w_here, ctx_here, keep, far, sems) = rest[4:8], rest[8:]
    live_steps = lengths[lax.axis_index("tensor")] >> 4
    loading = begin(sems, (w_full.at[3], w_here), (ctx, ctx_here), (keep_hbm, keep), (far_hbm, far))
    finish(loading[:1])
    sums = [jnp.zeros((1, D), F32) for _ in range(4)]
    for start in range(0, ROWS, 256):
        run = slice(start, start + 256)
        hat, rstd = moments(mid[run, :])
        back = gnorm[run, :]
        scaled = back * gain[...]
        cot = grad[run, :].astype(F32)
        mean_one = jnp.mean(scaled, axis=-1, keepdims=True)
        mean_two = jnp.mean(scaled * hat, axis=-1, keepdims=True)
        result = cot + rstd * (scaled - mean_one - hat * mean_two)
        gmid[run, :] = result
        low = result.astype(BF16)
        attn[run, :] = low
        step = lax.broadcasted_iota(jnp.int32, (256, 1), 0) + start
        step = split_blocks(step)[1]
        gcontext[run, :] = jnp.where(step < live_steps, dot_nt(low, w_here[...]), 0.0).astype(BF16)
        terms = (cot, back * hat, back, low.astype(F32))
        sums = [running + jnp.sum(term, axis=0, keepdims=True) for running, term in zip(sums, terms)]
    finish(loading[1:])
    gw_out[...] = dot_tn(ctx_here[...], attn[...]).astype(BF16)
    for k in range(4):
        for slot in range(4):
            both[k][slot] = (keep[slot, k].astype(F32) + far[slot, k].astype(F32)).astype(BF16)
    small[...] = jnp.concatenate(sums + [jnp.zeros((4, D), F32)], axis=0)


REVERSE = (0, 2, 1)


def attention_backward(qkv, prob, gcontext, gain, small, small_up, gmid, x_in, n_in, gw_out, w_full, *rest):
    g_quad, g_low, keep, send = rest[:4]
    fx, cx, px, sx, heads_in, heads_out, packed, tmp = rest[4:12]
    bx, middle, x_here, n_here, gw_here, w_here, scores, sems = rest[12:]
    me, t = lax.axis_index("dp") & 7, lax.axis_index("tensor")
    loading = begin(sems, (gmid, middle), (x_in, x_here), (n_in, n_here), (gw_out, gw_here), (w_full, w_here))
    heads_in[...] = head_sum_matrix()
    heads_out[...] = head_spread_matrix()
    scale = 1.0 / math.sqrt(DH)
    extend(fx, lambda at, count: qkv[1, at : at + count, :].astype(F32))
    extend(bx, lambda at, count: qkv[2, at : at + count, :].astype(F32))
    packed[:, USED:ROWS, :] = jnp.zeros((3, ROWS - USED, D), BF16)
    for (first, count, level, child, keys), (_, _, _, _, values) in zip(groups(fx), groups(bx)):
        run = slice(first, first + count)
        slots = [s for s in range(len(keys)) if keys[s] is not None]
        cot = gcontext[run, :]
        gprob = jnp.zeros((count, 128), F32)
        for s in slots:
            gprob = gprob + dot_nn(cot * values[s](), heads_in[D * s : D * s + D, :])
        here = prob[run, :]
        gscore = (here * (gprob - slot_sum(here * gprob))).astype(BF16)
        scores[run, :] = gscore.astype(F32)
        gquery = jnp.zeros((count, D), F32)
        for s in slots:
            gquery = gquery + dot_nn(gscore, heads_out[:, D * s : D * s + D]) * keys[s]()
        packed[0, run, :] = (gquery * scale).astype(BF16)
    extend(fx, lambda at, count: qkv[0, at : at + count, :].astype(F32) * scale)
    extend(cx, lambda at, count: gcontext[at : at + count, :].astype(F32))
    extend(px, lambda at, count: prob[at : at + count, :])
    extend(sx, lambda at, count: scores[at : at + count, :])
    for quers, grads, probs, scors in zip(groups(fx), groups(cx), groups(px), groups(sx)):
        first, count, level, child, queries = quers
        gkey = jnp.zeros((count, D), F32)
        gvalue = jnp.zeros((count, D), F32)
        for s in range(len(queries)):
            if queries[s] is None:
                continue
            weight, score = probs[4][s](), scors[4][s]()
            if s < 3:
                back = REVERSE[s]
            elif s == 3:
                back = 4 + child
            else:
                back = 3
            if level == 1 and s == 3:
                wide_p = jnp.concatenate(
                    [dot_nn(weight[0:BLK, :], heads_out[:, D * (4 + d) : D * (5 + d)]) for d in range(4)], axis=0
                )
                wide_s = jnp.concatenate(
                    [dot_nn(score[0:BLK, :], heads_out[:, D * (4 + d) : D * (5 + d)]) for d in range(4)], axis=0
                )
            else:
                wide_p = dot_nn(weight, heads_out[:, D * back : D * back + D])
                wide_s = dot_nn(score, heads_out[:, D * back : D * back + D])
            gkey = gkey + wide_s * queries[s]()
            gvalue = gvalue + wide_p * grads[4][s]()
        packed[1, first : first + count, :] = gkey.astype(BF16)
        packed[2, first : first + count, :] = gvalue.astype(BF16)
    finish(loading)
    normed_t = n_here[...].T
    for i in range(3):
        tmp[i] = dot_nn(normed_t, packed[i]).astype(BF16)
    sums = [jnp.zeros((1, D), F32) for _ in range(2)]
    for start in range(0, ROWS, 256):
        run = slice(start, start + 256)
        back = dot_nt(packed[0, run, :], w_here[0])
        back = back + dot_nt(packed[1, run, :], w_here[1])
        back = back + dot_nt(packed[2, run, :], w_here[2])
        hat, rstd = moments(x_here[run, :].astype(F32))
        scaled = back * gain[...]
        mean_one = jnp.mean(scaled, axis=-1, keepdims=True)
        mean_two = jnp.mean(scaled * hat, axis=-1, keepdims=True)
        result = (middle[run, :] + rstd * (scaled - mean_one - hat * mean_two)).astype(BF16)
        if start < L1_ROW:
            g_quad[run, :] = result
        else:
            g_low[...] = result[0 : USED - L1_ROW, :]
        terms = (back * hat, back)
        sums = [running + jnp.sum(term, axis=0, keepdims=True) for running, term in zip(sums, terms)]
    sums = [small[i : i + 1, :] for i in range(4)] + sums
    for s in range(4):
        slot = ((t - s) & 3) ^ t
        vectors = sums + [small_up[s : s + 1, :]]
        rows = [vector[:, 128 * i : 128 * i + 128] for vector in vectors for i in range(4)]
        rows = jnp.concatenate(rows + [jnp.zeros((4, 128), F32)], axis=0).astype(BF16)
        for half, target in enumerate((keep, send)):
            for k in range(4):
                parity = (me & 1) ^ half
                at = pl.multiple_of((2 * k + parity) * 64, 64)
                for i in range(3):
                    target[k, slot, 64 * i : 64 * i + 64, :] = tmp[i, pl.ds(at, 64), 128 * s : 128 * s + 128]
                top = pl.multiple_of(128 * s + 64 * parity, 64)
                target[k, slot, 192:256, :] = gw_here[pl.ds(top, 64), 128 * k : 128 * k + 128]
                target[k, slot, 256:288, :] = rows


def spread_rows(quad, low, recv, low0, low1, low2, out):
    t = lax.axis_index("tensor")
    moved = recv[...] + jnp.concatenate([low0[...], low1[...], low2[...], jnp.zeros((48, D), BF16)], axis=0)
    for start in range(0, SHARD, 240):
        source = spread_source(start, t)
        rows = dot_nn(one_hot(source, 0, L1_ROW), quad[...])
        rows = rows + dot_nn(one_hot(source, L1_ROW, USED - L1_ROW), low[...])
        rows = rows + dot_nn(one_hot(source, ROWS, L1_ROW), moved)
        out[start : start + 240, :] = rows.astype(out.dtype)


def unpack_weights(in_a, in_b, g_qkv, g_out, g_up, g_down, down_t):
    for p in range(8):
        g_up[64 * p : 64 * p + 64, :] = in_b[p, 0:64, :].astype(F32)
        down_t[64 * p : 64 * p + 64, :] = in_b[p, 64:128, :].astype(F32)
    g_down[...] = down_t[...].T
    for p in range(8):
        for i in range(3):
            g_qkv[i, 64 * p : 64 * p + 64, :] = in_a[p, 64 * i : 64 * i + 64, :].astype(F32)
        top, side = 64 * (p % 2), 128 * (p // 2)
        g_out[top : top + 64, side : side + 128] = in_a[p, 192:256, :].astype(F32)


def call(body, name, ins, outs, scratch=(), moved=1000, far_ins=(), far_outs=()):
    specs = [pl.BlockSpec(memory_space=pl.ANY if i in far_ins else pltpu.VMEM) for i in range(len(ins))]
    if ins[0].ndim == 1:
        specs[0] = pl.BlockSpec(memory_space=pltpu.SMEM)
    return pl.pallas_call(
        body,
        out_shape=tuple(outs),
        in_specs=specs,
        out_specs=tuple(pl.BlockSpec(memory_space=pl.ANY if i in far_outs else pltpu.VMEM) for i in range(len(outs))),
        scratch_shapes=list(scratch),
        compiler_params=pltpu.CompilerParams(vmem_limit_bytes=VMEM_BYTES),
        cost_estimate=pl.CostEstimate(flops=1000, bytes_accessed=moved, transcendentals=0),
        name=name,
    )(*ins)


def struct(shape, dtype):
    return jax.ShapeDtypeStruct(shape, dtype)


def shards(
    tokens,
    cotangent,
    lengths,
    neighbours,
    ln1_gain,
    ln1_shift,
    w_qkv,
    w_out,
    b_out,
    ln2_gain,
    ln2_shift,
    w_up,
    b_up,
    w_down,
    b_down,
    n_dp,
):
    sub = lax.axis_index("dp") & 7
    planes = [[8 * g + 2 * k + c for k in range(4)] for g in range(n_dp // 8) for c in range(2)]
    eights = [[8 * g + k for k in range(8)] for g in range(n_dp // 8)]

    def to_peer(value, e):
        return lax.ppermute(value, "dp", [(i, i ^ e) for i in range(n_dp)])

    def along(value, step):
        return lax.ppermute(value, "tensor", [(i, (i + step) % 4) for i in range(4)])

    def hop(value, pairs):
        return lax.ppermute(value, "tensor", pairs)

    def row(vec):
        return vec.reshape(1, -1)

    def after(values, *others):
        return lax.optimization_barrier((values, others))[0]

    def lower(terms):
        return sum(v.astype(F32) for v in terms).astype(BF16)

    act, wide = struct((ROWS, D), BF16), struct((ROWS, D), F32)
    quad_rows, low_rows = struct((L1_ROW, D), BF16), struct((USED - L1_ROW, D), BF16)
    extended, narrow = pltpu.VMEM((EXT, D), F32), pltpu.VMEM((EXT, 128), BF16)
    sum_heads, spread_heads = pltpu.VMEM((8 * D, 128), BF16), pltpu.VMEM((128, 8 * D), BF16)

    piece_a = jnp.concatenate(
        [
            lax.dynamic_slice(w_qkv, (0, 64 * sub, 0), (3, 64, 128)),
            lax.dynamic_slice(w_out, (64 * (sub % 2), 128 * (sub // 2)), (64, 128))[None],
        ],
        axis=0,
    )
    piece = jnp.concatenate(
        [
            lax.dynamic_slice(w_up, (64 * sub, 0), (64, D)),
            lax.dynamic_slice(w_down, (64 * sub, 0), (64, D)),
            row(b_up),
            jnp.zeros((15, D), BF16),
            piece_a.swapaxes(0, 1).reshape(64, D),
        ],
        axis=0,
    )
    arrived = [along(piece, s) for s in (1, 2, 3)]
    first_a = jnp.stack([v[144:].reshape(64, 4, 128).swapaxes(0, 1) for v in arrived])
    first_b = jnp.stack([v[:144] for v in arrived])
    plane_a = lax.all_gather(first_a, "dp", axis=0, axis_index_groups=planes)
    other_a = to_peer(plane_a, 1)
    pieces_b = lax.all_gather(first_b, "dp", axis=0, axis_index_groups=eights)

    def bring(rows, *others):
        cuts = [rows[SEND_LO:]]
        for w in range(3):
            cuts.append(jnp.concatenate([rows[at : at + size] for at, size in ((LOW_HEAD[w], 192), (LOW_TAIL[w], 64))]))
        cuts = after(cuts, *others)
        return [hop(cuts[0], [(0, 1), (1, 2), (2, 3)])] + [hop(cuts[1 + w], [(3, w)]) for w in range(3)]

    token_rows = bring(tokens, first_a)
    grad_rows = bring(cotangent, *token_rows)
    rows_low = pltpu.VMEM((ROWS, D), BF16)
    all_rows = pltpu.VMEM((3, ROWS, D), BF16)
    weights = pltpu.VMEM((4, D, D), BF16)
    piece_rows = pltpu.VMEM((4, 3, 4, 64, 128), BF16)
    low_extended = pltpu.VMEM((EXT, D), BF16)
    sems = pltpu.SemaphoreType.DMA
    x, n_one, qkv, prob, ctx, mid, w_full = call(
        attention_forward,
        "attention_forward",
        [lengths, tokens] + token_rows + [row(ln1_gain), row(ln1_shift), row(b_out), w_qkv, w_out, plane_a, other_a],
        [act, act, struct((3, ROWS, D), BF16), struct((ROWS, 128), F32), act, wide, struct((4, D, D), BF16)],
        [
            rows_low,
            rows_low,
            all_rows,
            weights,
            pltpu.VMEM((3, D, 128), BF16),
            pltpu.VMEM((128, D), BF16),
            piece_rows,
            piece_rows,
            low_extended,
            extended,
            sum_heads,
            spread_heads,
            sems((4,)),
            sems((4,)),
        ],
        far_ins=(9, 10, 11, 12),
        far_outs=(0, 1, 2, 6),
    )
    half_b = struct((4, 4, 128, D), BF16)
    square = pltpu.VMEM((D, D), BF16)
    turned = pltpu.VMEM((D, ROWS), BF16)
    y_quad, y_low, keep_b, send_b, gnorm, grad, small_up = call(
        feed_forward,
        "feed_forward",
        [cotangent]
        + grad_rows
        + [mid, row(ln2_gain), row(ln2_shift), row(b_down), w_up, row(b_up), w_down, pieces_b],
        [quad_rows, low_rows, half_b, half_b, wide, act, struct((4, D), F32)],
        [weights, weights, square, square, pltpu.VMEM((4, D), F32), rows_low, rows_low, turned, turned]
        + [rows_low, rows_low, pltpu.VMEM((ROWS, D), F32), pltpu.VMEM((2, D, D), BF16)]
        + [pltpu.VMEM((8, 3, 144, D), BF16), pltpu.VMEM((4, 4, 128, D), BF16), pltpu.VMEM((4, 4, 128, D), BF16)]
        + [sems((3,)), sems((9,))],
        far_ins=(9, 11, 12),
        far_outs=(2, 3, 5),
    )
    far_send = to_peer(send_b, 1)
    piece_b = struct((4, 128, D), BF16)
    quarters = pltpu.VMEM((4, 4, 128, D), BF16)
    gmid, gcontext, gw_out, small, *both_b = call(
        norm_backward,
        "norm_backward",
        [lengths, mid, gnorm, grad, row(ln2_gain), ctx, w_full, keep_b, far_send],
        [wide, act, struct((D, D), BF16), struct((8, D), F32)] + [piece_b] * 4,
        [rows_low, square, rows_low, quarters, quarters, sems((4,))],
        25000000,
        far_ins=(5, 6, 7, 8),
    )

    def across(value, bits):
        return lax.ppermute(value, "tensor", [(i, i ^ bits) for i in range(4)])

    def wider(plane):
        bit = 8
        while bit < n_dp:
            plane = [lower([v, to_peer(v, bit)]) for v in plane]
            bit *= 2
        return plane

    left = [(1, 0), (2, 1), (3, 2)]
    y_lows = [hop(y_low, [(w, 3)]) for w in range(3)]
    gcontext = after(gcontext, y_lows[0], y_lows[1])
    y_recv = hop(after(y_quad, gcontext, y_lows[0], y_lows[1]), left)
    half_a = struct((4, 4, 288, 128), BF16)
    g_quad, g_low, keep_a, send_a = call(
        attention_backward,
        "attention_backward",
        [qkv, prob, gcontext, row(ln1_gain), small, small_up, gmid, x, n_one, gw_out, w_full],
        [quad_rows, low_rows, half_a, half_a],
        [extended, extended, narrow, narrow, sum_heads, spread_heads, all_rows, pltpu.VMEM((3, D, D), BF16)]
        + [low_extended, pltpu.VMEM((ROWS, D), F32), rows_low, rows_low, square, weights]
        + [pltpu.VMEM((ROWS, 128), F32), sems((5,))],
        60000000,
        far_ins=(6, 7, 8, 9, 10),
    )
    parts_b = after([both_b[0]] + [to_peer(both_b[k], 2 * k) for k in (1, 2, 3)], keep_a)
    far_a = to_peer(after(send_a, y_recv, *y_lows, *parts_b), 1)
    plane_b = wider([lower([v[s] for v in parts_b]) for s in range(4)])
    far_b = [across(plane_b[s], s) for s in (1, 2, 3)]
    both_a = lower([keep_a, far_a])
    parts_a = lax.all_to_all(both_a, "dp", 0, 0, axis_index_groups=planes, tiled=True)
    g_lows = [hop(after(g_low, both_a), [(w, 3)]) for w in range(3)]
    g_recv = hop(after(g_quad, both_a), left)
    parts_a = after(parts_a, g_recv, *g_lows)
    mine_b = lower([plane_b[0]] + after(far_b, parts_a))
    plane_a = wider([lower([parts_a[i, s] for i in range(4)]) for s in range(4)])
    flat_b = lax.all_gather(mine_b, "dp", axis=0, axis_index_groups=eights)
    output = call(
        spread_rows, "spread_rows", [after(y_quad, both_a), y_low, y_recv] + y_lows, [struct((SHARD, D), BF16)]
    )[0]
    mine_a = lower([plane_a[0]] + [across(plane_a[s], s) for s in (1, 2, 3)])
    grad_tokens = call(
        spread_rows, "spread_rows", [after(g_quad, parts_a), g_low, g_recv] + g_lows, [struct((SHARD, D), F32)]
    )[0]
    mine_a = after(mine_a, output, grad_tokens, mine_b)
    flat_a = lax.all_gather(mine_a, "dp", axis=0, axis_index_groups=eights)
    g_qkv, g_out, g_up, g_down = call(
        unpack_weights,
        "unpack_weights",
        [flat_a, flat_b],
        [struct((3, D, 128), F32), struct((128, D), F32), struct((D, D), F32), struct((D, D), F32)],
        [pltpu.VMEM((D, D), F32)],
    )
    sums = mine_a[256:284].astype(F32).reshape(7, D)
    return (
        output,
        grad_tokens,
        sums[4],
        sums[5],
        g_qkv,
        g_out,
        sums[3],
        sums[1],
        sums[2],
        g_up,
        sums[6],
        g_down,
        sums[0],
    )


def solution(mesh):
    n_dp = mesh.shape["dp"]
    placed = (
        P(("dp", "tensor"), None),
        P(("dp", "tensor"), None),
        P("dp"),
        P("dp", None),
        P(),
        P(),
        P(None, None, "tensor"),
        P("tensor", None),
        P(),
        P(),
        P(),
        P(None, "tensor"),
        P("tensor"),
        P("tensor", None),
        P(),
    )

    def run(*args):
        return shards(*args, n_dp)

    return jax.shard_map(
        run,
        mesh=mesh,
        in_specs=placed,
        out_specs=(
            P(("dp", "tensor"), None),
            P(("dp", "tensor"), None),
            P(),
            P(),
            P(None, None, "tensor"),
            P("tensor", None),
            P(),
            P(),
            P(),
            P(None, "tensor"),
            P("tensor"),
            P("tensor", None),
            P(),
        ),
        check_vma=False,
    )
```

profile of v0, /device:TPU:0, one launch (start us, length us, event | category | flops | bytes accessed | tf_op | source)
XLA Modules:
  0.0 241.2 jit_solution(8466039506265421970)
XLA Ops:
  7.3 0.8 reshape.141.b_up
  8.0 0.8 constant_dynamic-slice_fusion
  9.6 0.9 constant_dynamic-slice_fusion.1
  10.6 5.1 %collective-permute-start.2 = (bf16[208,512]{1,0:T(8,128)(2,1)S(1)}, bf16[208,512]{1,0:T(8,128)(2,1)S(1)}, u32[]{:S(2)}, u32[]{:S(2)}) collective-permute-start(bf16[208,512]{1,0:T(8,128)(2,1)S(1)} %concatenate.31), channel_id=1, source_target_pairs={{0,3},{1,0},{2,1},{3,2},{4,7},{5,4},{6,5},{7,6},{8,11},{9,8},{10,9... | collective-permute-start | bytes 638984 | tf_op jit(solution)/shard_map/ppermute | solution.py:541
  15.7 1.0 collective-permute-start.1
  16.7 4.6 %collective-permute-done.2 = bf16[208,512]{1,0:T(8,128)(2,1)S(1)} collective-permute-done((bf16[208,512]{1,0:T(8,128)(2,1)S(1)}, bf16[208,512]{1,0:T(8,128)(2,1)S(1)}, u32[]{:S(2)}, u32[]{:S(2)}) %collective-permute-start.2) | collective-permute-done | bytes 213024 | tf_op jit(solution)/shard_map/ppermute | solution.py:541
  21.4 12.4 %collective-permute-done.1 = bf16[208,512]{1,0:T(8,128)(2,1)S(1)} collective-permute-done((bf16[208,512]{1,0:T(8,128)(2,1)S(1)}, bf16[208,512]{1,0:T(8,128)(2,1)S(1)}, u32[]{:S(2)}, u32[]{:S(2)}) %collective-permute-start.1) | collective-permute-done | bytes 213024 | tf_op jit(solution)/shard_map/ppermute | solution.py:541
  33.9 0.8 pad_maximum_fusion
  34.7 0.9 slice.194
  36.4 0.8 pad_maximum_fusion.4
  37.5 1.8 collective-permute-start.3
  39.4 0.8 pad_maximum_fusion.1
  40.3 1.3 collective-permute-start.4
  42.9 13.7 %all-gather = bf16[12,4,64,128]{3,2,1,0:T(8,128)(2,1)S(1)} all-gather(bf16[3,4,64,128]{3,2,1,0:T(8,128)(2,1)S(1)} %copy.33), channel_id=2, replica_groups={{0,8,16,24},{4,12,20,28},{1,9,17,25},{5,13,21,29},{2,10,18,26},{6,14,22..., dimensions={0}, use_global_device_ids=true | all-gather | bytes 983040 | tf_op jit(solution)/shard_map/all_gather | solution.py:580
  56.7 0.9 pad_maximum_fusion.3
  57.7 3.8 %collective-permute-start.7 = (bf16[720,512]{1,0:T(8,128)(2,1)S(1)}, bf16[720,512]{1,0:T(8,128)(2,1)S(1)}, u32[]{:S(2)}, u32[]{:S(2)}) collective-permute-start(bf16[720,512]{1,0:T(8,128)(2,1)S(1)} %slice.187), channel_id=1, source_target_pairs={{0,1},{1,2},{2,3},{4,5},{5,6},{6,7},{8,9},{9,10},{10,11},{12,13},{... | collective-permute-start | bytes 2211848 | tf_op jit(solution)/shard_map/ppermute | solution.py:544
  62.3 1.3 collective-permute-start.8
  63.6 1.9 collective-permute-start.9
  65.5 0.8 copy-done.6
  66.3 15.2 %attention_forward.1 = (bf16[1024,512]{1,0:T(8,128)(2,1)}, bf16[1024,512]{1,0:T(8,128)(2,1)}, bf16[3,1024,512]{2,1,0:T(8,128)(2,1)}, f32[1024,128]{1,0:T(8,128)}...) custom-call(s32[4]{0:T(128)} %lengths.3, bf16[960,512]{1,0:T(8,128)(2,1)} %own.2, ...), custom_call_target="tpu_custom_call" | custom-call | flops 1000 | bytes 1000 | tf_op jit(solution)/shard_map/attention_forward/pallas_call | solution.py:499
  82.5 26.4 %feed_forward.1 = (bf16[768,512]{1,0:T(8,128)(2,1)}, bf16[240,512]{1,0:T(8,128)(2,1)}, bf16[4,4,128,512]{3,2,1,0:T(8,128)(2,1)}, bf16[4,4,128,512]{3,2,1,0:T(8,1...) custom-call(bf16[960,512]{1,0:T(8,128)(2,1)} %own.3, bf16[720,512]{1,0:T(8,128)(2,1)} %copy-done.10, ...), custom_call_target="tpu_custom_call" | custom-call | flops 1000 | bytes 1000 | tf_op jit(solution)/shard_map/feed_forward/pallas_call | solution.py:499
  109.1 9.2 %collective-permute-start.13 = (bf16[240,512]{1,0:T(8,128)(2,1)}, bf16[240,512]{1,0:T(8,128)(2,1)S(1)}, u32[]{:S(2)}, u32[]{:S(2)}) collective-permute-start(bf16[240,512]{1,0:T(8,128)(2,1)} %get-tuple-element.86.low), channel_id=1, source_target_pairs={{0,3},{4,7},{8,11},{12,15},{16,19},{20,23},{24,27},{28,31}} | collective-permute-start | bytes 737288 | tf_op jit(solution)/shard_map/ppermute | solution.py:544
  119.0 1.3 copy-done.3
  120.4 8.6 %norm_backward.1 = (f32[1024,512]{1,0:T(8,128)}, bf16[1024,512]{1,0:T(8,128)(2,1)}, bf16[512,512]{1,0:T(8,128)(2,1)}, f32[8,512]{1,0:T(8,128)}, bf16[4,128,512]{...) custom-call(s32[4]{0:T(128)} %lengths.3, ...), custom_call_target="tpu_custom_call" | custom-call | flops 1000 | bytes 25000000 | tf_op jit(solution)/shard_map/norm_backward/pallas_call | solution.py:499
  129.0 1.3 collective-permute-start.15
  130.3 1.6 collective-permute-start.17
  131.9 1.5 collective-permute-start.18
  133.9 0.9 collective-permute-start.16
  134.8 16.3 %attention_backward.1 = (bf16[768,512]{1,0:T(8,128)(2,1)}, bf16[240,512]{1,0:T(8,128)(2,1)}, bf16[4,4,288,128]{3,2,1,0:T(8,128)(2,1)}, bf16[4,4,288,128]{3,2,1,0:T(8,128)(2,1)}) custom-call(bf16[3,1024,512]{2,1,0:T(8,128)(2,1)} %get-tuple-element.77.qkv, f32[1024,128]{1,0:T(8,128)} %get-tuple-element.78.prob, bf16[1024,512]{1,0:T(8,128)(2,1)} %get-tuple-element.87.gcontext, ...), custom_call_target="tpu_custom_call" | custom-call | flops 1000 | bytes 60000000 | tf_op jit(solution)/shard_map/attention_backward/pallas_call | solution.py:499
  151.1 6.0 %collective-permute-done.18 = bf16[4,128,512]{2,1,0:T(8,128)(2,1)S(1)} collective-permute-done((bf16[4,128,512]{2,1,0:T(8,128)(2,1)}, bf16[4,128,512]{2,1,0:T(8,128)(2,1)S(1)}, u32[]{:S(2)}, u32[]{:S(2)}) %collective-permute-start.18) | collective-permute-done | bytes 524320 | tf_op jit(solution)/shard_map/ppermute | solution.py:538
  157.1 0.8 copy-done.13
  158.2 3.0 %collective-permute-done.20 = bf16[4,4,288,128]{3,2,1,0:T(8,128)(2,1)S(1)} collective-permute-done((bf16[4,4,288,128]{3,2,1,0:T(8,128)(2,1)}, bf16[4,4,288,128]{3,2,1,0:T(8,128)(2,1)S(1)}, u32[]{:S(2)}, u32[]{:S(2)}) %collective-permute-start.20) | collective-permute-done | bytes 1179680 | tf_op jit(solution)/shard_map/ppermute | solution.py:538
  161.3 2.6 %add_convert_fusion = bf16[4,4,288,128]{3,2,1,0:T(8,128)(2,1)} fusion(bf16[4,4,288,128]{3,2,1,0:T(8,128)(2,1)S(1)} %collective-permute-done.20, bf16[4,4,288,128]{3,2,1,0:T(8,128)(2,1)} %get-tuple-element.94), kind=kLoop, calls=%fused_computation | loop fusion | flops 2359296 | bytes 3538944 | tf_op jit(solution)/shard_map/convert_element_type | solution.py:553
  163.9 3.5 %all-to-all-start = ((bf16[4,4,288,128]{3,2,1,0:T(8,128)(2,1)}), bf16[4,4,288,128]{3,2,1,0:T(8,128)(2,1)S(1)}, u32[]{:S(2)}, u32[]{:S(2)}) async-start(bf16[4,4,288,128]{3,2,1,0:T(8,128)(2,1)} %add_convert_fusion), calls=%async_computation | async-start | bytes 2359296 | tf_op jit(solution)/shard_map/all_to_all | solution.py:684
  167.5 1.3 collective-permute-start.21
  168.8 7.9 %collective-permute-start.22 = (bf16[240,512]{1,0:T(8,128)(2,1)S(1)}, bf16[240,512]{1,0:T(8,128)(2,1)S(1)}, u32[]{:S(2)}, u32[]{:S(2)}) collective-permute-start(bf16[240,512]{1,0:T(8,128)(2,1)S(1)} %copy-done.23), channel_id=1, source_target_pairs={{0,3},{4,7},{8,11},{12,15},{16,19},{20,23},{24,27},{28,31}} | collective-permute-start | bytes 737288 | tf_op jit(solution)/shard_map/ppermute | solution.py:544
  177.3 0.9 collective-permute-start.24
  178.3 2.2 fusion.9
  180.5 1.2 collective-permute-start.28
  182.4 12.0 %collective-permute-start.30 = (bf16[128,512]{1,0:T(8,128)(2,1)}, bf16[128,512]{1,0:T(8,128)(2,1)}, u32[]{:S(2)}, u32[]{:S(2)}) collective-permute-start(bf16[128,512]{1,0:T(8,128)(2,1)} %get-tuple-element.121), channel_id=1, source_target_pairs={{0,3},{1,2},{2,1},{3,0},{4,7},{5,6},{6,5},{7,4},{8,11},{9,10},{10,... | collective-permute-start | bytes 393224 | tf_op jit(solution)/shard_map/ppermute | solution.py:654
  195.6 5.3 %collective-permute-done.30 = bf16[128,512]{1,0:T(8,128)(2,1)} collective-permute-done((bf16[128,512]{1,0:T(8,128)(2,1)}, bf16[128,512]{1,0:T(8,128)(2,1)}, u32[]{:S(2)}, u32[]{:S(2)}) %collective-permute-start.30) | collective-permute-done | bytes 131104 | tf_op jit(solution)/shard_map/ppermute | solution.py:654
  200.8 2.0 fusion.2
  203.0 2.2 collective-permute-start.25
  205.2 2.8 %collective-permute-start.26 = (bf16[288,128]{1,0:T(8,128)(2,1)S(1)}, bf16[288,128]{1,0:T(8,128)(2,1)S(1)}, u32[]{:S(2)}, u32[]{:S(2)}) collective-permute-start(bf16[288,128]{1,0:T(8,128)(2,1)S(1)} %get-tuple-element.125), channel_id=1, source_target_pairs={{0,2},{1,3},{2,0},{3,1},{4,6},{5,7},{6,4},{7,5},{8,10},{9,11},{10,... | collective-permute-start | bytes 221192 | tf_op jit(solution)/shard_map/ppermute | solution.py:654
  208.0 4.8 %spread_rows.2 = bf16[960,512]{1,0:T(8,128)(2,1)} custom-call(bf16[768,512]{1,0:T(8,128)(2,1)} %get-tuple-element.106.quad, bf16[240,512]{1,0:T(8,128)(2,1)} %get-tuple-element.86.low, bf16[768,512]{1,0:T(8,128)(2,1)} %copy-done.5, bf16[240,512]{1,0:T(8,128)(2,1)} %copy-done.20, bf16[240,512]{1,0:T(8,128)(2,1)} %copy-done.21, bf16[240,512]{1,0:T(8,128)(2,1)} %copy-done.22), custom_call_target="tpu_custom_call" | custom-call | flops 1000 | bytes 1000 | tf_op jit(solution)/shard_map/spread_rows/pallas_call | solution.py:499
  212.7 5.1 %spread_rows.3 = f32[960,512]{1,0:T(8,128)} custom-call(bf16[768,512]{1,0:T(8,128)(2,1)} %get-tuple-element.112.quad, bf16[240,512]{1,0:T(8,128)(2,1)} %get-tuple-element.110.low, bf16[768,512]{1,0:T(8,128)(2,1)} %copy-done.8, bf16[240,512]{1,0:T(8,128)(2,1)} %copy-done.24, bf16[240,512]{1,0:T(8,128)(2,1)} %copy-done.25, bf16[240,512]{1,0:T(8,128)(2,1)} %copy-done.26), custom_call_target="tpu_custom_call" | custom-call | flops 1000 | bytes 1000 | tf_op jit(solution)/shard_map/spread_rows/pallas_call | solution.py:499
  217.9 12.3 %all-gather.2 = bf16[2304,128]{1,0:T(8,128)(2,1)} all-gather(bf16[288,128]{1,0:T(8,128)(2,1)S(1)} %fusion.5), channel_id=4, replica_groups={{0,4,8,12,16,20,24,28},{1,5,9,13,17,21,25,29},{2,6,10,14,18,22,26,30},{..., dimensions={0}, use_global_device_ids=true | all-gather | bytes 663552 | tf_op jit(solution)/shard_map/all_gather | solution.py:699
  230.8 3.3 %unpack_weights.1 = (f32[3,512,128]{2,1,0:T(8,128)}, f32[128,512]{1,0:T(8,128)}, f32[512,512]{1,0:T(8,128)}, f32[512,512]{1,0:T(8,128)}) custom-call(bf16[8,288,128]{2,1,0:T(8,128)(2,1)} %bitcast.72, bf16[8,128,512]{2,1,0:T(8,128)(2,1)} %bitcast.73), custom_call_target="tpu_custom_call" | custom-call | flops 1000 | bytes 1000 | tf_op jit(solution)/shard_map/unpack_weights/pallas_call | solution.py:499
  (123 shorter events, 10.1 us)
Async XLA Ops:
  7.2 27.5 %copy-start = (bf16[960,512]{1,0:T(8,128)(2,1)S(1)}, bf16[960,512]{1,0:T(8,128)(2,1)}, u32[]{:S(2)}) copy-start(bf16[960,512]{1,0:T(8,128)(2,1)} %own.2) | copy-start | bytes 2949124
  7.2 74.5 %all-gather.7.cloned.1.call-start = ((), (), s32[]{:S(2)}) async-start(), calls=%async_computation.1 | async-start | bytes 3981312 | tf_op jit(solution)/shard_map/all_gather | solution.py:582
  8.0 27.6 %copy-start.27 = (bf16[1,512]{1,0:T(2,128)(2,1)}, bf16[1,512]{1,0:T(2,128)(2,1)S(1)}, u32[]{:S(2)}) copy-start(bf16[1,512]{1,0:T(2,128)(2,1)S(1)} %reshape.141.b_up) | copy-start | bytes 3076
  10.6 10.8 %collective-permute-start.2 = (bf16[208,512]{1,0:T(8,128)(2,1)S(1)}, bf16[208,512]{1,0:T(8,128)(2,1)S(1)}, u32[]{:S(2)}, u32[]{:S(2)}) collective-permute-start(bf16[208,512]{1,0:T(8,128)(2,1)S(1)} %concatenate.31), channel_id=1, source_target_pairs={{0,3},{1,0},{2,1},{3,2},{4,7},{5,4},{6,5},{7,6},{8,11},{9,8},{10,9... | collective-permute-start | bytes 638984 | tf_op jit(solution)/shard_map/ppermute | solution.py:541
  15.7 18.1 %collective-permute-start = (bf16[208,512]{1,0:T(8,128)(2,1)S(1)}, bf16[208,512]{1,0:T(8,128)(2,1)S(1)}, u32[]{:S(2)}, u32[]{:S(2)}) collective-permute-start(bf16[208,512]{1,0:T(8,128)(2,1)S(1)} %concatenate.31), channel_id=1, source_target_pairs={{0,1},{1,2},{2,3},{3,0},{4,5},{5,6},{6,7},{7,4},{8,9},{9,10},{10,1... | collective-permute-start | bytes 638984 | tf_op jit(solution)/shard_map/ppermute | solution.py:541
  15.7 18.1 %collective-permute-start.1 = (bf16[208,512]{1,0:T(8,128)(2,1)S(1)}, bf16[208,512]{1,0:T(8,128)(2,1)S(1)}, u32[]{:S(2)}, u32[]{:S(2)}) collective-permute-start(bf16[208,512]{1,0:T(8,128)(2,1)S(1)} %concatenate.31), channel_id=1, source_target_pairs={{0,2},{1,3},{2,0},{3,1},{4,6},{5,7},{6,4},{7,5},{8,10},{9,11},{10,... | collective-permute-start | bytes 638984 | tf_op jit(solution)/shard_map/ppermute | solution.py:541
  37.5 20.2 %collective-permute-start.3 = (bf16[720,512]{1,0:T(8,128)(2,1)}, bf16[720,512]{1,0:T(8,128)(2,1)S(1)}, u32[]{:S(2)}, u32[]{:S(2)}) collective-permute-start(bf16[720,512]{1,0:T(8,128)(2,1)} %slice.194), channel_id=1, source_target_pairs={{0,1},{1,2},{2,3},{4,5},{5,6},{6,7},{8,9},{9,10},{10,11},{12,13},{... | collective-permute-start | bytes 2211848 | tf_op jit(solution)/shard_map/ppermute | solution.py:544
  40.3 17.4 %collective-permute-start.4 = (bf16[256,512]{1,0:T(8,128)(2,1)}, bf16[256,512]{1,0:T(8,128)(2,1)S(1)}, u32[]{:S(2)}, u32[]{:S(2)}) collective-permute-start(bf16[256,512]{1,0:T(8,128)(2,1)} %get-tuple-element.68), channel_id=1, source_target_pairs={{3,0},{7,4},{11,8},{15,12},{19,16},{23,20},{27,24},{31,28}} | collective-permute-start | bytes 786440 | tf_op jit(solution)/shard_map/ppermute | solution.py:544
  41.6 16.1 %collective-permute-start.5 = (bf16[256,512]{1,0:T(8,128)(2,1)}, bf16[256,512]{1,0:T(8,128)(2,1)S(1)}, u32[]{:S(2)}, u32[]{:S(2)}) collective-permute-start(bf16[256,512]{1,0:T(8,128)(2,1)} %get-tuple-element.69), channel_id=1, source_target_pairs={{3,1},{7,5},{11,9},{15,13},{19,17},{23,21},{27,25},{31,29}} | collective-permute-start | bytes 786440 | tf_op jit(solution)/shard_map/ppermute | solution.py:544
  42.2 15.4 %collective-permute-start.6 = (bf16[256,512]{1,0:T(8,128)(2,1)}, bf16[256,512]{1,0:T(8,128)(2,1)S(1)}, u32[]{:S(2)}, u32[]{:S(2)}) collective-permute-start(bf16[256,512]{1,0:T(8,128)(2,1)} %pad_maximum_fusion.6), channel_id=1, source_target_pairs={{3,2},{7,6},{11,10},{15,14},{19,18},{23,22},{27,26},{31,30}} | collective-permute-start | bytes 786440 | tf_op jit(solution)/shard_map/ppermute | solution.py:544
  56.6 8.9 %copy-start.2 = (bf16[12,4,64,128]{3,2,1,0:T(8,128)(2,1)}, bf16[12,4,64,128]{3,2,1,0:T(8,128)(2,1)S(1)}, u32[]{:S(2)}) copy-start(bf16[12,4,64,128]{3,2,1,0:T(8,128)(2,1)S(1)} %all-gather) | copy-start | bytes 2359300
  56.6 8.8 %collective-permute-start.11 = (bf16[4,3,4,64,128]{4,3,2,1,0:T(8,128)(2,1)S(1)}, bf16[4,3,4,64,128]{4,3,2,1,0:T(8,128)(2,1)S(1)}, u32[]{:S(2)}, u32[]{:S(2)}) collective-permute-start(bf16[4,3,4,64,128]{4,3,2,1,0:T(8,128)(2,1)S(1)} %bitcast.70), channel_id=1, source_target_pairs={{0,4},{4,0},{8,12},{12,8},{16,20},{20,16},{24,28},{28,24},{1,5},{5... | collective-permute-start | bytes 2359304 | tf_op jit(solution)/shard_map/ppermute | solution.py:538
  57.6 7.8 %copy-start.15 = (bf16[256,512]{1,0:T(8,128)(2,1)}, bf16[256,512]{1,0:T(8,128)(2,1)S(1)}, u32[]{:S(2)}) copy-start(bf16[256,512]{1,0:T(8,128)(2,1)S(1)} %collective-permute-done.4.low0) | copy-start | bytes 786436
  57.7 7.8 %copy-start.16 = (bf16[256,512]{1,0:T(8,128)(2,1)}, bf16[256,512]{1,0:T(8,128)(2,1)S(1)}, u32[]{:S(2)}) copy-start(bf16[256,512]{1,0:T(8,128)(2,1)S(1)} %collective-permute-done.5.low1) | copy-start | bytes 786436
  57.7 23.9 %collective-permute-start.7 = (bf16[720,512]{1,0:T(8,128)(2,1)S(1)}, bf16[720,512]{1,0:T(8,128)(2,1)S(1)}, u32[]{:S(2)}, u32[]{:S(2)}) collective-permute-start(bf16[720,512]{1,0:T(8,128)(2,1)S(1)} %slice.187), channel_id=1, source_target_pairs={{0,1},{1,2},{2,3},{4,5},{5,6},{6,7},{8,9},{9,10},{10,11},{12,13},{... | collective-permute-start | bytes 2211848 | tf_op jit(solution)/shard_map/ppermute | solution.py:544
  61.6 20.0 %collective-permute-start.10 = (bf16[256,512]{1,0:T(8,128)(2,1)}, bf16[256,512]{1,0:T(8,128)(2,1)S(1)}, u32[]{:S(2)}, u32[]{:S(2)}) collective-permute-start(bf16[256,512]{1,0:T(8,128)(2,1)} %pad_maximum_fusion.3), channel_id=1, source_target_pairs={{3,2},{7,6},{11,10},{15,14},{19,18},{23,22},{27,26},{31,30}} | collective-permute-start | bytes 786440 | tf_op jit(solution)/shard_map/ppermute | solution.py:544
  62.3 19.4 %collective-permute-start.8 = (bf16[256,512]{1,0:T(8,128)(2,1)}, bf16[256,512]{1,0:T(8,128)(2,1)}, u32[]{:S(2)}, u32[]{:S(2)}) collective-permute-start(bf16[256,512]{1,0:T(8,128)(2,1)} %get-tuple-element.72), channel_id=1, source_target_pairs={{3,0},{7,4},{11,8},{15,12},{19,16},{23,20},{27,24},{31,28}} | collective-permute-start | bytes 786440 | tf_op jit(solution)/shard_map/ppermute | solution.py:544
  63.6 18.1 %collective-permute-start.9 = (bf16[256,512]{1,0:T(8,128)(2,1)}, bf16[256,512]{1,0:T(8,128)(2,1)}, u32[]{:S(2)}, u32[]{:S(2)}) collective-permute-start(bf16[256,512]{1,0:T(8,128)(2,1)} %get-tuple-element.73), channel_id=1, source_target_pairs={{3,1},{7,5},{11,9},{15,13},{19,17},{23,21},{27,25},{31,29}} | collective-permute-start | bytes 786440 | tf_op jit(solution)/shard_map/ppermute | solution.py:544
  109.0 10.0 %collective-permute-start.12 = (bf16[4,4,128,512]{3,2,1,0:T(8,128)(2,1)}, bf16[4,4,128,512]{3,2,1,0:T(8,128)(2,1)S(1)}, u32[]{:S(2)}, u32[]{:S(2)}) collective-permute-start(bf16[4,4,128,512]{3,2,1,0:T(8,128)(2,1)} %get-tuple-element.84), channel_id=1, source_target_pairs={{0,4},{4,0},{8,12},{12,8},{16,20},{20,16},{24,28},{28,24},{1,5},{5... | collective-permute-start | bytes 6291464 | tf_op jit(solution)/shard_map/ppermute | solution.py:538
  109.1 19.9 %collective-permute-start.13 = (bf16[240,512]{1,0:T(8,128)(2,1)}, bf16[240,512]{1,0:T(8,128)(2,1)S(1)}, u32[]{:S(2)}, u32[]{:S(2)}) collective-permute-start(bf16[240,512]{1,0:T(8,128)(2,1)} %get-tuple-element.86.low), channel_id=1, source_target_pairs={{0,3},{4,7},{8,11},{12,15},{16,19},{20,23},{24,27},{28,31}} | collective-permute-start | bytes 737288 | tf_op jit(solution)/shard_map/ppermute | solution.py:544
  118.3 10.7 %collective-permute-start.14 = (bf16[240,512]{1,0:T(8,128)(2,1)}, bf16[240,512]{1,0:T(8,128)(2,1)S(1)}, u32[]{:S(2)}, u32[]{:S(2)}) collective-permute-start(bf16[240,512]{1,0:T(8,128)(2,1)} %get-tuple-element.86.low), channel_id=1, source_target_pairs={{1,3},{5,7},{9,11},{13,15},{17,19},{21,23},{25,27},{29,31}} | collective-permute-start | bytes 737288 | tf_op jit(solution)/shard_map/ppermute | solution.py:544
  120.4 8.6 %copy-start.4 = (bf16[768,512]{1,0:T(8,128)(2,1)S(1)}, bf16[768,512]{1,0:T(8,128)(2,1)}, u32[]{:S(2)}) copy-start(bf16[768,512]{1,0:T(8,128)(2,1)} %get-tuple-element.106.quad) | copy-start | bytes 2359300
  120.4 13.5 %copy-start.19 = (bf16[240,512]{1,0:T(8,128)(2,1)S(1)}, bf16[240,512]{1,0:T(8,128)(2,1)}, u32[]{:S(2)}) copy-start(bf16[240,512]{1,0:T(8,128)(2,1)} %get-tuple-element.86.low) | copy-start | bytes 737284
  129.0 28.1 %collective-permute-start.15 = (bf16[768,512]{1,0:T(8,128)(2,1)S(1)}, bf16[768,512]{1,0:T(8,128)(2,1)S(1)}, u32[]{:S(2)}, u32[]{:S(2)}) collective-permute-start(bf16[768,512]{1,0:T(8,128)(2,1)S(1)} %copy-done.4), channel_id=1, source_target_pairs={{1,0},{2,1},{3,2},{5,4},{6,5},{7,6},{9,8},{10,9},{11,10},{13,12},{... | collective-permute-start | bytes 2359304 | tf_op jit(solution)/shard_map/ppermute | solution.py:544
  130.3 20.7 %collective-permute-start.17 = (bf16[4,128,512]{2,1,0:T(8,128)(2,1)}, bf16[4,128,512]{2,1,0:T(8,128)(2,1)S(1)}, u32[]{:S(2)}, u32[]{:S(2)}) collective-permute-start(bf16[4,128,512]{2,1,0:T(8,128)(2,1)} %get-tuple-element.98), channel_id=1, source_target_pairs={{0,8},{4,12},{8,0},{12,4},{16,24},{20,28},{24,16},{28,20},{1,9},{5... | collective-permute-start | bytes 1572872 | tf_op jit(solution)/shard_map/ppermute | solution.py:538
  131.9 25.2 %collective-permute-start.18 = (bf16[4,128,512]{2,1,0:T(8,128)(2,1)}, bf16[4,128,512]{2,1,0:T(8,128)(2,1)S(1)}, u32[]{:S(2)}, u32[]{:S(2)}) collective-permute-start(bf16[4,128,512]{2,1,0:T(8,128)(2,1)} %get-tuple-element.99), channel_id=1, source_target_pairs={{0,16},{4,20},{8,24},{12,28},{16,0},{20,4},{24,8},{28,12},{1,17},{... | collective-permute-start | bytes 1572872 | tf_op jit(solution)/shard_map/ppermute | solution.py:538
  133.4 23.7 %collective-permute-start.19 = (bf16[4,128,512]{2,1,0:T(8,128)(2,1)}, bf16[4,128,512]{2,1,0:T(8,128)(2,1)S(1)}, u32[]{:S(2)}, u32[]{:S(2)}) collective-permute-start(bf16[4,128,512]{2,1,0:T(8,128)(2,1)} %get-tuple-element.100), channel_id=1, source_target_pairs={{0,24},{4,28},{8,16},{12,20},{16,8},{20,12},{24,0},{28,4},{1,25},{... | collective-permute-start | bytes 1572872 | tf_op jit(solution)/shard_map/ppermute | solution.py:538
  133.9 23.2 %collective-permute-start.16 = (bf16[240,512]{1,0:T(8,128)(2,1)S(1)}, bf16[240,512]{1,0:T(8,128)(2,1)S(1)}, u32[]{:S(2)}, u32[]{:S(2)}) collective-permute-start(bf16[240,512]{1,0:T(8,128)(2,1)S(1)} %copy-done.19), channel_id=1, source_target_pairs={{2,3},{6,7},{10,11},{14,15},{18,19},{22,23},{26,27},{30,31}} | collective-permute-start | bytes 737288 | tf_op jit(solution)/shard_map/ppermute | solution.py:544
  151.1 12.8 %copy-start.12 = (bf16[4,128,512]{2,1,0:T(8,128)(2,1)}, bf16[4,128,512]{2,1,0:T(8,128)(2,1)S(1)}, u32[]{:S(2)}) copy-start(bf16[4,128,512]{2,1,0:T(8,128)(2,1)S(1)} %collective-permute-done.17) | copy-start | bytes 1572868
  158.1 9.3 %copy-start.7 = (bf16[768,512]{1,0:T(8,128)(2,1)S(1)}, bf16[768,512]{1,0:T(8,128)(2,1)}, u32[]{:S(2)}) copy-start(bf16[768,512]{1,0:T(8,128)(2,1)} %get-tuple-element.112.quad) | copy-start | bytes 2359300
  158.1 10.6 %copy-start.23 = (bf16[240,512]{1,0:T(8,128)(2,1)S(1)}, bf16[240,512]{1,0:T(8,128)(2,1)}, u32[]{:S(2)}) copy-start(bf16[240,512]{1,0:T(8,128)(2,1)} %get-tuple-element.110.low) | copy-start | bytes 737284
  158.1 20.1 %copy-start.11 = (bf16[4,128,512]{2,1,0:T(8,128)(2,1)S(1)}, bf16[4,128,512]{2,1,0:T(8,128)(2,1)}, u32[]{:S(2)}) copy-start(bf16[4,128,512]{2,1,0:T(8,128)(2,1)} %get-tuple-element.101) | copy-start | bytes 1572868
  158.1 3.1 %collective-permute-start.20 = (bf16[4,4,288,128]{3,2,1,0:T(8,128)(2,1)}, bf16[4,4,288,128]{3,2,1,0:T(8,128)(2,1)S(1)}, u32[]{:S(2)}, u32[]{:S(2)}) collective-permute-start(bf16[4,4,288,128]{3,2,1,0:T(8,128)(2,1)} %get-tuple-element.105), channel_id=1, source_target_pairs={{0,4},{4,0},{8,12},{12,8},{16,20},{20,16},{24,28},{28,24},{1,5},{5... | collective-permute-start | bytes 3538952 | tf_op jit(solution)/shard_map/ppermute | solution.py:538
  163.9 31.3 %all-to-all-start = ((bf16[4,4,288,128]{3,2,1,0:T(8,128)(2,1)}), bf16[4,4,288,128]{3,2,1,0:T(8,128)(2,1)S(1)}, u32[]{:S(2)}, u32[]{:S(2)}) async-start(bf16[4,4,288,128]{3,2,1,0:T(8,128)(2,1)} %add_convert_fusion), calls=%async_computation | async-start | bytes 2359296 | tf_op jit(solution)/shard_map/all_to_all | solution.py:684
  167.4 63.4 %all-gather.9.cloned.1.call-start = ((), (), s32[]{:S(2)}) async-start(), calls=%async_computation.2 | async-start | bytes 1179648 | tf_op jit(solution)/shard_map/all_gather | solution.py:690
  167.5 27.7 %collective-permute-start.21 = (bf16[768,512]{1,0:T(8,128)(2,1)S(1)}, bf16[768,512]{1,0:T(8,128)(2,1)S(1)}, u32[]{:S(2)}, u32[]{:S(2)}) collective-permute-start(bf16[768,512]{1,0:T(8,128)(2,1)S(1)} %copy-done.7), channel_id=1, source_target_pairs={{1,0},{2,1},{3,2},{5,4},{6,5},{7,6},{9,8},{10,9},{11,10},{13,12},{... | collective-permute-start | bytes 2359304 | tf_op jit(solution)/shard_map/ppermute | solution.py:544
  168.8 13.4 %collective-permute-start.22 = (bf16[240,512]{1,0:T(8,128)(2,1)S(1)}, bf16[240,512]{1,0:T(8,128)(2,1)S(1)}, u32[]{:S(2)}, u32[]{:S(2)}) collective-permute-start(bf16[240,512]{1,0:T(8,128)(2,1)S(1)} %copy-done.23), channel_id=1, source_target_pairs={{0,3},{4,7},{8,11},{12,15},{16,19},{20,23},{24,27},{28,31}} | collective-permute-start | bytes 737288 | tf_op jit(solution)/shard_map/ppermute | solution.py:544
  176.6 5.7 %collective-permute-start.23 = (bf16[240,512]{1,0:T(8,128)(2,1)S(1)}, bf16[240,512]{1,0:T(8,128)(2,1)S(1)}, u32[]{:S(2)}, u32[]{:S(2)}) collective-permute-start(bf16[240,512]{1,0:T(8,128)(2,1)S(1)} %copy-done.23), channel_id=1, source_target_pairs={{1,3},{5,7},{9,11},{13,15},{17,19},{21,23},{25,27},{29,31}} | collective-permute-start | bytes 737288 | tf_op jit(solution)/shard_map/ppermute | solution.py:544
  177.3 17.1 %collective-permute-start.24 = (bf16[240,512]{1,0:T(8,128)(2,1)S(1)}, bf16[240,512]{1,0:T(8,128)(2,1)S(1)}, u32[]{:S(2)}, u32[]{:S(2)}) collective-permute-start(bf16[240,512]{1,0:T(8,128)(2,1)S(1)} %copy-done.23), channel_id=1, source_target_pairs={{2,3},{6,7},{10,11},{14,15},{18,19},{22,23},{26,27},{30,31}} | collective-permute-start | bytes 737288 | tf_op jit(solution)/shard_map/ppermute | solution.py:544
  180.5 15.1 %collective-permute-start.28 = (bf16[128,512]{1,0:T(8,128)(2,1)}, bf16[128,512]{1,0:T(8,128)(2,1)}, u32[]{:S(2)}, u32[]{:S(2)}) collective-permute-start(bf16[128,512]{1,0:T(8,128)(2,1)} %get-tuple-element.123), channel_id=1, source_target_pairs={{0,1},{1,0},{2,3},{3,2},{4,5},{5,4},{6,7},{7,6},{8,9},{9,8},{10,11... | collective-permute-start | bytes 393224 | tf_op jit(solution)/shard_map/ppermute | solution.py:654
  182.2 12.2 %copy-start.24 = (bf16[240,512]{1,0:T(8,128)(2,1)}, bf16[240,512]{1,0:T(8,128)(2,1)S(1)}, u32[]{:S(2)}) copy-start(bf16[240,512]{1,0:T(8,128)(2,1)S(1)} %collective-permute-done.22.low0) | copy-start | bytes 737284
  182.2 13.4 %collective-permute-start.29 = (bf16[128,512]{1,0:T(8,128)(2,1)}, bf16[128,512]{1,0:T(8,128)(2,1)}, u32[]{:S(2)}, u32[]{:S(2)}) collective-permute-start(bf16[128,512]{1,0:T(8,128)(2,1)} %get-tuple-element.122), channel_id=1, source_target_pairs={{0,2},{1,3},{2,0},{3,1},{4,6},{5,7},{6,4},{7,5},{8,10},{9,11},{10,... | collective-permute-start | bytes 393224 | tf_op jit(solution)/shard_map/ppermute | solution.py:654
  182.4 12.1 %copy-start.25 = (bf16[240,512]{1,0:T(8,128)(2,1)}, bf16[240,512]{1,0:T(8,128)(2,1)S(1)}, u32[]{:S(2)}) copy-start(bf16[240,512]{1,0:T(8,128)(2,1)S(1)} %collective-permute-done.23.low1) | copy-start | bytes 737284
  182.4 18.4 %collective-permute-start.30 = (bf16[128,512]{1,0:T(8,128)(2,1)}, bf16[128,512]{1,0:T(8,128)(2,1)}, u32[]{:S(2)}, u32[]{:S(2)}) collective-permute-start(bf16[128,512]{1,0:T(8,128)(2,1)} %get-tuple-element.121), channel_id=1, source_target_pairs={{0,3},{1,2},{2,1},{3,0},{4,7},{5,6},{6,5},{7,4},{8,11},{9,10},{10,... | collective-permute-start | bytes 393224 | tf_op jit(solution)/shard_map/ppermute | solution.py:654
  195.2 17.6 %copy-start.8 = (bf16[768,512]{1,0:T(8,128)(2,1)}, bf16[768,512]{1,0:T(8,128)(2,1)S(1)}, u32[]{:S(2)}) copy-start(bf16[768,512]{1,0:T(8,128)(2,1)S(1)} %collective-permute-done.21.recv) | copy-start | bytes 2359300
  203.0 14.9 %collective-permute-start.25 = (bf16[288,128]{1,0:T(8,128)(2,1)S(1)}, bf16[288,128]{1,0:T(8,128)(2,1)S(1)}, u32[]{:S(2)}, u32[]{:S(2)}) collective-permute-start(bf16[288,128]{1,0:T(8,128)(2,1)S(1)} %get-tuple-element.124), channel_id=1, source_target_pairs={{0,1},{1,0},{2,3},{3,2},{4,5},{5,4},{6,7},{7,6},{8,9},{9,8},{10,11... | collective-permute-start | bytes 221192 | tf_op jit(solution)/shard_map/ppermute | solution.py:654
  205.2 12.6 %collective-permute-start.26 = (bf16[288,128]{1,0:T(8,128)(2,1)S(1)}, bf16[288,128]{1,0:T(8,128)(2,1)S(1)}, u32[]{:S(2)}, u32[]{:S(2)}) collective-permute-start(bf16[288,128]{1,0:T(8,128)(2,1)S(1)} %get-tuple-element.125), channel_id=1, source_target_pairs={{0,2},{1,3},{2,0},{3,1},{4,6},{5,7},{6,4},{7,5},{8,10},{9,11},{10,... | collective-permute-start | bytes 221192 | tf_op jit(solution)/shard_map/ppermute | solution.py:654
  207.9 9.9 %collective-permute-start.27 = (bf16[288,128]{1,0:T(8,128)(2,1)S(1)}, bf16[288,128]{1,0:T(8,128)(2,1)S(1)}, u32[]{:S(2)}, u32[]{:S(2)}) collective-permute-start(bf16[288,128]{1,0:T(8,128)(2,1)S(1)} %get-tuple-element.126), channel_id=1, source_target_pairs={{0,3},{1,2},{2,1},{3,0},{4,7},{5,6},{6,5},{7,4},{8,11},{9,10},{10,... | collective-permute-start | bytes 221192 | tf_op jit(solution)/shard_map/ppermute | solution.py:654
  (14 other events, 39.7 us)
Sparse Core Ops, SparseCore 0:
  34.8 35.9 all-gather.6
  202.9 26.9 all-gather.8
where the time goes:
time: 245 us; the launch traced here: 241 us
  Pallas kernels  79.6 us (32%)
  starting transfers between devices  66.8 us (27%)
  waiting for transfers between devices  32.5 us (13%)
  blocking collectives  26 us (11%)
  between operations  15 us (6%)
  other arithmetic  11.2 us (5%)
  local copies, waits for them, and re-layouts  9.98 us (4%)
    pallas_call x7, Pallas kernels, call(): pl.pallas_call(body, out_shape=tuple(outs), in_specs=specs, out_specs=tup...  79.6 us
    ppermute x16, starting transfers between devices, hop(): return lax.ppermute(value, 'tensor', pairs)  35 us
    ppermute x6, starting transfers between devices, across(): return lax.ppermute(value, 'tensor', [(i, i ^ bits) for i in range(4)])  18.4 us
    ppermute x3, waiting for transfers between devices, along(): lax.ppermute(value, 'tensor', [(i, (i + step) % 4) for i in range(4)])  17.1 us
    all_gather x1, blocking collectives, shards(): plane_a = lax.all_gather(first_a, 'dp', axis=0, axis_index_groups=planes)  13.7 us
    all_gather x1, blocking collectives, shards(): flat_a = lax.all_gather(mine_a, 'dp', axis=0, axis_index_groups=eights)  12.3 us
    ppermute x6, waiting for transfers between devices, to_peer(): return lax.ppermute(value, 'dp', [(i, i ^ e) for i in range(n_dp)])  9.09 us
    ppermute x3, starting transfers between devices, along(): lax.ppermute(value, 'tensor', [(i, (i + step) % 4) for i in range(4)])  6.11 us
  transfers between devices with their start and end apart: 34, of which 7 were waited for; matrix products, arithmetic and copies ran while one was open for 3% of the time, Pallas kernels for 21%

commit v1 on v0

--- a/solution.py
+++ b/solution.py
@@ -280,8 +280,6 @@
         cot = gathered_rows(start, t, own, recv, (low0, low1, low2)).astype(BF16)
         grad[run, :] = cot
         grad_t[:, run] = cot.T
-    total[...] = jnp.zeros_like(total)
-    gnorm[...] = jnp.zeros_like(gnorm)
     finish(loading)
     storing = begin(out_sems.at[8:9], (grad, grad_hbm))
     bias[0:1, :] = b_up[...].astype(F32)
@@ -292,13 +290,13 @@
     for s in range(1, 4):
         bias[s : s + 1, :] = arrived[0, s - 1, 128:129, :].astype(F32)
 
-    def hidden(s, carry):
+    for s in range(4):
         up_here, down_here = up_w[s], down_w[s]
         up_t[...] = up_here.T
         down_t[...] = down_here.T
         sums = jnp.zeros((1, D), F32)
-        for start in range(0, ROWS, 256):
-            run = slice(start, start + 256)
+        for start in range(0, ROWS, 512):
+            run = slice(start, start + 512)
             pre = dot_nn(normed[run, :], up_here) + bias[pl.ds(s, 1), :]
             square = pre * pre
             root = math.sqrt(2.0 / math.pi)
@@ -310,39 +308,40 @@
             act_s[run, :] = act
             gup_s[run, :] = gup
             sums = sums + jnp.sum(gup.astype(F32), axis=0, keepdims=True)
-            total[run, :] += dot_nn(act, down_here)
-            gnorm[run, :] += dot_nn(gup, up_t[...])
+            if s == 0:
+                total[run, :] = dot_nn(act, down_here)
+                gnorm[run, :] = dot_nn(gup, up_t[...])
+            else:
+                total[run, :] += dot_nn(act, down_here)
+                gnorm[run, :] += dot_nn(gup, up_t[...])
         grad_bias[pl.ds(s, 1), :] = sums
         tmp[0] = dot_nn(normed_t[...], gup_s[...]).astype(BF16)
         tmp[1] = dot_nn(grad_t[...], act_s[...]).astype(BF16)
-        slot = ((t - s) & 3) ^ t
+        slot = (t - s) & 3
         for half, target in enumerate((keep, send)):
             for k in range(4):
                 at = pl.multiple_of((me ^ (2 * k + half)) * 64, 64)
                 target[slot, k, 0:64, :] = tmp[0, pl.ds(at, 64), :]
                 target[slot, k, 64:128, :] = tmp[1, pl.ds(at, 64), :]
         begin(out_sems.at[pl.ds(2 * s, 2)], (keep.at[slot], keep_hbm.at[slot]), (send.at[slot], send_hbm.at[slot]))
-        return carry
-
-    lax.fori_loop(0, 4, hidden, 0)
     for start in range(0, ROWS, 256):
         run = slice(start, start + 256)
         out = (mid[run, :] + (total[run, :] + b_down[...])).astype(BF16)
         if start < L1_ROW:
             y_quad[run, :] = out
         else:
-            y_low[...] = out[0 : USED - L1_ROW, :]
+            y_low[...] = out
     for s in range(4):
         pltpu.make_async_copy(keep.at[s], keep_hbm.at[s], out_sems.at[2 * s]).wait()
         pltpu.make_async_copy(send.at[s], send_hbm.at[s], out_sems.at[2 * s + 1]).wait()
     finish(storing)
 
 
-def norm_backward(lengths, mid, gnorm, grad, gain, ctx, w_full, keep_hbm, far_hbm, *rest):
+def norm_backward(lengths, mid, gnorm, grad, gain, ctx, w_full, *rest):
     gmid, gcontext, gw_out, small = rest[:4]
-    both, (attn, w_here, ctx_here, keep, far, sems) = rest[4:8], rest[8:]
+    attn, w_here, ctx_here, sems = rest[4:]
     live_steps = lengths[lax.axis_index("tensor")] >> 4
-    loading = begin(sems, (w_full.at[3], w_here), (ctx, ctx_here), (keep_hbm, keep), (far_hbm, far))
+    loading = begin(sems, (w_full.at[3], w_here), (ctx, ctx_here))
     finish(loading[:1])
     sums = [jnp.zeros((1, D), F32) for _ in range(4)]
     for start in range(0, ROWS, 256):
@@ -364,10 +363,13 @@
         sums = [running + jnp.sum(term, axis=0, keepdims=True) for running, term in zip(sums, terms)]
     finish(loading[1:])
     gw_out[...] = dot_tn(ctx_here[...], attn[...]).astype(BF16)
+    small[...] = jnp.concatenate(sums + [jnp.zeros((4, D), F32)], axis=0)
+
+
+def pair_sum(keep, far, *both):
     for k in range(4):
         for slot in range(4):
             both[k][slot] = (keep[slot, k].astype(F32) + far[slot, k].astype(F32)).astype(BF16)
-    small[...] = jnp.concatenate(sums + [jnp.zeros((4, D), F32)], axis=0)
 
 
 REVERSE = (0, 2, 1)
@@ -469,13 +471,18 @@
                 target[k, slot, 256:288, :] = rows
 
 
-def spread_rows(quad, low, recv, low0, low1, low2, out):
-    t = lax.axis_index("tensor")
-    moved = recv[...] + jnp.concatenate([low0[...], low1[...], low2[...], jnp.zeros((48, D), BF16)], axis=0)
+def spread_rows(quad, low, recv, *rest):
+    t, (*lows, out) = lax.axis_index("tensor"), rest
+    count = USED - L1_ROW
+    if len(lows) == 3:
+        others = [part[...] for part in lows]
+    else:
+        others = [jnp.where(t == 3, lows[0][w, 0:count, :], jnp.zeros((count, D), BF16)) for w in range(3)]
+    moved = recv[...] + jnp.concatenate(others + [jnp.zeros((48, D), BF16)], axis=0)
     for start in range(0, SHARD, 240):
         source = spread_source(start, t)
         rows = dot_nn(one_hot(source, 0, L1_ROW), quad[...])
-        rows = rows + dot_nn(one_hot(source, L1_ROW, USED - L1_ROW), low[...])
+        rows = rows + dot_nn(one_hot(source, L1_ROW, count), low[0:count, :])
         rows = rows + dot_nn(one_hot(source, ROWS, L1_ROW), moved)
         out[start : start + 240, :] = rows.astype(out.dtype)
 
@@ -629,7 +636,7 @@
         [cotangent]
         + grad_rows
         + [mid, row(ln2_gain), row(ln2_shift), row(b_down), w_up, row(b_up), w_down, pieces_b],
-        [quad_rows, low_rows, half_b, half_b, wide, act, struct((4, D), F32)],
+        [quad_rows, struct((256, D), BF16), half_b, half_b, wide, act, struct((4, D), F32)],
         [weights, weights, square, square, pltpu.VMEM((4, D), F32), rows_low, rows_low, turned, turned]
         + [rows_low, rows_low, pltpu.VMEM((ROWS, D), F32), pltpu.VMEM((2, D, D), BF16)]
         + [pltpu.VMEM((8, 3, 144, D), BF16), pltpu.VMEM((4, 4, 128, D), BF16), pltpu.VMEM((4, 4, 128, D), BF16)]
@@ -638,17 +645,16 @@
         far_outs=(2, 3, 5),
     )
     far_send = to_peer(send_b, 1)
-    piece_b = struct((4, 128, D), BF16)
-    quarters = pltpu.VMEM((4, 4, 128, D), BF16)
-    gmid, gcontext, gw_out, small, *both_b = call(
+    gmid, gcontext, gw_out, small = call(
         norm_backward,
         "norm_backward",
-        [lengths, mid, gnorm, grad, row(ln2_gain), ctx, w_full, keep_b, far_send],
-        [wide, act, struct((D, D), BF16), struct((8, D), F32)] + [piece_b] * 4,
-        [rows_low, square, rows_low, quarters, quarters, sems((4,))],
+        [lengths, mid, gnorm, grad, row(ln2_gain), ctx, w_full],
+        [wide, act, struct((D, D), BF16), struct((8, D), F32)],
+        [rows_low, square, rows_low, sems((2,))],
         25000000,
-        far_ins=(5, 6, 7, 8),
-    )
+        far_ins=(5, 6),
+    )
+    both_b = call(pair_sum, "pair_sum", [keep_b, after(far_send, small)], [struct((4, 128, D), BF16)] * 4)
 
     def across(value, bits):
         return lax.ppermute(value, "tensor", [(i, i ^ bits) for i in range(4)])
@@ -661,9 +667,8 @@
         return plane
 
     left = [(1, 0), (2, 1), (3, 2)]
-    y_lows = [hop(y_low, [(w, 3)]) for w in range(3)]
-    gcontext = after(gcontext, y_lows[0], y_lows[1])
-    y_recv = hop(after(y_quad, gcontext, y_lows[0], y_lows[1]), left)
+    y_lows = [lax.all_gather(y_low, "tensor", axis=0)]
+    y_recv = hop(after(y_quad, gcontext), left)
     half_a = struct((4, 4, 288, 128), BF16)
     g_quad, g_low, keep_a, send_a = call(
         attention_backward,
@@ -679,18 +684,18 @@
     parts_b = after([both_b[0]] + [to_peer(both_b[k], 2 * k) for k in (1, 2, 3)], keep_a)
     far_a = to_peer(after(send_a, y_recv, *y_lows, *parts_b), 1)
     plane_b = wider([lower([v[s] for v in parts_b]) for s in range(4)])
-    far_b = [across(plane_b[s], s) for s in (1, 2, 3)]
+    mine_b = lax.psum_scatter(jnp.concatenate(plane_b), "tensor", scatter_dimension=0, tiled=True)
     both_a = lower([keep_a, far_a])
     parts_a = lax.all_to_all(both_a, "dp", 0, 0, axis_index_groups=planes, tiled=True)
     g_lows = [hop(after(g_low, both_a), [(w, 3)]) for w in range(3)]
     g_recv = hop(after(g_quad, both_a), left)
-    parts_a = after(parts_a, g_recv, *g_lows)
-    mine_b = lower([plane_b[0]] + after(far_b, parts_a))
-    plane_a = wider([lower([parts_a[i, s] for i in range(4)]) for s in range(4)])
-    flat_b = lax.all_gather(mine_b, "dp", axis=0, axis_index_groups=eights)
     output = call(
         spread_rows, "spread_rows", [after(y_quad, both_a), y_low, y_recv] + y_lows, [struct((SHARD, D), BF16)]
     )[0]
+    parts_a = after(parts_a, g_recv, output, *g_lows)
+    plane_a = wider([lower([parts_a[i, s] for i in range(4)]) for s in range(4)])
+    mine_b = after(mine_b, parts_a)
+    flat_b = lax.all_gather(mine_b, "dp", axis=0, axis_index_groups=eights)
     mine_a = lower([plane_a[0]] + [across(plane_a[s], s) for s in (1, 2, 3)])
     grad_tokens = call(
         spread_rows, "spread_rows", [after(g_quad, parts_a), g_low, g_recv] + g_lows, [struct((SHARD, D), F32)]

time: 245 us -> 234 us (0.955)
  starting transfers between devices: 66.8 us -> 45.6 us
  waiting for transfers between devices: 32.5 us -> 47.4 us
  other arithmetic: 11.2 us -> 8.37 us
    ppermute x16 -> x13, waiting for transfers between devices: 0.57 us -> 18.9 us  [hop(): return lax.ppermute(value, 'tensor', pairs)]
    ppermute x6 -> x3, starting transfers between devices: 18.4 us -> 4.71 us  [across(): return lax.ppermute(value, 'tensor', [(i, i ^ bits) for i in range(4)])]
    ppermute x16 -> x13, starting transfers between devices: 35 us -> 27.3 us  [hop(): return lax.ppermute(value, 'tensor', pairs)]
    ppermute x6 -> x3, waiting for transfers between devices: 5.68 us -> 1.17 us  [across(): return lax.ppermute(value, 'tensor', [(i, i ^ bits) for i in range(4)])]
    convert_element_type x3 -> x2, other arithmetic: 4.63 us -> 1.6 us  [lower(): return sum((v.astype(F32) for v in terms)).astype(BF16)]
    all_gather x1, waiting for transfers between devices: 0.01 us -> 2.55 us  [shards(): flat_b = lax.all_gather(mine_b, 'dp', axis=0, axis_index_groups=eights)]
    pallas_call x7 -> x8, Pallas kernels: 79.6 us -> 81 us  [call(): pl.pallas_call(body, out_shape=tuple(outs), in_specs=specs, out_specs=tup...]
  transfers between devices with their start and end apart: 34 -> 30, of which waited for: 7 -> 9; matrix products, arithmetic and copies ran while one was open for 3% -> 4% of each run, Pallas kernels for 21% -> 23%
where the time goes in v1:
time: 234 us; the launch traced here: 230 us
  Pallas kernels  81 us (35%)
  waiting for transfers between devices  47.4 us (20%)
  starting transfers between devices  45.6 us (19%)
  blocking collectives  24.5 us (10%)
  between operations  14.6 us (6%)
  local copies, waits for them, and re-layouts  8.96 us (4%)
  other arithmetic  8.37 us (4%)
    pallas_call x8, Pallas kernels, call(): pl.pallas_call(body, out_shape=tuple(outs), in_specs=specs, out_specs=tup...  81 us
    ppermute x13, starting transfers between devices, hop(): return lax.ppermute(value, 'tensor', pairs)  27.3 us
    ppermute x13, waiting for transfers between devices, hop(): return lax.ppermute(value, 'tensor', pairs)  18.9 us
    ppermute x3, waiting for transfers between devices, along(): lax.ppermute(value, 'tensor', [(i, (i + step) % 4) for i in range(4)])  17.1 us
    all_gather x1, blocking collectives, shards(): plane_a = lax.all_gather(first_a, 'dp', axis=0, axis_index_groups=planes)  13.5 us
    all_gather x1, blocking collectives, shards(): flat_a = lax.all_gather(mine_a, 'dp', axis=0, axis_index_groups=eights)  11 us
    ppermute x6, waiting for transfers between devices, to_peer(): return lax.ppermute(value, 'dp', [(i, i ^ e) for i in range(n_dp)])  7.64 us
    ppermute x3, starting transfers between devices, along(): lax.ppermute(value, 'tensor', [(i, (i + step) % 4) for i in range(4)])  6.11 us
  transfers between devices with their start and end apart: 30, of which 9 were waited for; matrix products, arithmetic and copies ran while one was open for 4% of the time, Pallas kernels for 23%

profile of v1, /device:TPU:0, one launch (start us, length us, event | category | flops | bytes accessed | tf_op | source)
XLA Modules:
  0.0 230.4 jit_solution(10041927689020101807)
XLA Ops:
  7.3 0.8 reshape.141.b_up
  8.0 0.8 constant_dynamic-slice_fusion
  9.6 0.9 constant_dynamic-slice_fusion.1
  10.6 5.1 %collective-permute-start.2 = (bf16[208,512]{1,0:T(8,128)(2,1)S(1)}, bf16[208,512]{1,0:T(8,128)(2,1)S(1)}, u32[]{:S(2)}, u32[]{:S(2)}) collective-permute-start(bf16[208,512]{1,0:T(8,128)(2,1)S(1)} %concatenate.34), channel_id=1, source_target_pairs={{0,3},{1,0},{2,1},{3,2},{4,7},{5,4},{6,5},{7,6},{8,11},{9,8},{10,9... | collective-permute-start | bytes 638984 | tf_op jit(solution)/shard_map/ppermute | solution.py:548
  15.7 1.0 collective-permute-start
  16.7 4.7 %collective-permute-done.2 = bf16[208,512]{1,0:T(8,128)(2,1)S(1)} collective-permute-done((bf16[208,512]{1,0:T(8,128)(2,1)S(1)}, bf16[208,512]{1,0:T(8,128)(2,1)S(1)}, u32[]{:S(2)}, u32[]{:S(2)}) %collective-permute-start.2) | collective-permute-done | bytes 213024 | tf_op jit(solution)/shard_map/ppermute | solution.py:548
  21.4 12.4 %collective-permute-done.1 = bf16[208,512]{1,0:T(8,128)(2,1)S(1)} collective-permute-done((bf16[208,512]{1,0:T(8,128)(2,1)S(1)}, bf16[208,512]{1,0:T(8,128)(2,1)S(1)}, u32[]{:S(2)}, u32[]{:S(2)}) %collective-permute-start.1) | collective-permute-done | bytes 213024 | tf_op jit(solution)/shard_map/ppermute | solution.py:548
  33.9 0.8 pad_maximum_fusion.1
  34.8 0.9 slice.194
  35.8 0.7 pad_maximum_fusion.7
  36.5 0.8 pad_maximum_fusion.5
  37.6 2.8 %collective-permute-start.3 = (bf16[720,512]{1,0:T(8,128)(2,1)}, bf16[720,512]{1,0:T(8,128)(2,1)S(1)}, u32[]{:S(2)}, u32[]{:S(2)}) collective-permute-start(bf16[720,512]{1,0:T(8,128)(2,1)} %slice.194), channel_id=1, source_target_pairs={{0,1},{1,2},{2,3},{4,5},{5,6},{6,7},{8,9},{9,10},{10,11},{12,13},{... | collective-permute-start | bytes 2211848 | tf_op jit(solution)/shard_map/ppermute | solution.py:551
  40.5 0.8 pad_maximum_fusion.2
  41.3 1.3 collective-permute-start.4
  44.0 13.5 %all-gather = bf16[12,4,64,128]{3,2,1,0:T(8,128)(2,1)S(1)} all-gather(bf16[3,4,64,128]{3,2,1,0:T(8,128)(2,1)S(1)} %copy.33), channel_id=2, replica_groups={{0,8,16,24},{4,12,20,28},{1,9,17,25},{5,13,21,29},{2,10,18,26},{6,14,22..., dimensions={0}, use_global_device_ids=true | all-gather | bytes 983040 | tf_op jit(solution)/shard_map/all_gather | solution.py:587
  57.5 0.8 pad_maximum_fusion.4
  58.4 4.2 %collective-permute-start.7 = (bf16[720,512]{1,0:T(8,128)(2,1)S(1)}, bf16[720,512]{1,0:T(8,128)(2,1)S(1)}, u32[]{:S(2)}, u32[]{:S(2)}) collective-permute-start(bf16[720,512]{1,0:T(8,128)(2,1)S(1)} %slice.187), channel_id=1, source_target_pairs={{0,1},{1,2},{2,3},{4,5},{5,6},{6,7},{8,9},{9,10},{10,11},{12,13},{... | collective-permute-start | bytes 2211848 | tf_op jit(solution)/shard_map/ppermute | solution.py:551
  62.7 1.3 collective-permute-start.8
  64.0 1.4 collective-permute-start.9
  65.3 1.5 collective-permute-start.10
  66.9 0.8 copy-done.5
  67.7 15.2 %attention_forward.1 = (bf16[1024,512]{1,0:T(8,128)(2,1)}, bf16[1024,512]{1,0:T(8,128)(2,1)}, bf16[3,1024,512]{2,1,0:T(8,128)(2,1)}, f32[1024,128]{1,0:T(8,128)}...) custom-call(s32[4]{0:T(128)} %lengths.3, bf16[960,512]{1,0:T(8,128)(2,1)} %own.2, ...), custom_call_target="tpu_custom_call" | custom-call | flops 1000 | bytes 1000 | tf_op jit(solution)/shard_map/attention_forward/pallas_call | solution.py:506
  83.9 25.0 %feed_forward.1 = (bf16[768,512]{1,0:T(8,128)(2,1)}, bf16[256,512]{1,0:T(8,128)(2,1)}, bf16[4,4,128,512]{3,2,1,0:T(8,128)(2,1)}, bf16[4,4,128,512]{3,2,1,0:T(8,1...) custom-call(bf16[960,512]{1,0:T(8,128)(2,1)} %own.3, bf16[720,512]{1,0:T(8,128)(2,1)} %copy-done.10, ...), custom_call_target="tpu_custom_call" | custom-call | flops 1000 | bytes 1000 | tf_op jit(solution)/shard_map/feed_forward/pallas_call | solution.py:506
  109.2 7.6 %norm_backward.1 = (f32[1024,512]{1,0:T(8,128)}, bf16[1024,512]{1,0:T(8,128)(2,1)}, bf16[512,512]{1,0:T(8,128)(2,1)}, f32[8,512]{1,0:T(8,128)}) custom-call(s32[4]{0:T(128)} %lengths.3, f32[1024,512]{1,0:T(8,128)} %get-tuple-element.73.mid, f32[1024,512]{1,0:T(8,128)} %get-tuple-element.77.gnorm, bf16[1024,512]{1,0:T(8,128)(2,1)} %get-tuple-element.78.grad, ...), custom_call_target="tpu_custom_call" | custom-call | flops 1000 | bytes 25000000 | tf_op jit(solution)/shard_map/norm_backward/pallas_call | solution.py:506
  116.8 1.3 collective-permute-start.12
  118.1 1.3 copy-done.3
  119.4 3.8 %pair_sum.1 = (bf16[4,128,512]{2,1,0:T(8,128)(2,1)}, bf16[4,128,512]{2,1,0:T(8,128)(2,1)}, bf16[4,128,512]{2,1,0:T(8,128)(2,1)}, bf16[4,128,512]{2,1,0:T(8,128)(2,1)}) custom-call(bf16[4,4,128,512]{3,2,1,0:T(8,128)(2,1)} %get-tuple-element.92.keep, bf16[4,4,128,512]{3,2,1,0:T(8,128)(2,1)} %copy-done.3), custom_call_target="tpu_custom_call" | custom-call | flops 1000 | bytes 1000 | tf_op jit(solution)/shard_map/pair_sum/pallas_call | solution.py:506
  123.2 1.3 collective-permute-start.14
  124.5 1.6 collective-permute-start.15
  126.7 16.3 %attention_backward.1 = (bf16[768,512]{1,0:T(8,128)(2,1)}, bf16[240,512]{1,0:T(8,128)(2,1)}, bf16[4,4,288,128]{3,2,1,0:T(8,128)(2,1)}, bf16[4,4,288,128]{3,2,1,0:T(8,128)(2,1)}) custom-call(bf16[3,1024,512]{2,1,0:T(8,128)(2,1)} %get-tuple-element.75.qkv, f32[1024,128]{1,0:T(8,128)} %get-tuple-element.76.prob, bf16[1024,512]{1,0:T(8,128)(2,1)} %get-tuple-element.81.gcontext, ...), custom_call_target="tpu_custom_call" | custom-call | flops 1000 | bytes 60000000 | tf_op jit(solution)/shard_map/attention_backward/pallas_call | solution.py:506
  143.1 7.1 %collective-permute-done.15 = bf16[4,128,512]{2,1,0:T(8,128)(2,1)} collective-permute-done((bf16[4,128,512]{2,1,0:T(8,128)(2,1)}, bf16[4,128,512]{2,1,0:T(8,128)(2,1)}, u32[]{:S(2)}, u32[]{:S(2)}) %collective-permute-start.15) | collective-permute-done | bytes 524320 | tf_op jit(solution)/shard_map/ppermute | solution.py:545
  150.2 6.9 %collective-permute-done.12.recv = bf16[768,512]{1,0:T(8,128)(2,1)} collective-permute-done((bf16[768,512]{1,0:T(8,128)(2,1)S(1)}, bf16[768,512]{1,0:T(8,128)(2,1)}, u32[]{:S(2)}, u32[]{:S(2)}) %collective-permute-start.12) | collective-permute-done | bytes 786464 | tf_op jit(solution)/shard_map/ppermute | solution.py:551
  157.0 1.6 fusion.3
  158.7 0.8 pad_maximum_fusion
  160.1 1.5 add_convert_fusion
  161.6 3.7 %all-to-all-start = ((bf16[4,4,288,128]{3,2,1,0:T(8,128)(2,1)}), bf16[4,4,288,128]{3,2,1,0:T(8,128)(2,1)S(1)}, u32[]{:S(2)}, u32[]{:S(2)}) async-start(bf16[4,4,288,128]{3,2,1,0:T(8,128)(2,1)} %add_convert_fusion), calls=%async_computation | async-start | bytes 2359296 | tf_op jit(solution)/shard_map/all_to_all | solution.py:689
  165.3 1.3 collective-permute-start.18
  168.0 9.5 %collective-permute-start.19 = (bf16[240,512]{1,0:T(8,128)(2,1)S(1)}, bf16[240,512]{1,0:T(8,128)(2,1)S(1)}, u32[]{:S(2)}, u32[]{:S(2)}) collective-permute-start(bf16[240,512]{1,0:T(8,128)(2,1)S(1)} %copy-done.16), channel_id=1, source_target_pairs={{0,3},{4,7},{8,11},{12,15},{16,19},{20,23},{24,27},{28,31}} | collective-permute-start | bytes 737288 | tf_op jit(solution)/shard_map/ppermute | solution.py:551
  177.5 4.8 %spread_rows.2 = bf16[960,512]{1,0:T(8,128)(2,1)} custom-call(bf16[768,512]{1,0:T(8,128)(2,1)} %get-tuple-element.104.quad, bf16[256,512]{1,0:T(8,128)(2,1)} %get-tuple-element.91.low, bf16[768,512]{1,0:T(8,128)(2,1)} %collective-permute-done.12.recv, bf16[4,256,512]{2,1,0:T(8,128)(2,1)} %bitcast.72), custom_call_target="tpu_custom_call" | custom-call | flops 1000 | bytes 1000 | tf_op jit(solution)/shard_map/spread_rows/pallas_call | solution.py:506
  182.3 2.4 %collective-permute-done.19.rest_0_ = bf16[240,512]{1,0:T(8,128)(2,1)S(1)} collective-permute-done((bf16[240,512]{1,0:T(8,128)(2,1)S(1)}, bf16[240,512]{1,0:T(8,128)(2,1)S(1)}, u32[]{:S(2)}, u32[]{:S(2)}) %collective-permute-start.19) | collective-permute-done | bytes 245792 | tf_op jit(solution)/shard_map/ppermute | solution.py:551
  185.4 9.6 %collective-permute-done.18.recv = bf16[768,512]{1,0:T(8,128)(2,1)S(1)} collective-permute-done((bf16[768,512]{1,0:T(8,128)(2,1)S(1)}, bf16[768,512]{1,0:T(8,128)(2,1)S(1)}, u32[]{:S(2)}, u32[]{:S(2)}) %collective-permute-start.18) | collective-permute-done | bytes 786464 | tf_op jit(solution)/shard_map/ppermute | solution.py:551
  195.2 1.5 collective-permute-start.22
  196.7 3.2 %collective-permute-start.23 = (bf16[288,128]{1,0:T(8,128)(2,1)S(1)}, bf16[288,128]{1,0:T(8,128)(2,1)S(1)}, u32[]{:S(2)}, u32[]{:S(2)}) collective-permute-start(bf16[288,128]{1,0:T(8,128)(2,1)S(1)} %get-tuple-element.122), channel_id=1, source_target_pairs={{0,2},{1,3},{2,0},{3,1},{4,6},{5,7},{6,4},{7,5},{8,10},{9,11},{10,... | collective-permute-start | bytes 221192 | tf_op jit(solution)/shard_map/ppermute | solution.py:660
  199.9 5.1 %spread_rows.3 = f32[960,512]{1,0:T(8,128)} custom-call(bf16[768,512]{1,0:T(8,128)(2,1)} %get-tuple-element.110.quad, bf16[240,512]{1,0:T(8,128)(2,1)} %get-tuple-element.108.low, bf16[768,512]{1,0:T(8,128)(2,1)} %copy-done.8, bf16[240,512]{1,0:T(8,128)(2,1)} %copy-done.19, bf16[240,512]{1,0:T(8,128)(2,1)} %copy-done.18, bf16[240,512]{1,0:T(8,128)(2,1)} %copy-done.17), custom_call_target="tpu_custom_call" | custom-call | flops 1000 | bytes 1000 | tf_op jit(solution)/shard_map/spread_rows/pallas_call | solution.py:506
  205.0 1.2 collective-permute-done.24
  206.2 11.0 %all-gather.3 = bf16[2304,128]{1,0:T(8,128)(2,1)} all-gather(bf16[288,128]{1,0:T(8,128)(2,1)S(1)} %fusion.2), channel_id=5, replica_groups={{0,4,8,12,16,20,24,28},{1,5,9,13,17,21,25,29},{2,6,10,14,18,22,26,30},{..., dimensions={0}, use_global_device_ids=true | all-gather | bytes 663552 | tf_op jit(solution)/shard_map/all_gather | solution.py:704
  217.8 2.5 %all-gather.13.cloned.1.call-done = bf16[1024,512]{1,0:T(8,128)(2,1)} async-done(((bf16[128,512]{1,0:T(8,128)(2,1)}), bf16[1024,512]{1,0:T(8,128)(2,1)}) %all-gather.13.cloned.1.call-update) | async-done | bytes 1048592 | tf_op jit(solution)/shard_map/all_gather | solution.py:698
  220.4 3.3 %unpack_weights.1 = (f32[3,512,128]{2,1,0:T(8,128)}, f32[128,512]{1,0:T(8,128)}, f32[512,512]{1,0:T(8,128)}, f32[512,512]{1,0:T(8,128)}) custom-call(bf16[8,288,128]{2,1,0:T(8,128)(2,1)} %bitcast.70, bf16[8,128,512]{2,1,0:T(8,128)(2,1)} %bitcast.71), custom_call_target="tpu_custom_call" | custom-call | flops 1000 | bytes 1000 | tf_op jit(solution)/shard_map/unpack_weights/pallas_call | solution.py:506
  (104 shorter events, 8.1 us)
Async XLA Ops:
  7.2 27.6 %copy-start = (bf16[960,512]{1,0:T(8,128)(2,1)S(1)}, bf16[960,512]{1,0:T(8,128)(2,1)}, u32[]{:S(2)}) copy-start(bf16[960,512]{1,0:T(8,128)(2,1)} %own.2) | copy-start | bytes 2949124
  7.2 75.9 %all-gather.9.cloned.1.call-start = ((), (), s32[]{:S(2)}) async-start(), calls=%async_computation.3 | async-start | bytes 3981312 | tf_op jit(solution)/shard_map/all_gather | solution.py:589
  8.0 27.7 %copy-start.20 = (bf16[1,512]{1,0:T(2,128)(2,1)}, bf16[1,512]{1,0:T(2,128)(2,1)S(1)}, u32[]{:S(2)}) copy-start(bf16[1,512]{1,0:T(2,128)(2,1)S(1)} %reshape.141.b_up) | copy-start | bytes 3076
  10.6 10.8 %collective-permute-start.2 = (bf16[208,512]{1,0:T(8,128)(2,1)S(1)}, bf16[208,512]{1,0:T(8,128)(2,1)S(1)}, u32[]{:S(2)}, u32[]{:S(2)}) collective-permute-start(bf16[208,512]{1,0:T(8,128)(2,1)S(1)} %concatenate.34), channel_id=1, source_target_pairs={{0,3},{1,0},{2,1},{3,2},{4,7},{5,4},{6,5},{7,6},{8,11},{9,8},{10,9... | collective-permute-start | bytes 638984 | tf_op jit(solution)/shard_map/ppermute | solution.py:548
  15.7 18.1 %collective-permute-start.1 = (bf16[208,512]{1,0:T(8,128)(2,1)S(1)}, bf16[208,512]{1,0:T(8,128)(2,1)S(1)}, u32[]{:S(2)}, u32[]{:S(2)}) collective-permute-start(bf16[208,512]{1,0:T(8,128)(2,1)S(1)} %concatenate.34), channel_id=1, source_target_pairs={{0,2},{1,3},{2,0},{3,1},{4,6},{5,7},{6,4},{7,5},{8,10},{9,11},{10,... | collective-permute-start | bytes 638984 | tf_op jit(solution)/shard_map/ppermute | solution.py:548
  15.7 18.1 %collective-permute-start = (bf16[208,512]{1,0:T(8,128)(2,1)S(1)}, bf16[208,512]{1,0:T(8,128)(2,1)S(1)}, u32[]{:S(2)}, u32[]{:S(2)}) collective-permute-start(bf16[208,512]{1,0:T(8,128)(2,1)S(1)} %concatenate.34), channel_id=1, source_target_pairs={{0,1},{1,2},{2,3},{3,0},{4,5},{5,6},{6,7},{7,4},{8,9},{9,10},{10,1... | collective-permute-start | bytes 638984 | tf_op jit(solution)/shard_map/ppermute | solution.py:548
  34.7 122.3 %all-gather.11.cloned.1.call-start = ((), (), s32[]{:S(2)}) async-start(), calls=%async_computation.4 | async-start | bytes 1310720 | tf_op jit(solution)/shard_map/all_gather | solution.py:670
  35.7 4.7 %copy-start.1 = (bf16[960,512]{1,0:T(8,128)(2,1)S(1)}, bf16[960,512]{1,0:T(8,128)(2,1)}, u32[]{:S(2)}) copy-start(bf16[960,512]{1,0:T(8,128)(2,1)} %own.3) | copy-start | bytes 2949124
  37.6 20.8 %collective-permute-start.3 = (bf16[720,512]{1,0:T(8,128)(2,1)}, bf16[720,512]{1,0:T(8,128)(2,1)S(1)}, u32[]{:S(2)}, u32[]{:S(2)}) collective-permute-start(bf16[720,512]{1,0:T(8,128)(2,1)} %slice.194), channel_id=1, source_target_pairs={{0,1},{1,2},{2,3},{4,5},{5,6},{6,7},{8,9},{9,10},{10,11},{12,13},{... | collective-permute-start | bytes 2211848 | tf_op jit(solution)/shard_map/ppermute | solution.py:551
  41.3 17.0 %collective-permute-start.4 = (bf16[256,512]{1,0:T(8,128)(2,1)}, bf16[256,512]{1,0:T(8,128)(2,1)S(1)}, u32[]{:S(2)}, u32[]{:S(2)}) collective-permute-start(bf16[256,512]{1,0:T(8,128)(2,1)} %get-tuple-element.66), channel_id=1, source_target_pairs={{3,0},{7,4},{11,8},{15,12},{19,16},{23,20},{27,24},{31,28}} | collective-permute-start | bytes 786440 | tf_op jit(solution)/shard_map/ppermute | solution.py:551
  42.6 15.7 %collective-permute-start.5 = (bf16[256,512]{1,0:T(8,128)(2,1)}, bf16[256,512]{1,0:T(8,128)(2,1)S(1)}, u32[]{:S(2)}, u32[]{:S(2)}) collective-permute-start(bf16[256,512]{1,0:T(8,128)(2,1)} %get-tuple-element.67), channel_id=1, source_target_pairs={{3,1},{7,5},{11,9},{15,13},{19,17},{23,21},{27,25},{31,29}} | collective-permute-start | bytes 786440 | tf_op jit(solution)/shard_map/ppermute | solution.py:551
  43.3 15.0 %collective-permute-start.6 = (bf16[256,512]{1,0:T(8,128)(2,1)}, bf16[256,512]{1,0:T(8,128)(2,1)S(1)}, u32[]{:S(2)}, u32[]{:S(2)}) collective-permute-start(bf16[256,512]{1,0:T(8,128)(2,1)} %pad_maximum_fusion.7), channel_id=1, source_target_pairs={{3,2},{7,6},{11,10},{15,14},{19,18},{23,22},{27,26},{31,30}} | collective-permute-start | bytes 786440 | tf_op jit(solution)/shard_map/ppermute | solution.py:551
  57.5 9.4 %copy-start.2 = (bf16[12,4,64,128]{3,2,1,0:T(8,128)(2,1)}, bf16[12,4,64,128]{3,2,1,0:T(8,128)(2,1)S(1)}, u32[]{:S(2)}) copy-start(bf16[12,4,64,128]{3,2,1,0:T(8,128)(2,1)S(1)} %all-gather) | copy-start | bytes 2359300
  57.5 9.4 %collective-permute-start.11 = (bf16[4,3,4,64,128]{4,3,2,1,0:T(8,128)(2,1)S(1)}, bf16[4,3,4,64,128]{4,3,2,1,0:T(8,128)(2,1)S(1)}, u32[]{:S(2)}, u32[]{:S(2)}) collective-permute-start(bf16[4,3,4,64,128]{4,3,2,1,0:T(8,128)(2,1)S(1)} %bitcast.68), channel_id=1, source_target_pairs={{0,4},{4,0},{8,12},{12,8},{16,20},{20,16},{24,28},{28,24},{1,5},{5... | collective-permute-start | bytes 2359304 | tf_op jit(solution)/shard_map/ppermute | solution.py:545
  58.3 8.5 %copy-start.12 = (bf16[256,512]{1,0:T(8,128)(2,1)}, bf16[256,512]{1,0:T(8,128)(2,1)S(1)}, u32[]{:S(2)}) copy-start(bf16[256,512]{1,0:T(8,128)(2,1)S(1)} %collective-permute-done.4.low0) | copy-start | bytes 786436
  58.4 8.5 %copy-start.13 = (bf16[256,512]{1,0:T(8,128)(2,1)}, bf16[256,512]{1,0:T(8,128)(2,1)S(1)}, u32[]{:S(2)}) copy-start(bf16[256,512]{1,0:T(8,128)(2,1)S(1)} %collective-permute-done.5.low1) | copy-start | bytes 786436
  58.4 8.5 %copy-start.14 = (bf16[256,512]{1,0:T(8,128)(2,1)}, bf16[256,512]{1,0:T(8,128)(2,1)S(1)}, u32[]{:S(2)}) copy-start(bf16[256,512]{1,0:T(8,128)(2,1)S(1)} %collective-permute-done.6.low2) | copy-start | bytes 786436
  58.4 8.5 %copy-start.9 = (bf16[720,512]{1,0:T(8,128)(2,1)}, bf16[720,512]{1,0:T(8,128)(2,1)S(1)}, u32[]{:S(2)}) copy-start(bf16[720,512]{1,0:T(8,128)(2,1)S(1)} %collective-permute-done.3.recv) | copy-start | bytes 2211844
  58.4 24.6 %collective-permute-start.7 = (bf16[720,512]{1,0:T(8,128)(2,1)S(1)}, bf16[720,512]{1,0:T(8,128)(2,1)S(1)}, u32[]{:S(2)}, u32[]{:S(2)}) collective-permute-start(bf16[720,512]{1,0:T(8,128)(2,1)S(1)} %slice.187), channel_id=1, source_target_pairs={{0,1},{1,2},{2,3},{4,5},{5,6},{6,7},{8,9},{9,10},{10,11},{12,13},{... | collective-permute-start | bytes 2211848 | tf_op jit(solution)/shard_map/ppermute | solution.py:551
  62.7 20.3 %collective-permute-start.8 = (bf16[256,512]{1,0:T(8,128)(2,1)}, bf16[256,512]{1,0:T(8,128)(2,1)S(1)}, u32[]{:S(2)}, u32[]{:S(2)}) collective-permute-start(bf16[256,512]{1,0:T(8,128)(2,1)} %get-tuple-element.70), channel_id=1, source_target_pairs={{3,0},{7,4},{11,8},{15,12},{19,16},{23,20},{27,24},{31,28}} | collective-permute-start | bytes 786440 | tf_op jit(solution)/shard_map/ppermute | solution.py:551
  64.0 19.0 %collective-permute-start.9 = (bf16[256,512]{1,0:T(8,128)(2,1)}, bf16[256,512]{1,0:T(8,128)(2,1)}, u32[]{:S(2)}, u32[]{:S(2)}) collective-permute-start(bf16[256,512]{1,0:T(8,128)(2,1)} %get-tuple-element.71), channel_id=1, source_target_pairs={{3,1},{7,5},{11,9},{15,13},{19,17},{23,21},{27,25},{31,29}} | collective-permute-start | bytes 786440 | tf_op jit(solution)/shard_map/ppermute | solution.py:551
  65.3 17.7 %collective-permute-start.10 = (bf16[256,512]{1,0:T(8,128)(2,1)}, bf16[256,512]{1,0:T(8,128)(2,1)}, u32[]{:S(2)}, u32[]{:S(2)}) collective-permute-start(bf16[256,512]{1,0:T(8,128)(2,1)} %pad_maximum_fusion.4), channel_id=1, source_target_pairs={{3,2},{7,6},{11,10},{15,14},{19,18},{23,22},{27,26},{31,30}} | collective-permute-start | bytes 786440 | tf_op jit(solution)/shard_map/ppermute | solution.py:551
  83.0 0.9 copy-start.10
  108.9 9.2 %collective-permute-start.13 = (bf16[4,4,128,512]{3,2,1,0:T(8,128)(2,1)}, bf16[4,4,128,512]{3,2,1,0:T(8,128)(2,1)S(1)}, u32[]{:S(2)}, u32[]{:S(2)}) collective-permute-start(bf16[4,4,128,512]{3,2,1,0:T(8,128)(2,1)} %get-tuple-element.93), channel_id=1, source_target_pairs={{0,4},{4,0},{8,12},{12,8},{16,20},{20,16},{24,28},{28,24},{1,5},{5... | collective-permute-start | bytes 6291464 | tf_op jit(solution)/shard_map/ppermute | solution.py:545
  109.1 85.9 %reduce-scatter.2.cloned.1.call-start = ((), (), s32[]{:S(2)}) async-start(), calls=%async_computation.2 | async-start | bytes 655360 | tf_op jit(solution)/shard_map/reduce_scatter | solution.py:687
  109.2 7.6 %copy-start.6 = (bf16[768,512]{1,0:T(8,128)(2,1)S(1)}, bf16[768,512]{1,0:T(8,128)(2,1)}, u32[]{:S(2)}) copy-start(bf16[768,512]{1,0:T(8,128)(2,1)} %get-tuple-element.104.quad) | copy-start | bytes 2359300
  116.8 40.3 %collective-permute-start.12 = (bf16[768,512]{1,0:T(8,128)(2,1)S(1)}, bf16[768,512]{1,0:T(8,128)(2,1)}, u32[]{:S(2)}, u32[]{:S(2)}) collective-permute-start(bf16[768,512]{1,0:T(8,128)(2,1)S(1)} %copy-done.6), channel_id=1, source_target_pairs={{1,0},{2,1},{3,2},{5,4},{6,5},{7,6},{9,8},{10,9},{11,10},{13,12},{... | collective-permute-start | bytes 2359304 | tf_op jit(solution)/shard_map/ppermute | solution.py:551
  118.1 1.3 copy-start.3
  123.2 19.9 %collective-permute-start.14 = (bf16[4,128,512]{2,1,0:T(8,128)(2,1)}, bf16[4,128,512]{2,1,0:T(8,128)(2,1)S(1)}, u32[]{:S(2)}, u32[]{:S(2)}) collective-permute-start(bf16[4,128,512]{2,1,0:T(8,128)(2,1)} %get-tuple-element.96), channel_id=1, source_target_pairs={{0,8},{4,12},{8,0},{12,4},{16,24},{20,28},{24,16},{28,20},{1,9},{5... | collective-permute-start | bytes 1572872 | tf_op jit(solution)/shard_map/ppermute | solution.py:545
  124.5 25.6 %collective-permute-start.15 = (bf16[4,128,512]{2,1,0:T(8,128)(2,1)}, bf16[4,128,512]{2,1,0:T(8,128)(2,1)}, u32[]{:S(2)}, u32[]{:S(2)}) collective-permute-start(bf16[4,128,512]{2,1,0:T(8,128)(2,1)} %get-tuple-element.97), channel_id=1, source_target_pairs={{0,16},{4,20},{8,24},{12,28},{16,0},{20,4},{24,8},{28,12},{1,17},{... | collective-permute-start | bytes 1572872 | tf_op jit(solution)/shard_map/ppermute | solution.py:545
  126.1 24.1 %collective-permute-start.16 = (bf16[4,128,512]{2,1,0:T(8,128)(2,1)}, bf16[4,128,512]{2,1,0:T(8,128)(2,1)}, u32[]{:S(2)}, u32[]{:S(2)}) collective-permute-start(bf16[4,128,512]{2,1,0:T(8,128)(2,1)} %get-tuple-element.98), channel_id=1, source_target_pairs={{0,24},{4,28},{8,16},{12,20},{16,8},{20,12},{24,0},{28,4},{1,25},{... | collective-permute-start | bytes 1572872 | tf_op jit(solution)/shard_map/ppermute | solution.py:545
  126.7 30.3 %copy-start.11 = (bf16[4,128,512]{2,1,0:T(8,128)(2,1)S(1)}, bf16[4,128,512]{2,1,0:T(8,128)(2,1)}, u32[]{:S(2)}) copy-start(bf16[4,128,512]{2,1,0:T(8,128)(2,1)} %get-tuple-element.99) | copy-start | bytes 1572868
  157.0 3.1 %copy-start.4 = (bf16[4,4,288,128]{3,2,1,0:T(8,128)(2,1)S(1)}, bf16[4,4,288,128]{3,2,1,0:T(8,128)(2,1)}, u32[]{:S(2)}) copy-start(bf16[4,4,288,128]{3,2,1,0:T(8,128)(2,1)} %get-tuple-element.88) | copy-start | bytes 3538948
  157.0 3.1 %collective-permute-start.17 = (bf16[4,4,288,128]{3,2,1,0:T(8,128)(2,1)}, bf16[4,4,288,128]{3,2,1,0:T(8,128)(2,1)S(1)}, u32[]{:S(2)}, u32[]{:S(2)}) collective-permute-start(bf16[4,4,288,128]{3,2,1,0:T(8,128)(2,1)} %get-tuple-element.103), channel_id=1, source_target_pairs={{0,4},{4,0},{8,12},{12,8},{16,20},{20,16},{24,28},{28,24},{1,5},{5... | collective-permute-start | bytes 3538952 | tf_op jit(solution)/shard_map/ppermute | solution.py:545
  159.5 5.8 %copy-start.7 = (bf16[768,512]{1,0:T(8,128)(2,1)S(1)}, bf16[768,512]{1,0:T(8,128)(2,1)}, u32[]{:S(2)}) copy-start(bf16[768,512]{1,0:T(8,128)(2,1)} %get-tuple-element.110.quad) | copy-start | bytes 2359300
  159.6 7.1 %copy-start.16 = (bf16[240,512]{1,0:T(8,128)(2,1)S(1)}, bf16[240,512]{1,0:T(8,128)(2,1)}, u32[]{:S(2)}) copy-start(bf16[240,512]{1,0:T(8,128)(2,1)} %get-tuple-element.108.low) | copy-start | bytes 737284
  161.6 33.4 %all-to-all-start = ((bf16[4,4,288,128]{3,2,1,0:T(8,128)(2,1)}), bf16[4,4,288,128]{3,2,1,0:T(8,128)(2,1)S(1)}, u32[]{:S(2)}, u32[]{:S(2)}) async-start(bf16[4,4,288,128]{3,2,1,0:T(8,128)(2,1)} %add_convert_fusion), calls=%async_computation | async-start | bytes 2359296 | tf_op jit(solution)/shard_map/all_to_all | solution.py:689
  165.3 55.0 %all-gather.13.cloned.1.call-start = ((), (), s32[]{:S(2)}) async-start(), calls=%async_computation.5 | async-start | bytes 1179648 | tf_op jit(solution)/shard_map/all_gather | solution.py:698
  165.3 29.7 %collective-permute-start.18 = (bf16[768,512]{1,0:T(8,128)(2,1)S(1)}, bf16[768,512]{1,0:T(8,128)(2,1)S(1)}, u32[]{:S(2)}, u32[]{:S(2)}) collective-permute-start(bf16[768,512]{1,0:T(8,128)(2,1)S(1)} %copy-done.7), channel_id=1, source_target_pairs={{1,0},{2,1},{3,2},{5,4},{6,5},{7,6},{9,8},{10,9},{11,10},{13,12},{... | collective-permute-start | bytes 2359304 | tf_op jit(solution)/shard_map/ppermute | solution.py:551
  166.6 15.6 %collective-permute-start.21 = (bf16[240,512]{1,0:T(8,128)(2,1)S(1)}, bf16[240,512]{1,0:T(8,128)(2,1)S(1)}, u32[]{:S(2)}, u32[]{:S(2)}) collective-permute-start(bf16[240,512]{1,0:T(8,128)(2,1)S(1)} %copy-done.16), channel_id=1, source_target_pairs={{2,3},{6,7},{10,11},{14,15},{18,19},{22,23},{26,27},{30,31}} | collective-permute-start | bytes 737288 | tf_op jit(solution)/shard_map/ppermute | solution.py:551
  167.3 15.0 %collective-permute-start.20 = (bf16[240,512]{1,0:T(8,128)(2,1)S(1)}, bf16[240,512]{1,0:T(8,128)(2,1)S(1)}, u32[]{:S(2)}, u32[]{:S(2)}) collective-permute-start(bf16[240,512]{1,0:T(8,128)(2,1)S(1)} %copy-done.16), channel_id=1, source_target_pairs={{1,3},{5,7},{9,11},{13,15},{17,19},{21,23},{25,27},{29,31}} | collective-permute-start | bytes 737288 | tf_op jit(solution)/shard_map/ppermute | solution.py:551
  168.0 16.7 %collective-permute-start.19 = (bf16[240,512]{1,0:T(8,128)(2,1)S(1)}, bf16[240,512]{1,0:T(8,128)(2,1)S(1)}, u32[]{:S(2)}, u32[]{:S(2)}) collective-permute-start(bf16[240,512]{1,0:T(8,128)(2,1)S(1)} %copy-done.16), channel_id=1, source_target_pairs={{0,3},{4,7},{8,11},{12,15},{16,19},{20,23},{24,27},{28,31}} | collective-permute-start | bytes 737288 | tf_op jit(solution)/shard_map/ppermute | solution.py:551
  182.3 17.6 %copy-start.17 = (bf16[240,512]{1,0:T(8,128)(2,1)}, bf16[240,512]{1,0:T(8,128)(2,1)S(1)}, u32[]{:S(2)}) copy-start(bf16[240,512]{1,0:T(8,128)(2,1)S(1)} %collective-permute-done.21.rest_2_) | copy-start | bytes 737284
  182.3 2.4 %copy-start.18 = (bf16[240,512]{1,0:T(8,128)(2,1)}, bf16[240,512]{1,0:T(8,128)(2,1)S(1)}, u32[]{:S(2)}) copy-start(bf16[240,512]{1,0:T(8,128)(2,1)S(1)} %collective-permute-done.20.rest_1_) | copy-start | bytes 737284
  195.0 4.9 %copy-start.8 = (bf16[768,512]{1,0:T(8,128)(2,1)}, bf16[768,512]{1,0:T(8,128)(2,1)S(1)}, u32[]{:S(2)}) copy-start(bf16[768,512]{1,0:T(8,128)(2,1)S(1)} %collective-permute-done.18.recv) | copy-start | bytes 2359300
  195.2 9.8 %collective-permute-start.22 = (bf16[288,128]{1,0:T(8,128)(2,1)S(1)}, bf16[288,128]{1,0:T(8,128)(2,1)S(1)}, u32[]{:S(2)}, u32[]{:S(2)}) collective-permute-start(bf16[288,128]{1,0:T(8,128)(2,1)S(1)} %get-tuple-element.121), channel_id=1, source_target_pairs={{0,1},{1,0},{2,3},{3,2},{4,5},{5,4},{6,7},{7,6},{8,9},{9,8},{10,11... | collective-permute-start | bytes 221192 | tf_op jit(solution)/shard_map/ppermute | solution.py:660
  196.7 8.3 %collective-permute-start.23 = (bf16[288,128]{1,0:T(8,128)(2,1)S(1)}, bf16[288,128]{1,0:T(8,128)(2,1)S(1)}, u32[]{:S(2)}, u32[]{:S(2)}) collective-permute-start(bf16[288,128]{1,0:T(8,128)(2,1)S(1)} %get-tuple-element.122), channel_id=1, source_target_pairs={{0,2},{1,3},{2,0},{3,1},{4,6},{5,7},{6,4},{7,5},{8,10},{9,11},{10,... | collective-permute-start | bytes 221192 | tf_op jit(solution)/shard_map/ppermute | solution.py:660
  199.9 6.3 %collective-permute-start.24 = (bf16[288,128]{1,0:T(8,128)(2,1)S(1)}, bf16[288,128]{1,0:T(8,128)(2,1)S(1)}, u32[]{:S(2)}, u32[]{:S(2)}) collective-permute-start(bf16[288,128]{1,0:T(8,128)(2,1)S(1)} %get-tuple-element.123), channel_id=1, source_target_pairs={{0,3},{1,2},{2,1},{3,0},{4,7},{5,6},{6,5},{7,4},{8,11},{9,10},{10,... | collective-permute-start | bytes 221192 | tf_op jit(solution)/shard_map/ppermute | solution.py:660
  (3 other events, 2.3 us)
Sparse Core Ops, SparseCore 0:
  34.8 35.5 all-gather.8
  109.3 44.2 all-gather.10
  159.7 27.0 reduce-scatter.1
  195.1 25.1 all-gather.12

commit v2 on v1

--- a/solution.py
+++ b/solution.py
@@ -668,7 +668,7 @@
 
     left = [(1, 0), (2, 1), (3, 2)]
     y_lows = [lax.all_gather(y_low, "tensor", axis=0)]
-    y_recv = hop(after(y_quad, gcontext), left)
+    y_recv = hop(y_quad, left)
     half_a = struct((4, 4, 288, 128), BF16)
     g_quad, g_low, keep_a, send_a = call(
         attention_backward,

time: 234 us -> 230 us (0.983)
  waiting for transfers between devices: 47.4 us -> 42.3 us
    ppermute x13, waiting for transfers between devices: 18.9 us -> 13.1 us  [hop(): return lax.ppermute(value, 'tensor', pairs)]
where the time goes in v2:
time: 230 us; the launch traced here: 227 us
  Pallas kernels  81.4 us (35%)
  starting transfers between devices  46.7 us (20%)
  waiting for transfers between devices  42.3 us (18%)
  blocking collectives  24.4 us (11%)
  between operations  14.6 us (6%)
  local copies, waits for them, and re-layouts  9.06 us (4%)
  other arithmetic  8.15 us (4%)
    pallas_call x8, Pallas kernels, call(): pl.pallas_call(body, out_shape=tuple(outs), in_specs=specs, out_specs=tup...  81.4 us
    ppermute x13, starting transfers between devices, hop(): return lax.ppermute(value, 'tensor', pairs)  28.6 us
    ppermute x3, waiting for transfers between devices, along(): lax.ppermute(value, 'tensor', [(i, (i + step) % 4) for i in range(4)])  17.1 us
    all_gather x1, blocking collectives, shards(): plane_a = lax.all_gather(first_a, 'dp', axis=0, axis_index_groups=planes)  13.5 us
    ppermute x13, waiting for transfers between devices, hop(): return lax.ppermute(value, 'tensor', pairs)  13.1 us
    all_gather x1, blocking collectives, shards(): flat_a = lax.all_gather(mine_a, 'dp', axis=0, axis_index_groups=eights)  10.9 us
    ppermute x6, waiting for transfers between devices, to_peer(): return lax.ppermute(value, 'dp', [(i, i ^ e) for i in range(n_dp)])  7.48 us
    ppermute x3, starting transfers between devices, along(): lax.ppermute(value, 'tensor', [(i, (i + step) % 4) for i in range(4)])  6.11 us
  transfers between devices with their start and end apart: 30, of which 9 were waited for; matrix products, arithmetic and copies ran while one was open for 4% of the time, Pallas kernels for 23%

profile of v2, /device:TPU:0, one launch (start us, length us, event | category | flops | bytes accessed | tf_op | source)
XLA Modules:
  0.0 226.6 jit_solution(18432648439759080574)
XLA Ops:
  7.3 0.8 reshape.141.b_up
  8.0 0.8 constant_dynamic-slice_fusion
  9.6 0.9 constant_dynamic-slice_fusion.1
  10.6 5.1 %collective-permute-start.2 = (bf16[208,512]{1,0:T(8,128)(2,1)S(1)}, bf16[208,512]{1,0:T(8,128)(2,1)S(1)}, u32[]{:S(2)}, u32[]{:S(2)}) collective-permute-start(bf16[208,512]{1,0:T(8,128)(2,1)S(1)} %concatenate.34), channel_id=1, source_target_pairs={{0,3},{1,0},{2,1},{3,2},{4,7},{5,4},{6,5},{7,6},{8,11},{9,8},{10,9... | collective-permute-start | bytes 638984 | tf_op jit(solution)/shard_map/ppermute | solution.py:548
  15.7 1.0 collective-permute-start
  16.7 4.7 %collective-permute-done.2 = bf16[208,512]{1,0:T(8,128)(2,1)S(1)} collective-permute-done((bf16[208,512]{1,0:T(8,128)(2,1)S(1)}, bf16[208,512]{1,0:T(8,128)(2,1)S(1)}, u32[]{:S(2)}, u32[]{:S(2)}) %collective-permute-start.2) | collective-permute-done | bytes 213024 | tf_op jit(solution)/shard_map/ppermute | solution.py:548
  21.4 12.4 %collective-permute-done.1 = bf16[208,512]{1,0:T(8,128)(2,1)S(1)} collective-permute-done((bf16[208,512]{1,0:T(8,128)(2,1)S(1)}, bf16[208,512]{1,0:T(8,128)(2,1)S(1)}, u32[]{:S(2)}, u32[]{:S(2)}) %collective-permute-start.1) | collective-permute-done | bytes 213024 | tf_op jit(solution)/shard_map/ppermute | solution.py:548
  33.9 0.8 pad_maximum_fusion.1
  34.8 0.9 slice.194
  35.8 0.7 pad_maximum_fusion.7
  36.5 0.8 pad_maximum_fusion.5
  37.6 2.8 %collective-permute-start.3 = (bf16[720,512]{1,0:T(8,128)(2,1)}, bf16[720,512]{1,0:T(8,128)(2,1)S(1)}, u32[]{:S(2)}, u32[]{:S(2)}) collective-permute-start(bf16[720,512]{1,0:T(8,128)(2,1)} %slice.194), channel_id=1, source_target_pairs={{0,1},{1,2},{2,3},{4,5},{5,6},{6,7},{8,9},{9,10},{10,11},{12,13},{... | collective-permute-start | bytes 2211848 | tf_op jit(solution)/shard_map/ppermute | solution.py:551
  40.5 0.8 pad_maximum_fusion.2
  41.3 1.3 collective-permute-start.4
  44.0 13.5 %all-gather = bf16[12,4,64,128]{3,2,1,0:T(8,128)(2,1)S(1)} all-gather(bf16[3,4,64,128]{3,2,1,0:T(8,128)(2,1)S(1)} %copy.33), channel_id=2, replica_groups={{0,8,16,24},{4,12,20,28},{1,9,17,25},{5,13,21,29},{2,10,18,26},{6,14,22..., dimensions={0}, use_global_device_ids=true | all-gather | bytes 983040 | tf_op jit(solution)/shard_map/all_gather | solution.py:587
  57.5 0.8 pad_maximum_fusion.4
  58.4 4.3 %collective-permute-start.7 = (bf16[720,512]{1,0:T(8,128)(2,1)S(1)}, bf16[720,512]{1,0:T(8,128)(2,1)S(1)}, u32[]{:S(2)}, u32[]{:S(2)}) collective-permute-start(bf16[720,512]{1,0:T(8,128)(2,1)S(1)} %slice.187), channel_id=1, source_target_pairs={{0,1},{1,2},{2,3},{4,5},{5,6},{6,7},{8,9},{9,10},{10,11},{12,13},{... | collective-permute-start | bytes 2211848 | tf_op jit(solution)/shard_map/ppermute | solution.py:551
  62.7 1.3 collective-permute-start.8
  64.0 1.4 collective-permute-start.9
  65.3 1.5 collective-permute-start.10
  66.9 0.8 copy-done.5
  67.8 15.3 %attention_forward.1 = (bf16[1024,512]{1,0:T(8,128)(2,1)}, bf16[1024,512]{1,0:T(8,128)(2,1)}, bf16[3,1024,512]{2,1,0:T(8,128)(2,1)}, f32[1024,128]{1,0:T(8,128)}...) custom-call(s32[4]{0:T(128)} %lengths.3, bf16[960,512]{1,0:T(8,128)(2,1)} %own.2, ...), custom_call_target="tpu_custom_call" | custom-call | flops 1000 | bytes 1000 | tf_op jit(solution)/shard_map/attention_forward/pallas_call | solution.py:506
  84.1 25.1 %feed_forward.1 = (bf16[768,512]{1,0:T(8,128)(2,1)}, bf16[256,512]{1,0:T(8,128)(2,1)}, bf16[4,4,128,512]{3,2,1,0:T(8,128)(2,1)}, bf16[4,4,128,512]{3,2,1,0:T(8,1...) custom-call(bf16[960,512]{1,0:T(8,128)(2,1)} %own.3, bf16[720,512]{1,0:T(8,128)(2,1)} %copy-done.10, ...), custom_call_target="tpu_custom_call" | custom-call | flops 1000 | bytes 1000 | tf_op jit(solution)/shard_map/feed_forward/pallas_call | solution.py:506
  109.3 1.3 collective-permute-start.12
  110.6 7.5 %norm_backward.1 = (f32[1024,512]{1,0:T(8,128)}, bf16[1024,512]{1,0:T(8,128)(2,1)}, bf16[512,512]{1,0:T(8,128)(2,1)}, f32[8,512]{1,0:T(8,128)}) custom-call(s32[4]{0:T(128)} %lengths.3, f32[1024,512]{1,0:T(8,128)} %get-tuple-element.72.mid, f32[1024,512]{1,0:T(8,128)} %get-tuple-element.76.gnorm, bf16[1024,512]{1,0:T(8,128)(2,1)} %get-tuple-element.77.grad, ...), custom_call_target="tpu_custom_call" | custom-call | flops 1000 | bytes 25000000 | tf_op jit(solution)/shard_map/norm_backward/pallas_call | solution.py:506
  118.2 1.3 copy-done.3
  119.5 3.8 %pair_sum.1 = (bf16[4,128,512]{2,1,0:T(8,128)(2,1)}, bf16[4,128,512]{2,1,0:T(8,128)(2,1)}, bf16[4,128,512]{2,1,0:T(8,128)(2,1)}, bf16[4,128,512]{2,1,0:T(8,128)(2,1)}) custom-call(bf16[4,4,128,512]{3,2,1,0:T(8,128)(2,1)} %get-tuple-element.90.keep, bf16[4,4,128,512]{3,2,1,0:T(8,128)(2,1)} %copy-done.3), custom_call_target="tpu_custom_call" | custom-call | flops 1000 | bytes 1000 | tf_op jit(solution)/shard_map/pair_sum/pallas_call | solution.py:506
  123.3 1.4 collective-permute-start.14
  124.6 1.6 collective-permute-start.15
  126.7 16.6 %attention_backward.1 = (bf16[768,512]{1,0:T(8,128)(2,1)}, bf16[240,512]{1,0:T(8,128)(2,1)}, bf16[4,4,288,128]{3,2,1,0:T(8,128)(2,1)}, bf16[4,4,288,128]{3,2,1,0:T(8,128)(2,1)}) custom-call(bf16[3,1024,512]{2,1,0:T(8,128)(2,1)} %get-tuple-element.74.qkv, f32[1024,128]{1,0:T(8,128)} %get-tuple-element.75.prob, bf16[1024,512]{1,0:T(8,128)(2,1)} %get-tuple-element.80.gcontext, ...), custom_call_target="tpu_custom_call" | custom-call | flops 1000 | bytes 60000000 | tf_op jit(solution)/shard_map/attention_backward/pallas_call | solution.py:506
  143.3 6.9 %collective-permute-done.15 = bf16[4,128,512]{2,1,0:T(8,128)(2,1)} collective-permute-done((bf16[4,128,512]{2,1,0:T(8,128)(2,1)}, bf16[4,128,512]{2,1,0:T(8,128)(2,1)}, u32[]{:S(2)}, u32[]{:S(2)}) %collective-permute-start.15) | collective-permute-done | bytes 524320 | tf_op jit(solution)/shard_map/ppermute | solution.py:545
  150.3 0.8 all-gather.11.cloned.1.call-done
  151.2 1.6 fusion.3
  152.8 0.8 pad_maximum_fusion
  154.2 1.3 add_convert_fusion
  155.5 3.6 %all-to-all-start = ((bf16[4,4,288,128]{3,2,1,0:T(8,128)(2,1)}), bf16[4,4,288,128]{3,2,1,0:T(8,128)(2,1)S(1)}, u32[]{:S(2)}, u32[]{:S(2)}) async-start(bf16[4,4,288,128]{3,2,1,0:T(8,128)(2,1)} %add_convert_fusion), calls=%async_computation | async-start | bytes 2359296 | tf_op jit(solution)/shard_map/all_to_all | solution.py:689
  159.1 1.3 collective-permute-start.18
  161.8 10.8 %collective-permute-start.19 = (bf16[240,512]{1,0:T(8,128)(2,1)S(1)}, bf16[240,512]{1,0:T(8,128)(2,1)S(1)}, u32[]{:S(2)}, u32[]{:S(2)}) collective-permute-start(bf16[240,512]{1,0:T(8,128)(2,1)S(1)} %copy-done.16), channel_id=1, source_target_pairs={{0,3},{4,7},{8,11},{12,15},{16,19},{20,23},{24,27},{28,31}} | collective-permute-start | bytes 737288 | tf_op jit(solution)/shard_map/ppermute | solution.py:551
  172.6 4.8 %spread_rows.2 = bf16[960,512]{1,0:T(8,128)(2,1)} custom-call(bf16[768,512]{1,0:T(8,128)(2,1)} %get-tuple-element.102.quad, bf16[256,512]{1,0:T(8,128)(2,1)} %get-tuple-element.89.low, bf16[768,512]{1,0:T(8,128)(2,1)} %copy-done.7, bf16[4,256,512]{2,1,0:T(8,128)(2,1)} %bitcast.72), custom_call_target="tpu_custom_call" | custom-call | flops 1000 | bytes 1000 | tf_op jit(solution)/shard_map/spread_rows/pallas_call | solution.py:506
  177.4 3.8 %collective-permute-done.19.rest_0_ = bf16[240,512]{1,0:T(8,128)(2,1)S(1)} collective-permute-done((bf16[240,512]{1,0:T(8,128)(2,1)S(1)}, bf16[240,512]{1,0:T(8,128)(2,1)S(1)}, u32[]{:S(2)}, u32[]{:S(2)}) %collective-permute-start.19) | collective-permute-done | bytes 245792 | tf_op jit(solution)/shard_map/ppermute | solution.py:551
  181.9 9.3 %collective-permute-done.18.recv = bf16[768,512]{1,0:T(8,128)(2,1)S(1)} collective-permute-done((bf16[768,512]{1,0:T(8,128)(2,1)S(1)}, bf16[768,512]{1,0:T(8,128)(2,1)S(1)}, u32[]{:S(2)}, u32[]{:S(2)}) %collective-permute-start.18) | collective-permute-done | bytes 786464 | tf_op jit(solution)/shard_map/ppermute | solution.py:551
  191.4 1.8 collective-permute-start.22
  193.2 2.9 %collective-permute-start.23 = (bf16[288,128]{1,0:T(8,128)(2,1)S(1)}, bf16[288,128]{1,0:T(8,128)(2,1)S(1)}, u32[]{:S(2)}, u32[]{:S(2)}) collective-permute-start(bf16[288,128]{1,0:T(8,128)(2,1)S(1)} %get-tuple-element.120), channel_id=1, source_target_pairs={{0,2},{1,3},{2,0},{3,1},{4,6},{5,7},{6,4},{7,5},{8,10},{9,11},{10,... | collective-permute-start | bytes 221192 | tf_op jit(solution)/shard_map/ppermute | solution.py:660
  196.1 5.1 %spread_rows.3 = f32[960,512]{1,0:T(8,128)} custom-call(bf16[768,512]{1,0:T(8,128)(2,1)} %get-tuple-element.108.quad, bf16[240,512]{1,0:T(8,128)(2,1)} %get-tuple-element.106.low, bf16[768,512]{1,0:T(8,128)(2,1)} %copy-done.8, bf16[240,512]{1,0:T(8,128)(2,1)} %copy-done.19, bf16[240,512]{1,0:T(8,128)(2,1)} %copy-done.18, bf16[240,512]{1,0:T(8,128)(2,1)} %copy-done.17), custom_call_target="tpu_custom_call" | custom-call | flops 1000 | bytes 1000 | tf_op jit(solution)/shard_map/spread_rows/pallas_call | solution.py:506
  201.2 1.2 collective-permute-done.24
  202.4 10.9 %all-gather.3 = bf16[2304,128]{1,0:T(8,128)(2,1)} all-gather(bf16[288,128]{1,0:T(8,128)(2,1)S(1)} %fusion.2), channel_id=5, replica_groups={{0,4,8,12,16,20,24,28},{1,5,9,13,17,21,25,29},{2,6,10,14,18,22,26,30},{..., dimensions={0}, use_global_device_ids=true | all-gather | bytes 663552 | tf_op jit(solution)/shard_map/all_gather | solution.py:704
  214.0 2.6 %all-gather.13.cloned.1.call-done = bf16[1024,512]{1,0:T(8,128)(2,1)} async-done(((bf16[128,512]{1,0:T(8,128)(2,1)}), bf16[1024,512]{1,0:T(8,128)(2,1)}) %all-gather.13.cloned.1.call-update) | async-done | bytes 1048592 | tf_op jit(solution)/shard_map/all_gather | solution.py:698
  216.6 3.3 %unpack_weights.1 = (f32[3,512,128]{2,1,0:T(8,128)}, f32[128,512]{1,0:T(8,128)}, f32[512,512]{1,0:T(8,128)}, f32[512,512]{1,0:T(8,128)}) custom-call(bf16[8,288,128]{2,1,0:T(8,128)(2,1)} %bitcast.70, bf16[8,128,512]{2,1,0:T(8,128)(2,1)} %bitcast.71), custom_call_target="tpu_custom_call" | custom-call | flops 1000 | bytes 1000 | tf_op jit(solution)/shard_map/unpack_weights/pallas_call | solution.py:506
  (104 shorter events, 8.1 us)
Async XLA Ops:
  7.2 27.6 %copy-start = (bf16[960,512]{1,0:T(8,128)(2,1)S(1)}, bf16[960,512]{1,0:T(8,128)(2,1)}, u32[]{:S(2)}) copy-start(bf16[960,512]{1,0:T(8,128)(2,1)} %own.2) | copy-start | bytes 2949124
  7.2 76.0 %all-gather.9.cloned.1.call-start = ((), (), s32[]{:S(2)}) async-start(), calls=%async_computation.3 | async-start | bytes 3981312 | tf_op jit(solution)/shard_map/all_gather | solution.py:589
  8.0 27.7 %copy-start.20 = (bf16[1,512]{1,0:T(2,128)(2,1)}, bf16[1,512]{1,0:T(2,128)(2,1)S(1)}, u32[]{:S(2)}) copy-start(bf16[1,512]{1,0:T(2,128)(2,1)S(1)} %reshape.141.b_up) | copy-start | bytes 3076
  10.6 10.8 %collective-permute-start.2 = (bf16[208,512]{1,0:T(8,128)(2,1)S(1)}, bf16[208,512]{1,0:T(8,128)(2,1)S(1)}, u32[]{:S(2)}, u32[]{:S(2)}) collective-permute-start(bf16[208,512]{1,0:T(8,128)(2,1)S(1)} %concatenate.34), channel_id=1, source_target_pairs={{0,3},{1,0},{2,1},{3,2},{4,7},{5,4},{6,5},{7,6},{8,11},{9,8},{10,9... | collective-permute-start | bytes 638984 | tf_op jit(solution)/shard_map/ppermute | solution.py:548
  15.7 18.1 %collective-permute-start.1 = (bf16[208,512]{1,0:T(8,128)(2,1)S(1)}, bf16[208,512]{1,0:T(8,128)(2,1)S(1)}, u32[]{:S(2)}, u32[]{:S(2)}) collective-permute-start(bf16[208,512]{1,0:T(8,128)(2,1)S(1)} %concatenate.34), channel_id=1, source_target_pairs={{0,2},{1,3},{2,0},{3,1},{4,6},{5,7},{6,4},{7,5},{8,10},{9,11},{10,... | collective-permute-start | bytes 638984 | tf_op jit(solution)/shard_map/ppermute | solution.py:548
  15.7 18.1 %collective-permute-start = (bf16[208,512]{1,0:T(8,128)(2,1)S(1)}, bf16[208,512]{1,0:T(8,128)(2,1)S(1)}, u32[]{:S(2)}, u32[]{:S(2)}) collective-permute-start(bf16[208,512]{1,0:T(8,128)(2,1)S(1)} %concatenate.34), channel_id=1, source_target_pairs={{0,1},{1,2},{2,3},{3,0},{4,5},{5,6},{6,7},{7,4},{8,9},{9,10},{10,1... | collective-permute-start | bytes 638984 | tf_op jit(solution)/shard_map/ppermute | solution.py:548
  34.7 116.3 %all-gather.11.cloned.1.call-start = ((), (), s32[]{:S(2)}) async-start(), calls=%async_computation.4 | async-start | bytes 1310720 | tf_op jit(solution)/shard_map/all_gather | solution.py:670
  35.7 4.7 %copy-start.1 = (bf16[960,512]{1,0:T(8,128)(2,1)S(1)}, bf16[960,512]{1,0:T(8,128)(2,1)}, u32[]{:S(2)}) copy-start(bf16[960,512]{1,0:T(8,128)(2,1)} %own.3) | copy-start | bytes 2949124
  37.6 20.8 %collective-permute-start.3 = (bf16[720,512]{1,0:T(8,128)(2,1)}, bf16[720,512]{1,0:T(8,128)(2,1)S(1)}, u32[]{:S(2)}, u32[]{:S(2)}) collective-permute-start(bf16[720,512]{1,0:T(8,128)(2,1)} %slice.194), channel_id=1, source_target_pairs={{0,1},{1,2},{2,3},{4,5},{5,6},{6,7},{8,9},{9,10},{10,11},{12,13},{... | collective-permute-start | bytes 2211848 | tf_op jit(solution)/shard_map/ppermute | solution.py:551
  41.3 17.0 %collective-permute-start.4 = (bf16[256,512]{1,0:T(8,128)(2,1)}, bf16[256,512]{1,0:T(8,128)(2,1)S(1)}, u32[]{:S(2)}, u32[]{:S(2)}) collective-permute-start(bf16[256,512]{1,0:T(8,128)(2,1)} %get-tuple-element.65), channel_id=1, source_target_pairs={{3,0},{7,4},{11,8},{15,12},{19,16},{23,20},{27,24},{31,28}} | collective-permute-start | bytes 786440 | tf_op jit(solution)/shard_map/ppermute | solution.py:551
  42.6 15.7 %collective-permute-start.5 = (bf16[256,512]{1,0:T(8,128)(2,1)}, bf16[256,512]{1,0:T(8,128)(2,1)S(1)}, u32[]{:S(2)}, u32[]{:S(2)}) collective-permute-start(bf16[256,512]{1,0:T(8,128)(2,1)} %get-tuple-element.66), channel_id=1, source_target_pairs={{3,1},{7,5},{11,9},{15,13},{19,17},{23,21},{27,25},{31,29}} | collective-permute-start | bytes 786440 | tf_op jit(solution)/shard_map/ppermute | solution.py:551
  43.3 15.0 %collective-permute-start.6 = (bf16[256,512]{1,0:T(8,128)(2,1)}, bf16[256,512]{1,0:T(8,128)(2,1)S(1)}, u32[]{:S(2)}, u32[]{:S(2)}) collective-permute-start(bf16[256,512]{1,0:T(8,128)(2,1)} %pad_maximum_fusion.7), channel_id=1, source_target_pairs={{3,2},{7,6},{11,10},{15,14},{19,18},{23,22},{27,26},{31,30}} | collective-permute-start | bytes 786440 | tf_op jit(solution)/shard_map/ppermute | solution.py:551
  57.5 9.4 %copy-start.2 = (bf16[12,4,64,128]{3,2,1,0:T(8,128)(2,1)}, bf16[12,4,64,128]{3,2,1,0:T(8,128)(2,1)S(1)}, u32[]{:S(2)}) copy-start(bf16[12,4,64,128]{3,2,1,0:T(8,128)(2,1)S(1)} %all-gather) | copy-start | bytes 2359300
  57.5 9.4 %collective-permute-start.11 = (bf16[4,3,4,64,128]{4,3,2,1,0:T(8,128)(2,1)S(1)}, bf16[4,3,4,64,128]{4,3,2,1,0:T(8,128)(2,1)S(1)}, u32[]{:S(2)}, u32[]{:S(2)}) collective-permute-start(bf16[4,3,4,64,128]{4,3,2,1,0:T(8,128)(2,1)S(1)} %bitcast.68), channel_id=1, source_target_pairs={{0,4},{4,0},{8,12},{12,8},{16,20},{20,16},{24,28},{28,24},{1,5},{5... | collective-permute-start | bytes 2359304 | tf_op jit(solution)/shard_map/ppermute | solution.py:545
  58.3 8.5 %copy-start.12 = (bf16[256,512]{1,0:T(8,128)(2,1)}, bf16[256,512]{1,0:T(8,128)(2,1)S(1)}, u32[]{:S(2)}) copy-start(bf16[256,512]{1,0:T(8,128)(2,1)S(1)} %collective-permute-done.4.low0) | copy-start | bytes 786436
  58.4 8.5 %copy-start.13 = (bf16[256,512]{1,0:T(8,128)(2,1)}, bf16[256,512]{1,0:T(8,128)(2,1)S(1)}, u32[]{:S(2)}) copy-start(bf16[256,512]{1,0:T(8,128)(2,1)S(1)} %collective-permute-done.5.low1) | copy-start | bytes 786436
  58.4 8.5 %copy-start.14 = (bf16[256,512]{1,0:T(8,128)(2,1)}, bf16[256,512]{1,0:T(8,128)(2,1)S(1)}, u32[]{:S(2)}) copy-start(bf16[256,512]{1,0:T(8,128)(2,1)S(1)} %collective-permute-done.6.low2) | copy-start | bytes 786436
  58.4 8.5 %copy-start.9 = (bf16[720,512]{1,0:T(8,128)(2,1)}, bf16[720,512]{1,0:T(8,128)(2,1)S(1)}, u32[]{:S(2)}) copy-start(bf16[720,512]{1,0:T(8,128)(2,1)S(1)} %collective-permute-done.3.recv) | copy-start | bytes 2211844
  58.4 24.7 %collective-permute-start.7 = (bf16[720,512]{1,0:T(8,128)(2,1)S(1)}, bf16[720,512]{1,0:T(8,128)(2,1)S(1)}, u32[]{:S(2)}, u32[]{:S(2)}) collective-permute-start(bf16[720,512]{1,0:T(8,128)(2,1)S(1)} %slice.187), channel_id=1, source_target_pairs={{0,1},{1,2},{2,3},{4,5},{5,6},{6,7},{8,9},{9,10},{10,11},{12,13},{... | collective-permute-start | bytes 2211848 | tf_op jit(solution)/shard_map/ppermute | solution.py:551
  62.7 20.4 %collective-permute-start.8 = (bf16[256,512]{1,0:T(8,128)(2,1)}, bf16[256,512]{1,0:T(8,128)(2,1)S(1)}, u32[]{:S(2)}, u32[]{:S(2)}) collective-permute-start(bf16[256,512]{1,0:T(8,128)(2,1)} %get-tuple-element.69), channel_id=1, source_target_pairs={{3,0},{7,4},{11,8},{15,12},{19,16},{23,20},{27,24},{31,28}} | collective-permute-start | bytes 786440 | tf_op jit(solution)/shard_map/ppermute | solution.py:551
  64.0 19.2 %collective-permute-start.9 = (bf16[256,512]{1,0:T(8,128)(2,1)}, bf16[256,512]{1,0:T(8,128)(2,1)}, u32[]{:S(2)}, u32[]{:S(2)}) collective-permute-start(bf16[256,512]{1,0:T(8,128)(2,1)} %get-tuple-element.70), channel_id=1, source_target_pairs={{3,1},{7,5},{11,9},{15,13},{19,17},{23,21},{27,25},{31,29}} | collective-permute-start | bytes 786440 | tf_op jit(solution)/shard_map/ppermute | solution.py:551
  65.3 17.8 %collective-permute-start.10 = (bf16[256,512]{1,0:T(8,128)(2,1)}, bf16[256,512]{1,0:T(8,128)(2,1)}, u32[]{:S(2)}, u32[]{:S(2)}) collective-permute-start(bf16[256,512]{1,0:T(8,128)(2,1)} %pad_maximum_fusion.4), channel_id=1, source_target_pairs={{3,2},{7,6},{11,10},{15,14},{19,18},{23,22},{27,26},{31,30}} | collective-permute-start | bytes 786440 | tf_op jit(solution)/shard_map/ppermute | solution.py:551
  66.9 0.9 copy-start.5
  83.1 0.9 copy-start.10
  109.1 9.0 %collective-permute-start.13 = (bf16[4,4,128,512]{3,2,1,0:T(8,128)(2,1)}, bf16[4,4,128,512]{3,2,1,0:T(8,128)(2,1)S(1)}, u32[]{:S(2)}, u32[]{:S(2)}) collective-permute-start(bf16[4,4,128,512]{3,2,1,0:T(8,128)(2,1)} %get-tuple-element.91), channel_id=1, source_target_pairs={{0,4},{4,0},{8,12},{12,8},{16,20},{20,16},{24,28},{28,24},{1,5},{5... | collective-permute-start | bytes 6291464 | tf_op jit(solution)/shard_map/ppermute | solution.py:545
  109.3 82.0 %reduce-scatter.2.cloned.1.call-start = ((), (), s32[]{:S(2)}) async-start(), calls=%async_computation.2 | async-start | bytes 655360 | tf_op jit(solution)/shard_map/reduce_scatter | solution.py:687
  109.3 40.9 %collective-permute-start.12 = (bf16[768,512]{1,0:T(8,128)(2,1)}, bf16[768,512]{1,0:T(8,128)(2,1)S(1)}, u32[]{:S(2)}, u32[]{:S(2)}) collective-permute-start(bf16[768,512]{1,0:T(8,128)(2,1)} %get-tuple-element.102.quad), channel_id=1, source_target_pairs={{1,0},{2,1},{3,2},{5,4},{6,5},{7,6},{9,8},{10,9},{11,10},{13,12},{... | collective-permute-start | bytes 2359304 | tf_op jit(solution)/shard_map/ppermute | solution.py:551
  118.1 1.3 copy-start.3
  123.3 20.1 %collective-permute-start.14 = (bf16[4,128,512]{2,1,0:T(8,128)(2,1)}, bf16[4,128,512]{2,1,0:T(8,128)(2,1)S(1)}, u32[]{:S(2)}, u32[]{:S(2)}) collective-permute-start(bf16[4,128,512]{2,1,0:T(8,128)(2,1)} %get-tuple-element.94), channel_id=1, source_target_pairs={{0,8},{4,12},{8,0},{12,4},{16,24},{20,28},{24,16},{28,20},{1,9},{5... | collective-permute-start | bytes 1572872 | tf_op jit(solution)/shard_map/ppermute | solution.py:545
  124.6 25.6 %collective-permute-start.15 = (bf16[4,128,512]{2,1,0:T(8,128)(2,1)}, bf16[4,128,512]{2,1,0:T(8,128)(2,1)}, u32[]{:S(2)}, u32[]{:S(2)}) collective-permute-start(bf16[4,128,512]{2,1,0:T(8,128)(2,1)} %get-tuple-element.95), channel_id=1, source_target_pairs={{0,16},{4,20},{8,24},{12,28},{16,0},{20,4},{24,8},{28,12},{1,17},{... | collective-permute-start | bytes 1572872 | tf_op jit(solution)/shard_map/ppermute | solution.py:545
  126.2 24.1 %collective-permute-start.16 = (bf16[4,128,512]{2,1,0:T(8,128)(2,1)}, bf16[4,128,512]{2,1,0:T(8,128)(2,1)}, u32[]{:S(2)}, u32[]{:S(2)}) collective-permute-start(bf16[4,128,512]{2,1,0:T(8,128)(2,1)} %get-tuple-element.96), channel_id=1, source_target_pairs={{0,24},{4,28},{8,16},{12,20},{16,8},{20,12},{24,0},{28,4},{1,25},{... | collective-permute-start | bytes 1572872 | tf_op jit(solution)/shard_map/ppermute | solution.py:545
  126.7 24.4 %copy-start.11 = (bf16[4,128,512]{2,1,0:T(8,128)(2,1)S(1)}, bf16[4,128,512]{2,1,0:T(8,128)(2,1)}, u32[]{:S(2)}) copy-start(bf16[4,128,512]{2,1,0:T(8,128)(2,1)} %get-tuple-element.97) | copy-start | bytes 1572868
  151.2 3.1 %copy-start.4 = (bf16[4,4,288,128]{3,2,1,0:T(8,128)(2,1)S(1)}, bf16[4,4,288,128]{3,2,1,0:T(8,128)(2,1)}, u32[]{:S(2)}) copy-start(bf16[4,4,288,128]{3,2,1,0:T(8,128)(2,1)} %get-tuple-element.87) | copy-start | bytes 3538948
  151.2 3.1 %collective-permute-start.17 = (bf16[4,4,288,128]{3,2,1,0:T(8,128)(2,1)}, bf16[4,4,288,128]{3,2,1,0:T(8,128)(2,1)S(1)}, u32[]{:S(2)}, u32[]{:S(2)}) collective-permute-start(bf16[4,4,288,128]{3,2,1,0:T(8,128)(2,1)} %get-tuple-element.101), channel_id=1, source_target_pairs={{0,4},{4,0},{8,12},{12,8},{16,20},{20,16},{24,28},{28,24},{1,5},{5... | collective-permute-start | bytes 3538952 | tf_op jit(solution)/shard_map/ppermute | solution.py:545
  153.7 5.5 %copy-start.6 = (bf16[768,512]{1,0:T(8,128)(2,1)S(1)}, bf16[768,512]{1,0:T(8,128)(2,1)}, u32[]{:S(2)}) copy-start(bf16[768,512]{1,0:T(8,128)(2,1)} %get-tuple-element.108.quad) | copy-start | bytes 2359300
  153.7 6.8 %copy-start.16 = (bf16[240,512]{1,0:T(8,128)(2,1)S(1)}, bf16[240,512]{1,0:T(8,128)(2,1)}, u32[]{:S(2)}) copy-start(bf16[240,512]{1,0:T(8,128)(2,1)} %get-tuple-element.106.low) | copy-start | bytes 737284
  155.5 35.7 %all-to-all-start = ((bf16[4,4,288,128]{3,2,1,0:T(8,128)(2,1)}), bf16[4,4,288,128]{3,2,1,0:T(8,128)(2,1)S(1)}, u32[]{:S(2)}, u32[]{:S(2)}) async-start(bf16[4,4,288,128]{3,2,1,0:T(8,128)(2,1)} %add_convert_fusion), calls=%async_computation | async-start | bytes 2359296 | tf_op jit(solution)/shard_map/all_to_all | solution.py:689
  159.1 57.4 %all-gather.13.cloned.1.call-start = ((), (), s32[]{:S(2)}) async-start(), calls=%async_computation.5 | async-start | bytes 1179648 | tf_op jit(solution)/shard_map/all_gather | solution.py:698
  159.1 32.1 %collective-permute-start.18 = (bf16[768,512]{1,0:T(8,128)(2,1)S(1)}, bf16[768,512]{1,0:T(8,128)(2,1)S(1)}, u32[]{:S(2)}, u32[]{:S(2)}) collective-permute-start(bf16[768,512]{1,0:T(8,128)(2,1)S(1)} %copy-done.6), channel_id=1, source_target_pairs={{1,0},{2,1},{3,2},{5,4},{6,5},{7,6},{9,8},{10,9},{11,10},{13,12},{... | collective-permute-start | bytes 2359304 | tf_op jit(solution)/shard_map/ppermute | solution.py:551
  160.5 17.0 %collective-permute-start.21 = (bf16[240,512]{1,0:T(8,128)(2,1)S(1)}, bf16[240,512]{1,0:T(8,128)(2,1)S(1)}, u32[]{:S(2)}, u32[]{:S(2)}) collective-permute-start(bf16[240,512]{1,0:T(8,128)(2,1)S(1)} %copy-done.16), channel_id=1, source_target_pairs={{2,3},{6,7},{10,11},{14,15},{18,19},{22,23},{26,27},{30,31}} | collective-permute-start | bytes 737288 | tf_op jit(solution)/shard_map/ppermute | solution.py:551
  161.1 16.3 %collective-permute-start.20 = (bf16[240,512]{1,0:T(8,128)(2,1)S(1)}, bf16[240,512]{1,0:T(8,128)(2,1)S(1)}, u32[]{:S(2)}, u32[]{:S(2)}) collective-permute-start(bf16[240,512]{1,0:T(8,128)(2,1)S(1)} %copy-done.16), channel_id=1, source_target_pairs={{1,3},{5,7},{9,11},{13,15},{17,19},{21,23},{25,27},{29,31}} | collective-permute-start | bytes 737288 | tf_op jit(solution)/shard_map/ppermute | solution.py:551
  161.8 19.4 %collective-permute-start.19 = (bf16[240,512]{1,0:T(8,128)(2,1)S(1)}, bf16[240,512]{1,0:T(8,128)(2,1)S(1)}, u32[]{:S(2)}, u32[]{:S(2)}) collective-permute-start(bf16[240,512]{1,0:T(8,128)(2,1)S(1)} %copy-done.16), channel_id=1, source_target_pairs={{0,3},{4,7},{8,11},{12,15},{16,19},{20,23},{24,27},{28,31}} | collective-permute-start | bytes 737288 | tf_op jit(solution)/shard_map/ppermute | solution.py:551
  177.4 18.7 %copy-start.17 = (bf16[240,512]{1,0:T(8,128)(2,1)}, bf16[240,512]{1,0:T(8,128)(2,1)S(1)}, u32[]{:S(2)}) copy-start(bf16[240,512]{1,0:T(8,128)(2,1)S(1)} %collective-permute-done.21.rest_2_) | copy-start | bytes 737284
  177.4 3.8 %copy-start.18 = (bf16[240,512]{1,0:T(8,128)(2,1)}, bf16[240,512]{1,0:T(8,128)(2,1)S(1)}, u32[]{:S(2)}) copy-start(bf16[240,512]{1,0:T(8,128)(2,1)S(1)} %collective-permute-done.20.rest_1_) | copy-start | bytes 737284
  191.2 4.9 %copy-start.8 = (bf16[768,512]{1,0:T(8,128)(2,1)}, bf16[768,512]{1,0:T(8,128)(2,1)S(1)}, u32[]{:S(2)}) copy-start(bf16[768,512]{1,0:T(8,128)(2,1)S(1)} %collective-permute-done.18.recv) | copy-start | bytes 2359300
  191.4 9.8 %collective-permute-start.22 = (bf16[288,128]{1,0:T(8,128)(2,1)S(1)}, bf16[288,128]{1,0:T(8,128)(2,1)S(1)}, u32[]{:S(2)}, u32[]{:S(2)}) collective-permute-start(bf16[288,128]{1,0:T(8,128)(2,1)S(1)} %get-tuple-element.119), channel_id=1, source_target_pairs={{0,1},{1,0},{2,3},{3,2},{4,5},{5,4},{6,7},{7,6},{8,9},{9,8},{10,11... | collective-permute-start | bytes 221192 | tf_op jit(solution)/shard_map/ppermute | solution.py:660
  193.2 8.0 %collective-permute-start.23 = (bf16[288,128]{1,0:T(8,128)(2,1)S(1)}, bf16[288,128]{1,0:T(8,128)(2,1)S(1)}, u32[]{:S(2)}, u32[]{:S(2)}) collective-permute-start(bf16[288,128]{1,0:T(8,128)(2,1)S(1)} %get-tuple-element.120), channel_id=1, source_target_pairs={{0,2},{1,3},{2,0},{3,1},{4,6},{5,7},{6,4},{7,5},{8,10},{9,11},{10,... | collective-permute-start | bytes 221192 | tf_op jit(solution)/shard_map/ppermute | solution.py:660
  196.1 6.3 %collective-permute-start.24 = (bf16[288,128]{1,0:T(8,128)(2,1)S(1)}, bf16[288,128]{1,0:T(8,128)(2,1)S(1)}, u32[]{:S(2)}, u32[]{:S(2)}) collective-permute-start(bf16[288,128]{1,0:T(8,128)(2,1)S(1)} %get-tuple-element.121), channel_id=1, source_target_pairs={{0,3},{1,2},{2,1},{3,0},{4,7},{5,6},{6,5},{7,4},{8,11},{9,10},{10,... | collective-permute-start | bytes 221192 | tf_op jit(solution)/shard_map/ppermute | solution.py:660
  (3 other events, 2.3 us)
Sparse Core Ops, SparseCore 0:
  34.8 35.5 all-gather.8
  109.4 41.6 all-gather.10
  153.9 35.4 reduce-scatter.1
  191.4 25.1 all-gather.12

commit v3 on v2

--- a/solution.py
+++ b/solution.py
@@ -267,9 +267,9 @@
 def feed_forward(
     own, recv, low0, low1, low2, mid, gain, shift, b_down, w_up, b_up, w_down, pieces, *rest
 ):
-    y_quad, y_low, keep_hbm, send_hbm, gnorm, grad_hbm, grad_bias = rest[:7]
+    y_quad, y_low, keep_hbm, send_hbm, gnorm_hbm, grad_hbm, grad_bias = rest[:7]
     up_w, down_w, up_t, down_t, bias, normed, grad, normed_t, grad_t = rest[7:16]
-    act_s, gup_s, total, tmp, arrived, keep, send, in_sems, out_sems = rest[16:]
+    act_s, gup_s, total, gnorm, tmp, arrived, keep, send, in_sems, out_sems = rest[16:]
     me, t = lax.axis_index("dp") & 7, lax.axis_index("tensor")
     loading = begin(in_sems, (w_up, up_w.at[0]), (w_down, down_w.at[0]), (pieces, arrived))
     for start in range(0, ROWS, 256):
@@ -324,6 +324,7 @@
                 target[slot, k, 0:64, :] = tmp[0, pl.ds(at, 64), :]
                 target[slot, k, 64:128, :] = tmp[1, pl.ds(at, 64), :]
         begin(out_sems.at[pl.ds(2 * s, 2)], (keep.at[slot], keep_hbm.at[slot]), (send.at[slot], send_hbm.at[slot]))
+    storing += begin(out_sems.at[9:10], (gnorm, gnorm_hbm))
     for start in range(0, ROWS, 256):
         run = slice(start, start + 256)
         out = (mid[run, :] + (total[run, :] + b_down[...])).astype(BF16)
@@ -487,16 +488,21 @@
         out[start : start + 240, :] = rows.astype(out.dtype)
 
 
-def unpack_weights(in_a, in_b, g_qkv, g_out, g_up, g_down, down_t):
+def unpack_weights(in_a, in_b, *rest):
+    outs, (g_qkv, g_out, g_up, g_down, down_t, sems) = rest[:4], rest[4:]
     for p in range(8):
         g_up[64 * p : 64 * p + 64, :] = in_b[p, 0:64, :].astype(F32)
         down_t[64 * p : 64 * p + 64, :] = in_b[p, 64:128, :].astype(F32)
+    storing = begin(sems.at[0:1], (g_up, outs[2]))
     g_down[...] = down_t[...].T
+    storing += begin(sems.at[1:2], (g_down, outs[3]))
     for p in range(8):
         for i in range(3):
             g_qkv[i, 64 * p : 64 * p + 64, :] = in_a[p, 64 * i : 64 * i + 64, :].astype(F32)
         top, side = 64 * (p % 2), 128 * (p // 2)
         g_out[top : top + 64, side : side + 128] = in_a[p, 192:256, :].astype(F32)
+    storing += begin(sems.at[2:4], (g_qkv, outs[0]), (g_out, outs[1]))
+    finish(storing)
 
 
 def call(body, name, ins, outs, scratch=(), moved=1000, far_ins=(), far_outs=()):
@@ -638,11 +644,11 @@
         + [mid, row(ln2_gain), row(ln2_shift), row(b_down), w_up, row(b_up), w_down, pieces_b],
         [quad_rows, struct((256, D), BF16), half_b, half_b, wide, act, struct((4, D), F32)],
         [weights, weights, square, square, pltpu.VMEM((4, D), F32), rows_low, rows_low, turned, turned]
-        + [rows_low, rows_low, pltpu.VMEM((ROWS, D), F32), pltpu.VMEM((2, D, D), BF16)]
+        + [rows_low, rows_low, pltpu.VMEM((ROWS, D), F32), pltpu.VMEM((ROWS, D), F32), pltpu.VMEM((2, D, D), BF16)]
         + [pltpu.VMEM((8, 3, 144, D), BF16), pltpu.VMEM((4, 4, 128, D), BF16), pltpu.VMEM((4, 4, 128, D), BF16)]
-        + [sems((3,)), sems((9,))],
+        + [sems((3,)), sems((10,))],
         far_ins=(9, 11, 12),
-        far_outs=(2, 3, 5),
+        far_outs=(2, 3, 4, 5),
     )
     far_send = to_peer(send_b, 1)
     gmid, gcontext, gw_out, small = call(
@@ -707,7 +713,8 @@
         "unpack_weights",
         [flat_a, flat_b],
         [struct((3, D, 128), F32), struct((128, D), F32), struct((D, D), F32), struct((D, D), F32)],
-        [pltpu.VMEM((D, D), F32)],
+        [pltpu.VMEM((3, D, 128), F32), pltpu.VMEM((128, D), F32)] + [pltpu.VMEM((D, D), F32)] * 3 + [sems((4,))],
+        far_outs=(0, 1, 2, 3),
     )
     sums = mine_a[256:284].astype(F32).reshape(7, D)
     return (

time: 230 us -> 230 us (level)
  no operation moved by 1% of the time
where the time goes in v3:
time: 230 us; the launch traced here: 227 us
  Pallas kernels  81.4 us (35%)
  starting transfers between devices  46.8 us (20%)
  waiting for transfers between devices  42.3 us (18%)
  blocking collectives  24.4 us (11%)
  between operations  14.6 us (6%)
  local copies, waits for them, and re-layouts  9.02 us (4%)
  other arithmetic  8.15 us (4%)
    pallas_call x8, Pallas kernels, call(): pl.pallas_call(body, out_shape=tuple(outs), in_specs=specs, out_specs=tup...  81.4 us
    ppermute x13, starting transfers between devices, hop(): return lax.ppermute(value, 'tensor', pairs)  28.6 us
    ppermute x3, waiting for transfers between devices, along(): lax.ppermute(value, 'tensor', [(i, (i + step) % 4) for i in range(4)])  17.1 us
    all_gather x1, blocking collectives, shards(): plane_a = lax.all_gather(first_a, 'dp', axis=0, axis_index_groups=planes)  13.5 us
    ppermute x13, waiting for transfers between devices, hop(): return lax.ppermute(value, 'tensor', pairs)  13.1 us
    all_gather x1, blocking collectives, shards(): flat_a = lax.all_gather(mine_a, 'dp', axis=0, axis_index_groups=eights)  10.9 us
    ppermute x6, waiting for transfers between devices, to_peer(): return lax.ppermute(value, 'dp', [(i, i ^ e) for i in range(n_dp)])  7.49 us
    ppermute x3, starting transfers between devices, along(): lax.ppermute(value, 'tensor', [(i, (i + step) % 4) for i in range(4)])  6.11 us
  transfers between devices with their start and end apart: 30, of which 9 were waited for; matrix products, arithmetic and copies ran while one was open for 4% of the time, Pallas kernels for 23%

profile of v3, /device:TPU:0, one launch (start us, length us, event | category | flops | bytes accessed | tf_op | source)
XLA Modules:
  0.0 226.6 jit_solution(17506692488807293815)
XLA Ops:
  7.3 0.8 reshape.141.b_up
  8.0 0.8 constant_dynamic-slice_fusion
  9.6 0.9 constant_dynamic-slice_fusion.1
  10.6 5.1 %collective-permute-start.2 = (bf16[208,512]{1,0:T(8,128)(2,1)S(1)}, bf16[208,512]{1,0:T(8,128)(2,1)S(1)}, u32[]{:S(2)}, u32[]{:S(2)}) collective-permute-start(bf16[208,512]{1,0:T(8,128)(2,1)S(1)} %concatenate.34), channel_id=1, source_target_pairs={{0,3},{1,0},{2,1},{3,2},{4,7},{5,4},{6,5},{7,6},{8,11},{9,8},{10,9... | collective-permute-start | bytes 638984 | tf_op jit(solution)/shard_map/ppermute | solution.py:554
  15.7 1.0 collective-permute-start
  16.7 4.7 %collective-permute-done.2 = bf16[208,512]{1,0:T(8,128)(2,1)S(1)} collective-permute-done((bf16[208,512]{1,0:T(8,128)(2,1)S(1)}, bf16[208,512]{1,0:T(8,128)(2,1)S(1)}, u32[]{:S(2)}, u32[]{:S(2)}) %collective-permute-start.2) | collective-permute-done | bytes 213024 | tf_op jit(solution)/shard_map/ppermute | solution.py:554
  21.4 12.4 %collective-permute-done.1 = bf16[208,512]{1,0:T(8,128)(2,1)S(1)} collective-permute-done((bf16[208,512]{1,0:T(8,128)(2,1)S(1)}, bf16[208,512]{1,0:T(8,128)(2,1)S(1)}, u32[]{:S(2)}, u32[]{:S(2)}) %collective-permute-start.1) | collective-permute-done | bytes 213024 | tf_op jit(solution)/shard_map/ppermute | solution.py:554
  33.9 0.8 pad_maximum_fusion.1
  34.8 0.9 slice.194
  35.8 0.7 pad_maximum_fusion.7
  36.5 0.8 pad_maximum_fusion.5
  37.6 2.8 %collective-permute-start.3 = (bf16[720,512]{1,0:T(8,128)(2,1)}, bf16[720,512]{1,0:T(8,128)(2,1)S(1)}, u32[]{:S(2)}, u32[]{:S(2)}) collective-permute-start(bf16[720,512]{1,0:T(8,128)(2,1)} %slice.194), channel_id=1, source_target_pairs={{0,1},{1,2},{2,3},{4,5},{5,6},{6,7},{8,9},{9,10},{10,11},{12,13},{... | collective-permute-start | bytes 2211848 | tf_op jit(solution)/shard_map/ppermute | solution.py:557
  40.5 0.8 pad_maximum_fusion.2
  41.3 1.3 collective-permute-start.4
  44.0 13.5 %all-gather = bf16[12,4,64,128]{3,2,1,0:T(8,128)(2,1)S(1)} all-gather(bf16[3,4,64,128]{3,2,1,0:T(8,128)(2,1)S(1)} %copy.33), channel_id=2, replica_groups={{0,8,16,24},{4,12,20,28},{1,9,17,25},{5,13,21,29},{2,10,18,26},{6,14,22..., dimensions={0}, use_global_device_ids=true | all-gather | bytes 983040 | tf_op jit(solution)/shard_map/all_gather | solution.py:593
  57.5 0.8 pad_maximum_fusion.4
  58.4 4.3 %collective-permute-start.7 = (bf16[720,512]{1,0:T(8,128)(2,1)S(1)}, bf16[720,512]{1,0:T(8,128)(2,1)S(1)}, u32[]{:S(2)}, u32[]{:S(2)}) collective-permute-start(bf16[720,512]{1,0:T(8,128)(2,1)S(1)} %slice.187), channel_id=1, source_target_pairs={{0,1},{1,2},{2,3},{4,5},{5,6},{6,7},{8,9},{9,10},{10,11},{12,13},{... | collective-permute-start | bytes 2211848 | tf_op jit(solution)/shard_map/ppermute | solution.py:557
  62.7 1.3 collective-permute-start.8
  64.0 1.4 collective-permute-start.9
  65.3 1.5 collective-permute-start.10
  66.9 0.8 copy-done.5
  67.8 15.3 %attention_forward.1 = (bf16[1024,512]{1,0:T(8,128)(2,1)}, bf16[1024,512]{1,0:T(8,128)(2,1)}, bf16[3,1024,512]{2,1,0:T(8,128)(2,1)}, f32[1024,128]{1,0:T(8,128)}...) custom-call(s32[4]{0:T(128)} %lengths.3, bf16[960,512]{1,0:T(8,128)(2,1)} %own.2, ...), custom_call_target="tpu_custom_call" | custom-call | flops 1000 | bytes 1000 | tf_op jit(solution)/shard_map/attention_forward/pallas_call | solution.py:512
  84.1 25.0 %feed_forward.1 = (bf16[768,512]{1,0:T(8,128)(2,1)}, bf16[256,512]{1,0:T(8,128)(2,1)}, bf16[4,4,128,512]{3,2,1,0:T(8,128)(2,1)}, bf16[4,4,128,512]{3,2,1,0:T(8,1...) custom-call(bf16[960,512]{1,0:T(8,128)(2,1)} %own.3, bf16[720,512]{1,0:T(8,128)(2,1)} %copy-done.10, ...), custom_call_target="tpu_custom_call" | custom-call | flops 1000 | bytes 1000 | tf_op jit(solution)/shard_map/feed_forward/pallas_call | solution.py:512
  109.3 1.3 collective-permute-start.12
  110.6 7.5 %norm_backward.1 = (f32[1024,512]{1,0:T(8,128)}, bf16[1024,512]{1,0:T(8,128)(2,1)}, bf16[512,512]{1,0:T(8,128)(2,1)}, f32[8,512]{1,0:T(8,128)}) custom-call(s32[4]{0:T(128)} %lengths.3, f32[1024,512]{1,0:T(8,128)} %get-tuple-element.72.mid, f32[1024,512]{1,0:T(8,128)} %get-tuple-element.76.gnorm, bf16[1024,512]{1,0:T(8,128)(2,1)} %get-tuple-element.77.grad, ...), custom_call_target="tpu_custom_call" | custom-call | flops 1000 | bytes 25000000 | tf_op jit(solution)/shard_map/norm_backward/pallas_call | solution.py:512
  118.1 1.3 copy-done.3
  119.4 3.8 %pair_sum.1 = (bf16[4,128,512]{2,1,0:T(8,128)(2,1)}, bf16[4,128,512]{2,1,0:T(8,128)(2,1)}, bf16[4,128,512]{2,1,0:T(8,128)(2,1)}, bf16[4,128,512]{2,1,0:T(8,128)(2,1)}) custom-call(bf16[4,4,128,512]{3,2,1,0:T(8,128)(2,1)} %get-tuple-element.90.keep, bf16[4,4,128,512]{3,2,1,0:T(8,128)(2,1)} %copy-done.3), custom_call_target="tpu_custom_call" | custom-call | flops 1000 | bytes 1000 | tf_op jit(solution)/shard_map/pair_sum/pallas_call | solution.py:512
  123.2 1.4 collective-permute-start.14
  124.6 1.6 collective-permute-start.15
  126.7 16.6 %attention_backward.1 = (bf16[768,512]{1,0:T(8,128)(2,1)}, bf16[240,512]{1,0:T(8,128)(2,1)}, bf16[4,4,288,128]{3,2,1,0:T(8,128)(2,1)}, bf16[4,4,288,128]{3,2,1,0:T(8,128)(2,1)}) custom-call(bf16[3,1024,512]{2,1,0:T(8,128)(2,1)} %get-tuple-element.74.qkv, f32[1024,128]{1,0:T(8,128)} %get-tuple-element.75.prob, bf16[1024,512]{1,0:T(8,128)(2,1)} %get-tuple-element.80.gcontext, ...), custom_call_target="tpu_custom_call" | custom-call | flops 1000 | bytes 60000000 | tf_op jit(solution)/shard_map/attention_backward/pallas_call | solution.py:512
  143.3 6.9 %collective-permute-done.15 = bf16[4,128,512]{2,1,0:T(8,128)(2,1)} collective-permute-done((bf16[4,128,512]{2,1,0:T(8,128)(2,1)}, bf16[4,128,512]{2,1,0:T(8,128)(2,1)}, u32[]{:S(2)}, u32[]{:S(2)}) %collective-permute-start.15) | collective-permute-done | bytes 524320 | tf_op jit(solution)/shard_map/ppermute | solution.py:551
  150.2 0.8 all-gather.11.cloned.1.call-done
  151.1 1.6 fusion.3
  152.8 0.8 pad_maximum_fusion
  154.2 1.3 add_convert_fusion
  155.5 3.6 %all-to-all-start = ((bf16[4,4,288,128]{3,2,1,0:T(8,128)(2,1)}), bf16[4,4,288,128]{3,2,1,0:T(8,128)(2,1)S(1)}, u32[]{:S(2)}, u32[]{:S(2)}) async-start(bf16[4,4,288,128]{3,2,1,0:T(8,128)(2,1)} %add_convert_fusion), calls=%async_computation | async-start | bytes 2359296 | tf_op jit(solution)/shard_map/all_to_all | solution.py:695
  159.1 1.3 collective-permute-start.18
  161.8 10.8 %collective-permute-start.19 = (bf16[240,512]{1,0:T(8,128)(2,1)S(1)}, bf16[240,512]{1,0:T(8,128)(2,1)S(1)}, u32[]{:S(2)}, u32[]{:S(2)}) collective-permute-start(bf16[240,512]{1,0:T(8,128)(2,1)S(1)} %copy-done.16), channel_id=1, source_target_pairs={{0,3},{4,7},{8,11},{12,15},{16,19},{20,23},{24,27},{28,31}} | collective-permute-start | bytes 737288 | tf_op jit(solution)/shard_map/ppermute | solution.py:557
  172.6 4.8 %spread_rows.2 = bf16[960,512]{1,0:T(8,128)(2,1)} custom-call(bf16[768,512]{1,0:T(8,128)(2,1)} %get-tuple-element.102.quad, bf16[256,512]{1,0:T(8,128)(2,1)} %get-tuple-element.89.low, bf16[768,512]{1,0:T(8,128)(2,1)} %copy-done.7, bf16[4,256,512]{2,1,0:T(8,128)(2,1)} %bitcast.72), custom_call_target="tpu_custom_call" | custom-call | flops 1000 | bytes 1000 | tf_op jit(solution)/shard_map/spread_rows/pallas_call | solution.py:512
  177.4 3.8 %collective-permute-done.19.rest_0_ = bf16[240,512]{1,0:T(8,128)(2,1)S(1)} collective-permute-done((bf16[240,512]{1,0:T(8,128)(2,1)S(1)}, bf16[240,512]{1,0:T(8,128)(2,1)S(1)}, u32[]{:S(2)}, u32[]{:S(2)}) %collective-permute-start.19) | collective-permute-done | bytes 245792 | tf_op jit(solution)/shard_map/ppermute | solution.py:557
  181.9 9.3 %collective-permute-done.18.recv = bf16[768,512]{1,0:T(8,128)(2,1)S(1)} collective-permute-done((bf16[768,512]{1,0:T(8,128)(2,1)S(1)}, bf16[768,512]{1,0:T(8,128)(2,1)S(1)}, u32[]{:S(2)}, u32[]{:S(2)}) %collective-permute-start.18) | collective-permute-done | bytes 786464 | tf_op jit(solution)/shard_map/ppermute | solution.py:557
  191.4 1.8 collective-permute-start.22
  193.1 2.9 %collective-permute-start.23 = (bf16[288,128]{1,0:T(8,128)(2,1)S(1)}, bf16[288,128]{1,0:T(8,128)(2,1)S(1)}, u32[]{:S(2)}, u32[]{:S(2)}) collective-permute-start(bf16[288,128]{1,0:T(8,128)(2,1)S(1)} %get-tuple-element.120), channel_id=1, source_target_pairs={{0,2},{1,3},{2,0},{3,1},{4,6},{5,7},{6,4},{7,5},{8,10},{9,11},{10,... | collective-permute-start | bytes 221192 | tf_op jit(solution)/shard_map/ppermute | solution.py:666
  196.1 5.1 %spread_rows.3 = f32[960,512]{1,0:T(8,128)} custom-call(bf16[768,512]{1,0:T(8,128)(2,1)} %get-tuple-element.108.quad, bf16[240,512]{1,0:T(8,128)(2,1)} %get-tuple-element.106.low, bf16[768,512]{1,0:T(8,128)(2,1)} %copy-done.8, bf16[240,512]{1,0:T(8,128)(2,1)} %copy-done.19, bf16[240,512]{1,0:T(8,128)(2,1)} %copy-done.18, bf16[240,512]{1,0:T(8,128)(2,1)} %copy-done.17), custom_call_target="tpu_custom_call" | custom-call | flops 1000 | bytes 1000 | tf_op jit(solution)/shard_map/spread_rows/pallas_call | solution.py:512
  201.2 1.1 collective-permute-done.24
  202.4 10.9 %all-gather.3 = bf16[2304,128]{1,0:T(8,128)(2,1)} all-gather(bf16[288,128]{1,0:T(8,128)(2,1)S(1)} %fusion.2), channel_id=5, replica_groups={{0,4,8,12,16,20,24,28},{1,5,9,13,17,21,25,29},{2,6,10,14,18,22,26,30},{..., dimensions={0}, use_global_device_ids=true | all-gather | bytes 663552 | tf_op jit(solution)/shard_map/all_gather | solution.py:710
  213.9 2.6 %all-gather.13.cloned.1.call-done = bf16[1024,512]{1,0:T(8,128)(2,1)} async-done(((bf16[128,512]{1,0:T(8,128)(2,1)}), bf16[1024,512]{1,0:T(8,128)(2,1)}) %all-gather.13.cloned.1.call-update) | async-done | bytes 1048592 | tf_op jit(solution)/shard_map/all_gather | solution.py:704
  216.5 3.4 %unpack_weights.1 = (f32[3,512,128]{2,1,0:T(8,128)}, f32[128,512]{1,0:T(8,128)}, f32[512,512]{1,0:T(8,128)}, f32[512,512]{1,0:T(8,128)}) custom-call(bf16[8,288,128]{2,1,0:T(8,128)(2,1)} %bitcast.70, bf16[8,128,512]{2,1,0:T(8,128)(2,1)} %bitcast.71), custom_call_target="tpu_custom_call" | custom-call | flops 1000 | bytes 1000 | tf_op jit(solution)/shard_map/unpack_weights/pallas_call | solution.py:512
  (104 shorter events, 8.0 us)
Async XLA Ops:
  7.2 27.6 %copy-start = (bf16[960,512]{1,0:T(8,128)(2,1)S(1)}, bf16[960,512]{1,0:T(8,128)(2,1)}, u32[]{:S(2)}) copy-start(bf16[960,512]{1,0:T(8,128)(2,1)} %own.2) | copy-start | bytes 2949124
  7.2 76.0 %all-gather.9.cloned.1.call-start = ((), (), s32[]{:S(2)}) async-start(), calls=%async_computation.3 | async-start | bytes 3981312 | tf_op jit(solution)/shard_map/all_gather | solution.py:595
  8.0 27.7 %copy-start.20 = (bf16[1,512]{1,0:T(2,128)(2,1)}, bf16[1,512]{1,0:T(2,128)(2,1)S(1)}, u32[]{:S(2)}) copy-start(bf16[1,512]{1,0:T(2,128)(2,1)S(1)} %reshape.141.b_up) | copy-start | bytes 3076
  10.6 10.8 %collective-permute-start.2 = (bf16[208,512]{1,0:T(8,128)(2,1)S(1)}, bf16[208,512]{1,0:T(8,128)(2,1)S(1)}, u32[]{:S(2)}, u32[]{:S(2)}) collective-permute-start(bf16[208,512]{1,0:T(8,128)(2,1)S(1)} %concatenate.34), channel_id=1, source_target_pairs={{0,3},{1,0},{2,1},{3,2},{4,7},{5,4},{6,5},{7,6},{8,11},{9,8},{10,9... | collective-permute-start | bytes 638984 | tf_op jit(solution)/shard_map/ppermute | solution.py:554
  15.7 18.1 %collective-permute-start.1 = (bf16[208,512]{1,0:T(8,128)(2,1)S(1)}, bf16[208,512]{1,0:T(8,128)(2,1)S(1)}, u32[]{:S(2)}, u32[]{:S(2)}) collective-permute-start(bf16[208,512]{1,0:T(8,128)(2,1)S(1)} %concatenate.34), channel_id=1, source_target_pairs={{0,2},{1,3},{2,0},{3,1},{4,6},{5,7},{6,4},{7,5},{8,10},{9,11},{10,... | collective-permute-start | bytes 638984 | tf_op jit(solution)/shard_map/ppermute | solution.py:554
  15.7 18.1 %collective-permute-start = (bf16[208,512]{1,0:T(8,128)(2,1)S(1)}, bf16[208,512]{1,0:T(8,128)(2,1)S(1)}, u32[]{:S(2)}, u32[]{:S(2)}) collective-permute-start(bf16[208,512]{1,0:T(8,128)(2,1)S(1)} %concatenate.34), channel_id=1, source_target_pairs={{0,1},{1,2},{2,3},{3,0},{4,5},{5,6},{6,7},{7,4},{8,9},{9,10},{10,1... | collective-permute-start | bytes 638984 | tf_op jit(solution)/shard_map/ppermute | solution.py:554
  34.7 116.3 %all-gather.11.cloned.1.call-start = ((), (), s32[]{:S(2)}) async-start(), calls=%async_computation.4 | async-start | bytes 1310720 | tf_op jit(solution)/shard_map/all_gather | solution.py:676
  35.7 4.7 %copy-start.1 = (bf16[960,512]{1,0:T(8,128)(2,1)S(1)}, bf16[960,512]{1,0:T(8,128)(2,1)}, u32[]{:S(2)}) copy-start(bf16[960,512]{1,0:T(8,128)(2,1)} %own.3) | copy-start | bytes 2949124
  37.6 20.8 %collective-permute-start.3 = (bf16[720,512]{1,0:T(8,128)(2,1)}, bf16[720,512]{1,0:T(8,128)(2,1)S(1)}, u32[]{:S(2)}, u32[]{:S(2)}) collective-permute-start(bf16[720,512]{1,0:T(8,128)(2,1)} %slice.194), channel_id=1, source_target_pairs={{0,1},{1,2},{2,3},{4,5},{5,6},{6,7},{8,9},{9,10},{10,11},{12,13},{... | collective-permute-start | bytes 2211848 | tf_op jit(solution)/shard_map/ppermute | solution.py:557
  41.3 17.0 %collective-permute-start.4 = (bf16[256,512]{1,0:T(8,128)(2,1)}, bf16[256,512]{1,0:T(8,128)(2,1)S(1)}, u32[]{:S(2)}, u32[]{:S(2)}) collective-permute-start(bf16[256,512]{1,0:T(8,128)(2,1)} %get-tuple-element.65), channel_id=1, source_target_pairs={{3,0},{7,4},{11,8},{15,12},{19,16},{23,20},{27,24},{31,28}} | collective-permute-start | bytes 786440 | tf_op jit(solution)/shard_map/ppermute | solution.py:557
  42.6 15.7 %collective-permute-start.5 = (bf16[256,512]{1,0:T(8,128)(2,1)}, bf16[256,512]{1,0:T(8,128)(2,1)S(1)}, u32[]{:S(2)}, u32[]{:S(2)}) collective-permute-start(bf16[256,512]{1,0:T(8,128)(2,1)} %get-tuple-element.66), channel_id=1, source_target_pairs={{3,1},{7,5},{11,9},{15,13},{19,17},{23,21},{27,25},{31,29}} | collective-permute-start | bytes 786440 | tf_op jit(solution)/shard_map/ppermute | solution.py:557
  43.3 15.0 %collective-permute-start.6 = (bf16[256,512]{1,0:T(8,128)(2,1)}, bf16[256,512]{1,0:T(8,128)(2,1)S(1)}, u32[]{:S(2)}, u32[]{:S(2)}) collective-permute-start(bf16[256,512]{1,0:T(8,128)(2,1)} %pad_maximum_fusion.7), channel_id=1, source_target_pairs={{3,2},{7,6},{11,10},{15,14},{19,18},{23,22},{27,26},{31,30}} | collective-permute-start | bytes 786440 | tf_op jit(solution)/shard_map/ppermute | solution.py:557
  57.5 9.4 %copy-start.2 = (bf16[12,4,64,128]{3,2,1,0:T(8,128)(2,1)}, bf16[12,4,64,128]{3,2,1,0:T(8,128)(2,1)S(1)}, u32[]{:S(2)}) copy-start(bf16[12,4,64,128]{3,2,1,0:T(8,128)(2,1)S(1)} %all-gather) | copy-start | bytes 2359300
  57.5 9.4 %collective-permute-start.11 = (bf16[4,3,4,64,128]{4,3,2,1,0:T(8,128)(2,1)S(1)}, bf16[4,3,4,64,128]{4,3,2,1,0:T(8,128)(2,1)S(1)}, u32[]{:S(2)}, u32[]{:S(2)}) collective-permute-start(bf16[4,3,4,64,128]{4,3,2,1,0:T(8,128)(2,1)S(1)} %bitcast.68), channel_id=1, source_target_pairs={{0,4},{4,0},{8,12},{12,8},{16,20},{20,16},{24,28},{28,24},{1,5},{5... | collective-permute-start | bytes 2359304 | tf_op jit(solution)/shard_map/ppermute | solution.py:551
  58.3 8.5 %copy-start.12 = (bf16[256,512]{1,0:T(8,128)(2,1)}, bf16[256,512]{1,0:T(8,128)(2,1)S(1)}, u32[]{:S(2)}) copy-start(bf16[256,512]{1,0:T(8,128)(2,1)S(1)} %collective-permute-done.4.low0) | copy-start | bytes 786436
  58.4 8.5 %copy-start.13 = (bf16[256,512]{1,0:T(8,128)(2,1)}, bf16[256,512]{1,0:T(8,128)(2,1)S(1)}, u32[]{:S(2)}) copy-start(bf16[256,512]{1,0:T(8,128)(2,1)S(1)} %collective-permute-done.5.low1) | copy-start | bytes 786436
  58.4 8.5 %copy-start.14 = (bf16[256,512]{1,0:T(8,128)(2,1)}, bf16[256,512]{1,0:T(8,128)(2,1)S(1)}, u32[]{:S(2)}) copy-start(bf16[256,512]{1,0:T(8,128)(2,1)S(1)} %collective-permute-done.6.low2) | copy-start | bytes 786436
  58.4 8.5 %copy-start.9 = (bf16[720,512]{1,0:T(8,128)(2,1)}, bf16[720,512]{1,0:T(8,128)(2,1)S(1)}, u32[]{:S(2)}) copy-start(bf16[720,512]{1,0:T(8,128)(2,1)S(1)} %collective-permute-done.3.recv) | copy-start | bytes 2211844
  58.4 24.7 %collective-permute-start.7 = (bf16[720,512]{1,0:T(8,128)(2,1)S(1)}, bf16[720,512]{1,0:T(8,128)(2,1)S(1)}, u32[]{:S(2)}, u32[]{:S(2)}) collective-permute-start(bf16[720,512]{1,0:T(8,128)(2,1)S(1)} %slice.187), channel_id=1, source_target_pairs={{0,1},{1,2},{2,3},{4,5},{5,6},{6,7},{8,9},{9,10},{10,11},{12,13},{... | collective-permute-start | bytes 2211848 | tf_op jit(solution)/shard_map/ppermute | solution.py:557
  62.7 20.4 %collective-permute-start.8 = (bf16[256,512]{1,0:T(8,128)(2,1)}, bf16[256,512]{1,0:T(8,128)(2,1)S(1)}, u32[]{:S(2)}, u32[]{:S(2)}) collective-permute-start(bf16[256,512]{1,0:T(8,128)(2,1)} %get-tuple-element.69), channel_id=1, source_target_pairs={{3,0},{7,4},{11,8},{15,12},{19,16},{23,20},{27,24},{31,28}} | collective-permute-start | bytes 786440 | tf_op jit(solution)/shard_map/ppermute | solution.py:557
  64.0 19.2 %collective-permute-start.9 = (bf16[256,512]{1,0:T(8,128)(2,1)}, bf16[256,512]{1,0:T(8,128)(2,1)}, u32[]{:S(2)}, u32[]{:S(2)}) collective-permute-start(bf16[256,512]{1,0:T(8,128)(2,1)} %get-tuple-element.70), channel_id=1, source_target_pairs={{3,1},{7,5},{11,9},{15,13},{19,17},{23,21},{27,25},{31,29}} | collective-permute-start | bytes 786440 | tf_op jit(solution)/shard_map/ppermute | solution.py:557
  65.3 17.8 %collective-permute-start.10 = (bf16[256,512]{1,0:T(8,128)(2,1)}, bf16[256,512]{1,0:T(8,128)(2,1)}, u32[]{:S(2)}, u32[]{:S(2)}) collective-permute-start(bf16[256,512]{1,0:T(8,128)(2,1)} %pad_maximum_fusion.4), channel_id=1, source_target_pairs={{3,2},{7,6},{11,10},{15,14},{19,18},{23,22},{27,26},{31,30}} | collective-permute-start | bytes 786440 | tf_op jit(solution)/shard_map/ppermute | solution.py:557
  66.9 0.9 copy-start.5
  83.1 0.9 copy-start.10
  109.1 9.0 %collective-permute-start.13 = (bf16[4,4,128,512]{3,2,1,0:T(8,128)(2,1)}, bf16[4,4,128,512]{3,2,1,0:T(8,128)(2,1)S(1)}, u32[]{:S(2)}, u32[]{:S(2)}) collective-permute-start(bf16[4,4,128,512]{3,2,1,0:T(8,128)(2,1)} %get-tuple-element.91), channel_id=1, source_target_pairs={{0,4},{4,0},{8,12},{12,8},{16,20},{20,16},{24,28},{28,24},{1,5},{5... | collective-permute-start | bytes 6291464 | tf_op jit(solution)/shard_map/ppermute | solution.py:551
  109.2 82.0 %reduce-scatter.2.cloned.1.call-start = ((), (), s32[]{:S(2)}) async-start(), calls=%async_computation.2 | async-start | bytes 655360 | tf_op jit(solution)/shard_map/reduce_scatter | solution.py:693
  109.3 40.9 %collective-permute-start.12 = (bf16[768,512]{1,0:T(8,128)(2,1)}, bf16[768,512]{1,0:T(8,128)(2,1)S(1)}, u32[]{:S(2)}, u32[]{:S(2)}) collective-permute-start(bf16[768,512]{1,0:T(8,128)(2,1)} %get-tuple-element.102.quad), channel_id=1, source_target_pairs={{1,0},{2,1},{3,2},{5,4},{6,5},{7,6},{9,8},{10,9},{11,10},{13,12},{... | collective-permute-start | bytes 2359304 | tf_op jit(solution)/shard_map/ppermute | solution.py:557
  118.1 1.3 copy-start.3
  123.2 20.1 %collective-permute-start.14 = (bf16[4,128,512]{2,1,0:T(8,128)(2,1)}, bf16[4,128,512]{2,1,0:T(8,128)(2,1)S(1)}, u32[]{:S(2)}, u32[]{:S(2)}) collective-permute-start(bf16[4,128,512]{2,1,0:T(8,128)(2,1)} %get-tuple-element.94), channel_id=1, source_target_pairs={{0,8},{4,12},{8,0},{12,4},{16,24},{20,28},{24,16},{28,20},{1,9},{5... | collective-permute-start | bytes 1572872 | tf_op jit(solution)/shard_map/ppermute | solution.py:551
  124.6 25.6 %collective-permute-start.15 = (bf16[4,128,512]{2,1,0:T(8,128)(2,1)}, bf16[4,128,512]{2,1,0:T(8,128)(2,1)}, u32[]{:S(2)}, u32[]{:S(2)}) collective-permute-start(bf16[4,128,512]{2,1,0:T(8,128)(2,1)} %get-tuple-element.95), channel_id=1, source_target_pairs={{0,16},{4,20},{8,24},{12,28},{16,0},{20,4},{24,8},{28,12},{1,17},{... | collective-permute-start | bytes 1572872 | tf_op jit(solution)/shard_map/ppermute | solution.py:551
  126.1 24.1 %collective-permute-start.16 = (bf16[4,128,512]{2,1,0:T(8,128)(2,1)}, bf16[4,128,512]{2,1,0:T(8,128)(2,1)}, u32[]{:S(2)}, u32[]{:S(2)}) collective-permute-start(bf16[4,128,512]{2,1,0:T(8,128)(2,1)} %get-tuple-element.96), channel_id=1, source_target_pairs={{0,24},{4,28},{8,16},{12,20},{16,8},{20,12},{24,0},{28,4},{1,25},{... | collective-permute-start | bytes 1572872 | tf_op jit(solution)/shard_map/ppermute | solution.py:551
  126.7 24.4 %copy-start.11 = (bf16[4,128,512]{2,1,0:T(8,128)(2,1)S(1)}, bf16[4,128,512]{2,1,0:T(8,128)(2,1)}, u32[]{:S(2)}) copy-start(bf16[4,128,512]{2,1,0:T(8,128)(2,1)} %get-tuple-element.97) | copy-start | bytes 1572868
  151.1 3.1 %copy-start.4 = (bf16[4,4,288,128]{3,2,1,0:T(8,128)(2,1)S(1)}, bf16[4,4,288,128]{3,2,1,0:T(8,128)(2,1)}, u32[]{:S(2)}) copy-start(bf16[4,4,288,128]{3,2,1,0:T(8,128)(2,1)} %get-tuple-element.87) | copy-start | bytes 3538948
  151.1 3.1 %collective-permute-start.17 = (bf16[4,4,288,128]{3,2,1,0:T(8,128)(2,1)}, bf16[4,4,288,128]{3,2,1,0:T(8,128)(2,1)S(1)}, u32[]{:S(2)}, u32[]{:S(2)}) collective-permute-start(bf16[4,4,288,128]{3,2,1,0:T(8,128)(2,1)} %get-tuple-element.101), channel_id=1, source_target_pairs={{0,4},{4,0},{8,12},{12,8},{16,20},{20,16},{24,28},{28,24},{1,5},{5... | collective-permute-start | bytes 3538952 | tf_op jit(solution)/shard_map/ppermute | solution.py:551
  153.6 5.5 %copy-start.6 = (bf16[768,512]{1,0:T(8,128)(2,1)S(1)}, bf16[768,512]{1,0:T(8,128)(2,1)}, u32[]{:S(2)}) copy-start(bf16[768,512]{1,0:T(8,128)(2,1)} %get-tuple-element.108.quad) | copy-start | bytes 2359300
  153.6 6.8 %copy-start.16 = (bf16[240,512]{1,0:T(8,128)(2,1)S(1)}, bf16[240,512]{1,0:T(8,128)(2,1)}, u32[]{:S(2)}) copy-start(bf16[240,512]{1,0:T(8,128)(2,1)} %get-tuple-element.106.low) | copy-start | bytes 737284
  155.5 35.7 %all-to-all-start = ((bf16[4,4,288,128]{3,2,1,0:T(8,128)(2,1)}), bf16[4,4,288,128]{3,2,1,0:T(8,128)(2,1)S(1)}, u32[]{:S(2)}, u32[]{:S(2)}) async-start(bf16[4,4,288,128]{3,2,1,0:T(8,128)(2,1)} %add_convert_fusion), calls=%async_computation | async-start | bytes 2359296 | tf_op jit(solution)/shard_map/all_to_all | solution.py:695
  159.1 57.4 %all-gather.13.cloned.1.call-start = ((), (), s32[]{:S(2)}) async-start(), calls=%async_computation.5 | async-start | bytes 1179648 | tf_op jit(solution)/shard_map/all_gather | solution.py:704
  159.1 32.1 %collective-permute-start.18 = (bf16[768,512]{1,0:T(8,128)(2,1)S(1)}, bf16[768,512]{1,0:T(8,128)(2,1)S(1)}, u32[]{:S(2)}, u32[]{:S(2)}) collective-permute-start(bf16[768,512]{1,0:T(8,128)(2,1)S(1)} %copy-done.6), channel_id=1, source_target_pairs={{1,0},{2,1},{3,2},{5,4},{6,5},{7,6},{9,8},{10,9},{11,10},{13,12},{... | collective-permute-start | bytes 2359304 | tf_op jit(solution)/shard_map/ppermute | solution.py:557
  160.4 17.0 %collective-permute-start.21 = (bf16[240,512]{1,0:T(8,128)(2,1)S(1)}, bf16[240,512]{1,0:T(8,128)(2,1)S(1)}, u32[]{:S(2)}, u32[]{:S(2)}) collective-permute-start(bf16[240,512]{1,0:T(8,128)(2,1)S(1)} %copy-done.16), channel_id=1, source_target_pairs={{2,3},{6,7},{10,11},{14,15},{18,19},{22,23},{26,27},{30,31}} | collective-permute-start | bytes 737288 | tf_op jit(solution)/shard_map/ppermute | solution.py:557
  161.1 16.3 %collective-permute-start.20 = (bf16[240,512]{1,0:T(8,128)(2,1)S(1)}, bf16[240,512]{1,0:T(8,128)(2,1)S(1)}, u32[]{:S(2)}, u32[]{:S(2)}) collective-permute-start(bf16[240,512]{1,0:T(8,128)(2,1)S(1)} %copy-done.16), channel_id=1, source_target_pairs={{1,3},{5,7},{9,11},{13,15},{17,19},{21,23},{25,27},{29,31}} | collective-permute-start | bytes 737288 | tf_op jit(solution)/shard_map/ppermute | solution.py:557
  161.8 19.4 %collective-permute-start.19 = (bf16[240,512]{1,0:T(8,128)(2,1)S(1)}, bf16[240,512]{1,0:T(8,128)(2,1)S(1)}, u32[]{:S(2)}, u32[]{:S(2)}) collective-permute-start(bf16[240,512]{1,0:T(8,128)(2,1)S(1)} %copy-done.16), channel_id=1, source_target_pairs={{0,3},{4,7},{8,11},{12,15},{16,19},{20,23},{24,27},{28,31}} | collective-permute-start | bytes 737288 | tf_op jit(solution)/shard_map/ppermute | solution.py:557
  177.4 18.7 %copy-start.17 = (bf16[240,512]{1,0:T(8,128)(2,1)}, bf16[240,512]{1,0:T(8,128)(2,1)S(1)}, u32[]{:S(2)}) copy-start(bf16[240,512]{1,0:T(8,128)(2,1)S(1)} %collective-permute-done.21.rest_2_) | copy-start | bytes 737284
  177.4 3.8 %copy-start.18 = (bf16[240,512]{1,0:T(8,128)(2,1)}, bf16[240,512]{1,0:T(8,128)(2,1)S(1)}, u32[]{:S(2)}) copy-start(bf16[240,512]{1,0:T(8,128)(2,1)S(1)} %collective-permute-done.20.rest_1_) | copy-start | bytes 737284
  191.2 4.9 %copy-start.8 = (bf16[768,512]{1,0:T(8,128)(2,1)}, bf16[768,512]{1,0:T(8,128)(2,1)S(1)}, u32[]{:S(2)}) copy-start(bf16[768,512]{1,0:T(8,128)(2,1)S(1)} %collective-permute-done.18.recv) | copy-start | bytes 2359300
  191.4 9.8 %collective-permute-start.22 = (bf16[288,128]{1,0:T(8,128)(2,1)S(1)}, bf16[288,128]{1,0:T(8,128)(2,1)S(1)}, u32[]{:S(2)}, u32[]{:S(2)}) collective-permute-start(bf16[288,128]{1,0:T(8,128)(2,1)S(1)} %get-tuple-element.119), channel_id=1, source_target_pairs={{0,1},{1,0},{2,3},{3,2},{4,5},{5,4},{6,7},{7,6},{8,9},{9,8},{10,11... | collective-permute-start | bytes 221192 | tf_op jit(solution)/shard_map/ppermute | solution.py:666
  193.1 8.1 %collective-permute-start.23 = (bf16[288,128]{1,0:T(8,128)(2,1)S(1)}, bf16[288,128]{1,0:T(8,128)(2,1)S(1)}, u32[]{:S(2)}, u32[]{:S(2)}) collective-permute-start(bf16[288,128]{1,0:T(8,128)(2,1)S(1)} %get-tuple-element.120), channel_id=1, source_target_pairs={{0,2},{1,3},{2,0},{3,1},{4,6},{5,7},{6,4},{7,5},{8,10},{9,11},{10,... | collective-permute-start | bytes 221192 | tf_op jit(solution)/shard_map/ppermute | solution.py:666
  196.1 6.3 %collective-permute-start.24 = (bf16[288,128]{1,0:T(8,128)(2,1)S(1)}, bf16[288,128]{1,0:T(8,128)(2,1)S(1)}, u32[]{:S(2)}, u32[]{:S(2)}) collective-permute-start(bf16[288,128]{1,0:T(8,128)(2,1)S(1)} %get-tuple-element.121), channel_id=1, source_target_pairs={{0,3},{1,2},{2,1},{3,0},{4,7},{5,6},{6,5},{7,4},{8,11},{9,10},{10,... | collective-permute-start | bytes 221192 | tf_op jit(solution)/shard_map/ppermute | solution.py:666
  (3 other events, 2.3 us)
Sparse Core Ops, SparseCore 0:
  34.8 35.5 all-gather.8
  109.3 41.6 all-gather.10
  153.9 35.4 reduce-scatter.1
  191.4 25.0 all-gather.12
